TPU v7x, 128 devices: a whole 4x4x4 slice. The times are simulated.
128 devices in a mesh: grp: 4 (over x), shard: 32 (over z, y, core).
Axes of the slice: x: 4, y: 4, z: 4, core: 2. Of those that a mesh axis runs over, the one named last changes fastest.
Arguments:
- grads: bfloat16 [4, 32, 8192, 1024], P('grp', 'shard'), may hold values from -6 to 6
- momentum: float32 [4, 8192, 1024], P('grp', 'shard'), may hold values from -18 to 18
- positions: int32 [4, 128, 16, 32], P('grp', 'shard'), may hold values from 0 to 4095, as said below
- counts: int32 [4], P('grp'), may hold values from 4 to 32, as said below
Outputs:
- new_momentum: float32 [4, 8192, 1024], P('grp', 'shard')
- update: float32 [8192, 1024], P('shard')
Inputs may be any that keep to these rules, and one draw needn't show every extreme that they name: Within each block of each group the 32 positions are distinct. Each group uses the first counts[g] positions of every block; in every draw one group uses all 32.
All inputs are finite; a program needn't handle non-finite values.
Results may differ from a plain program's by a relative error of at most 0.0003.
Values sent between devices are 32-bit elements; how exact they have to be, the bound alone decides.
No kernel may reach another device: no remote copies, remote signals or barrier semaphores. Data moves between devices by JAX's collectives and lax.ppermute only.
A program may use at most 256 MiB of HBM per device.

v0:
```python
import jax
import jax.numpy as jnp
from jax import lax
from jax.sharding import PartitionSpec as P

SPAN = 64


momentum_decay = 0.999


def dct_basis(tile_width):
    frequency = lax.broadcasted_iota(jnp.int32, (tile_width, tile_width), 0).astype(jnp.float32)
    position = lax.broadcasted_iota(jnp.int32, (tile_width, tile_width), 1).astype(jnp.float32)
    norming = jnp.where(frequency == 0, jnp.sqrt(1.0 / tile_width), jnp.sqrt(2.0 / tile_width))
    return norming * jnp.cos(jnp.pi * (2.0 * position + 1.0) * frequency / (2.0 * tile_width))


def to_coefficients(field, basis):
    tile_width = basis.shape[0]
    height, across = field.shape
    tiles = field.reshape(height // tile_width, tile_width, across // tile_width, tile_width)
    result = jnp.einsum("km,amcn,ln->akcl", basis, tiles, basis, precision=lax.Precision.HIGHEST)
    return result.reshape(height, across)


def tile_major(coeffs, tile_width):
    height, across = coeffs.shape
    tiles = coeffs.reshape(height // tile_width, tile_width, across // tile_width, tile_width)
    return tiles.transpose(0, 2, 1, 3).reshape(
        height // tile_width, across // tile_width, tile_width * tile_width
    )


def to_field(coeffs, basis):
    tile_width = basis.shape[0]
    blocks_down, blocks_across, squared = coeffs.shape
    tiles = coeffs.reshape(blocks_down, blocks_across, tile_width, tile_width)
    result = jnp.einsum("km,abkl,ln->ambn", basis, tiles, basis, precision=lax.Precision.HIGHEST)
    return result.reshape(blocks_down * tile_width, blocks_across * tile_width)


def scatter_into(values, places, target_shape):
    blocks_down, blocks_across, squared = target_shape
    down_index = jnp.arange(blocks_down).reshape(blocks_down, 1, 1)
    across_index = jnp.arange(blocks_across).reshape(1, blocks_across, 1)
    return jnp.zeros(target_shape, jnp.float32).at[down_index, across_index, places].add(values)


def per_device(grads, momentum, positions, counts):
    basis = dct_basis(SPAN)
    local_grads = grads[0, 0]
    summed = lax.psum_scatter(
        local_grads.astype(jnp.float32), "shard", scatter_dimension=0, tiled=True
    )
    updated = momentum_decay * momentum[0] + summed
    coeffs = tile_major(to_coefficients(updated, basis), SPAN)
    places = positions[0]
    live_mask = lax.broadcasted_iota(jnp.int32, places.shape, 2) < counts[0]
    values = jnp.where(live_mask, jnp.take_along_axis(coeffs, places, axis=2), 0.0)
    own_coeffs = scatter_into(values, places, coeffs.shape)
    new_field = updated - to_field(own_coeffs, basis)
    combined = lax.psum(own_coeffs, "grp")
    update = to_field(combined / lax.axis_size("grp"), basis)
    return (new_field[None], update)


def solution(mesh):
    in_specs = (
        P("grp", "shard", None, None),
        P("grp", "shard", None),
        P("grp", "shard", None, None),
        P("grp"),
    )
    out_specs = (P("grp", "shard", None), P("shard", None))
    return jax.shard_map(
        per_device, mesh=mesh, in_specs=in_specs, out_specs=out_specs, check_vma=False
    )
```

profile of v0, /device:TPU:0, one launch (start us, length us, event | category | flops | bytes accessed | tf_op | source)
XLA Modules:
  0.0 298.5 jit_solution(11376388392337815492)
XLA Ops:
  7.2 0.0 reduce-scatter.2.cloned.1.call-start
  7.2 18.6 %bitcast_convert_fusion = f32[8192,1024]{1,0:T(8,128)} fusion(bf16[1,1,8192,1024]{3,2,1,0:T(8,128)(2,1)} %param.4), kind=kLoop, calls=%fused_computation.2 | loop fusion | flops 8388608 | bytes 50331648 | tf_op jit(solution)/shard_map/convert_element_type | solution.py:54
  25.8 0.0 copy-start.1
  25.8 0.0 copy-start.2
  25.8 0.0 copy-start.3
  25.8 0.0 copy-start
  25.8 0.0 reduce-scatter.2.cloned.1.call-update
  25.8 0.0 all-reduce.2.cloned.1.call-start
  25.9 0.7 copy-done.1
  26.6 0.0 copy-done.2
  26.6 0.1 multiply_reduce_fusion
  26.7 0.0 copy-done.3
  26.7 0.1 and_reduce_fusion
  26.8 0.1 reshape.88
  26.9 0.1 reshape.82
  27.6 165.9 %reduce-scatter.2.cloned.1.call-done = f32[256,1024]{1,0:T(8,128)} async-done(((f32[8192,1024]{1,0:T(8,128)}), f32[256,1024]{1,0:T(8,128)}) %reduce-scatter.2.cloned.1.call-update) | async-done | bytes 1048592 | tf_op jit(solution)/shard_map/reduce_scatter | solution.py:53
  193.5 0.0 copy-done
  193.5 1.4 bitcast_add_fusion
  194.9 0.6 reshape.70
  195.5 2.7 fusion
  198.2 3.3 %fusion.10 = f32[4,16,64,64]{3,2,1,0:T(8,128)} fusion(f32[4,16,64,64]{2,3,1,0:T(8,128)S(1)} %fusion, f32[64]{0:T(128)S(1)} %convert_multiply_fusion, f32[64]{0:T(128)S(1)} %get-tuple-element.5, f32[64]{0:T(128)S(1)} %get-tuple-element.4), kind=kOutput, calls=%fused_computation.23 | convolution fusion | flops 201338880 | bytes 2097920 | tf_op jit(solution)/shard_map/km,amcn,ln->akcl/dot_general | solution.py:23
  201.5 2.1 reshape.71
  203.6 20.6 %gather_fusion = f32[2048]{0:T(1024)S(1)} fusion(f32[4,16,4096]{2,1,0:T(8,128)S(1)} %reshape.71, s32[2048]{0:T(1024)S(1)} %reshape.82), kind=kCustom, calls=%fused_computation | custom fusion | bytes 40960 | tf_op jit(solution)/shard_map/jit(take_along_axis)/gather | solution.py:60
  224.2 0.1 reshape.85
  224.3 0.1 reshape.90
  224.4 11.7 %scatter_custom_fusion = f32[262144]{0:T(1024)S(1)} fusion(s32[2048]{0:T(1024)S(1)} %reshape.88, f32[2048]{0:T(1024)S(1)} %reshape.90, f32[]{:T(128)} %constant.14.clone.1), kind=kCustom, calls=%fused_computation.9 | custom fusion | flops 2048 | bytes 1048580
  236.1 1.2 reshape.79
  237.3 0.0 all-reduce.2.cloned.1.call-update
  237.3 1.7 reshape.72
  239.0 3.7 %fusion.8 = f32[4,16,64,64]{2,3,1,0:T(8,128)S(1)} fusion(f32[4,16,64,64]{3,2,1,0:T(8,128)} %reshape.72, f32[64]{0:T(128)S(1)} %convert_multiply_fusion, f32[64]{0:T(128)S(1)} %get-tuple-element.5, f32[64]{0:T(128)S(1)} %get-tuple-element.4), kind=kOutput, calls=%fused_computation.21 | convolution fusion | flops 201338880 | bytes 2097920 | tf_op jit(solution)/shard_map/km,abkl,ln->ambn/dot_general | solution.py:39
  242.7 2.0 convolution_bitcast_fusion.1
  244.8 1.2 copy.6
  246.0 1.5 reshape.73
  247.5 2.3 subtract_bitcast_fusion
  249.8 32.8 %all-reduce.2.cloned.1.call-done = f32[4,16,4096]{2,1,0:T(8,128)} async-done(((f32[4,16,4096]{2,1,0:T(8,128)}), f32[4,16,4096]{2,1,0:T(8,128)}) %all-reduce.2.cloned.1.call-update) | async-done | bytes 1048592 | tf_op jit(solution)/shard_map/psum | solution.py:63
  282.6 1.3 broadcast_multiply_fusion
  283.9 0.8 reshape.74
  284.8 2.1 fusion.5
  286.9 2.0 convolution_bitcast_fusion
  288.9 1.2 copy.7
  290.2 1.5 reshape.75
  (8 shorter events, 0.1 us)
Async XLA Ops:
  7.2 186.3 %reduce-scatter.2.cloned.1.call-start = ((), (), s32[]{:S(2)}) async-start(), calls=%async_computation.1 | async-start | bytes 34603008 | tf_op jit(solution)/shard_map/reduce_scatter | solution.py:53
  25.8 0.8 copy-start.1
  25.8 0.8 copy-start.2
  25.8 0.9 copy-start.3
  25.8 167.7 %copy-start = (f32[1,256,1024]{2,1,0:T(8,128)S(1)}, f32[1,256,1024]{2,1,0:T(8,128)}, u32[]{:S(2)}) copy-start(f32[1,256,1024]{2,1,0:T(8,128)} %param.5) | copy-start | bytes 3145732
  25.8 256.8 %all-reduce.2.cloned.1.call-start = ((), (), s32[]{:S(2)}) async-start(), calls=%async_computation.2 | async-start | bytes 2097152 | tf_op jit(solution)/shard_map/psum | solution.py:63
Sparse Core Ops, SparseCore 0:
  26.0 167.5 reduce-scatter.1
  237.4 45.1 all-reduce.1
where the time goes:
time: 299 us
  waiting for transfers between devices  199 us (67%)
  other arithmetic  35.5 us (12%)
  local copies, waits for them, and re-layouts  33.5 us (11%)
  matrix products  15.9 us (5%)
  between operations  14.9 us (5%)
    reduce_scatter x1, waiting for transfers between devices, per_device(): lax.psum_scatter(local_grads.astype(jnp.float32), 'shard', scatter_dimens...  166 us
    psum x1, waiting for transfers between devices, per_device(): combined = lax.psum(own_coeffs, 'grp')  32.8 us
    gather x2, local copies, waits for them, and re-layouts, per_device(): jnp.take_along_axis(coeffs, places, axis=2)  20.7 us
    convert_element_type x1, other arithmetic, per_device(): local_grads.astype(jnp.float32)  18.6 us
    unnamed x4, other arithmetic  11.9 us
    dot_general x4, matrix products, to_field(): jnp.einsum('km,abkl,ln->ambn', basis, tiles, basis, precision=lax.Precisi...  9.9 us
    dot_general x2, matrix products, to_coefficients(): jnp.einsum('km,amcn,ln->akcl', basis, tiles, basis, precision=lax.Precisi...  6.05 us
  transfers between devices with their start and end apart: 2, of which 2 were waited for; matrix products, arithmetic and copies ran while one was open for 4% of the time, Pallas kernels for 0%

commit v1 on v0

v1 whole, which is shorter than its diff:
```python
import functools

import jax
import jax.numpy as jnp
import numpy as np
from jax import lax
from jax.experimental import pallas as pl
from jax.experimental.pallas import tpu as pltpu
from jax.sharding import PartitionSpec as P

SPAN = 64
DECAY = 0.999
NZ, NY, NC, NX = 4, 4, 2, 4
ROWS, COLS = 256, 1024
HW = COLS // 2
TOPK = 32
NA, NT, TILE = ROWS // SPAN, 4, 256
PARTS = ((0, 128), (128, 128))
OFFSETS = ((2, 2), (1, -1), (-1, 1), (0, 0))
F32, BF16 = jnp.float32, jnp.bfloat16


def vm(shape, dtype=F32):
    return pltpu.VMEM(shape, dtype)


VSPEC = pl.BlockSpec(memory_space=pltpu.VMEM)
ASPEC = pl.BlockSpec(memory_space=pl.ANY)


def position():
    s = lax.axis_index("shard")
    return lax.axis_index("grp"), s // (NY * NC), (s // NC) % NY, s % NC


def axes(other=False):
    _, z, y, c = position()
    c = 1 - c if other else c
    return c, jnp.where(c == 0, z, y), jnp.where(c == 0, y, z)


def fetch(g_ref, buf, sems, stage, r0, rows, other):
    core, first, _ = axes(other)
    copies = []
    for h in range(2):
        mine = (first + (OFFSETS[stage][h] + 4)) % 4
        for s in range(4):
            zi, yi = jnp.where(core == 0, mine, s), jnp.where(core == 0, s, mine)
            src = g_ref.at[zi, yi, core, pl.ds(r0, rows), pl.ds(h * HW, HW)]
            cp = pltpu.make_async_copy(src, buf.at[h, s], sems.at[h, s])
            cp.start()
            copies.append(cp)
    return copies


def conv_kernel(stage, r0, rows, g_ref, w_ref, buf, sems):
    copies = fetch(g_ref, buf, sems, stage, r0, rows, True)
    for h in range(2):
        for s in range(4):
            copies[4 * h + s].wait()
            w_ref[h, s] = buf[h, s].astype(F32)


def sum_kernel(stage, r0, rows, n_in, g_ref, *refs):
    r_ref, refs = refs[0], refs[1:]
    ins, outs, (buf, sems) = refs[: 2 * n_in], refs[2 * n_in : 2 * n_in + 2], refs[-2:]
    copies = fetch(g_ref, buf, sems, stage, r0, rows, False)
    for h in range(2):
        for s in range(4):
            copies[4 * h + s].wait()
            total = buf[h, s].astype(F32) + r_ref[h, s]
            for m in range(n_in):
                total = total + ins[2 * m + h][s]
            outs[h][s] = total


def turn_kernel(r0, rows, g_ref, r_ref, *refs):
    ins, outs, (buf, sems) = refs[:4], refs[4:12], refs[-2:]
    copies = fetch(g_ref, buf, sems, 3, r0, rows, False)
    _, _, here = axes()
    for cp in copies:
        cp.wait()
    for h in range(2):
        for stage in range(4):
            s = (here + (OFFSETS[stage][h] + 4)) % 4
            outs[2 * stage + h][...] = (
                buf[h, s].astype(F32) + r_ref[h, s] + ins[h][s] + ins[2 + h][s]
            )


def relay_kernel(*refs):
    for h in range(2):
        refs[4 + h][...] = refs[h][...] + refs[2 + h][...]


def call(body, outs, args, name, scratch=(), limit=8, cost=(1_000_000, 4_000_000), onto=None):
    space = {"v": pltpu.VMEM, "h": pltpu.HBM}
    spec = {"v": VSPEC, "h": ASPEC, "s": pl.BlockSpec(memory_space=pltpu.SMEM)}
    vals = [pltpu.with_memory_space_constraint(a, space[kind]) if kind in space else a for a, kind in args]
    in_specs = [spec[kind] for _, kind in args]
    whole = isinstance(outs, jax.ShapeDtypeStruct)
    aliases = {}
    if onto is not None:
        vals, in_specs, aliases = vals + [onto], in_specs + [ASPEC], {len(vals): 0}
    return pl.pallas_call(
        body,
        out_shape=outs,
        in_specs=in_specs,
        out_specs=ASPEC if whole else jax.tree.map(lambda o: VSPEC, outs, is_leaf=lambda o: not isinstance(o, (list, tuple))),
        scratch_shapes=list(scratch),
        input_output_aliases=aliases,
        compiler_params=pltpu.CompilerParams(vmem_limit_bytes=limit * 2**20),
        cost_estimate=pl.CostEstimate(flops=cost[0], bytes_accessed=cost[1], transcendentals=0),
        name=name,
    )(*vals)


def place(z, y, c):
    return (z % NZ * NY + y % NY) * NC + c % NC


def everywhere():
    return [(z, y, c) for z in range(NZ) for y in range(NY) for c in range(NC)]


def to_other_core(x):
    return lax.ppermute(x, "shard", [(place(z, y, c), place(z, y, c + 1)) for z, y, c in everywhere()])


def along(x, step, second=False):
    pairs = []
    for z, y, c in everywhere():
        to = (z + step, y, c) if (c == 0) != second else (z, y + step, c)
        pairs.append((place(z, y, c), place(*to)))
    return lax.ppermute(x, "shard", pairs)


def move_grp(x, d):
    return lax.ppermute(x, "grp", [(i, (i + d) % NX) for i in range(NX)])


WAY = ((-1, 1), (1, -1), (-1, 1))


def reduce_part(g, r0, rows):
    scratch = [pltpu.VMEM((2, 4, rows, HW), BF16), pltpu.SemaphoreType.DMA((2, 4))]
    chunk, small = (4, rows, HW), (rows, HW)
    got = []
    for stage in range(4):
        w = call(functools.partial(conv_kernel, stage, r0, rows), vm((2,) + chunk), [(g, "h")], f"conv{stage}", scratch)
        got.append(to_other_core(w))

    def summed(stage, ins):
        n_in = len(ins) // 2
        return call(
            functools.partial(sum_kernel, stage, r0, rows, n_in),
            [vm(chunk)] * 2,
            [(g, "h"), (got[stage], "v")] + [(x, "v") for x in ins],
            f"sum{stage}",
            scratch,
        )

    first = [along(x, WAY[0][h]) for h, x in enumerate(summed(0, []))]
    direct = [along(x, WAY[1][h]) for h, x in enumerate(summed(1, []))]
    relay = [along(x, WAY[2][h]) for h, x in enumerate(summed(2, first))]
    turned = call(
        functools.partial(turn_kernel, r0, rows),
        [vm(small)] * 8,
        [(g, "h"), (got[3], "v")] + [(x, "v") for x in direct + relay],
        "turn",
        scratch,
    )
    first = [along(x, WAY[0][h], True) for h, x in enumerate(turned[0:2])]
    direct = [along(x, WAY[1][h], True) for h, x in enumerate(turned[2:4])]
    on = call(relay_kernel, [vm(small)] * 2, [(x, "v") for x in list(turned[4:6]) + first], "relay")
    relay = [along(x, WAY[2][h], True) for h, x in enumerate(on)]
    return list(turned[6:8]), direct, relay


def split(x):
    high = x.astype(BF16)
    return high, (x - high.astype(F32)).astype(BF16)


def dot(a, b, last=False):
    return lax.dot_general(a, b, (((1,), (1 if last else 0,)), ((), ())), preferred_element_type=F32)


def dot3(x, high, low):
    xh, xl = split(x)
    n = x.shape[0]
    both = dot(jnp.concatenate([xh, xl], axis=0), high)
    return both[:n] + both[n:] + dot(xh, low)


def basis():
    k, n = np.arange(SPAN)[:, None], np.arange(SPAN)[None, :]
    q = np.sqrt(np.where(k == 0, 1.0, 2.0) / SPAN) * np.cos(np.pi * (2 * n + 1) * k / (2 * SPAN))
    return q, np.kron(np.eye(TILE // SPAN), q.T)


def halves_of(m):
    high = m.astype(np.float32).astype(jnp.bfloat16)
    low = (m - high.astype(np.float64)).astype(np.float32).astype(jnp.bfloat16)
    return [jnp.asarray(high), jnp.asarray(low)]


def prep_kernel(p0, p1, p2, p3, qh_ref, ql_ref, bt_ref, l_ref):
    me = position()[0]
    block = lax.broadcasted_iota(jnp.int32, (1, 128), 1) // TOPK
    for i, ref in enumerate((p0, p1, p2, p3)):
        lanes = pl.ds(pl.multiple_of(((me + (4 - i)) % NX) * 128, 128), 128)

        @pl.loop(0, NA)
        def _(a, ref=ref, lanes=lanes):
            for t in range(NT):
                pos = ref[a, t : t + 1, :]
                row, col = pos // SPAN, pos % SPAN + block * SPAN
                hit = lax.broadcasted_iota(jnp.int32, (TILE, 128), 0) == col
                bt_ref[a, t, :, lanes] = jnp.where(hit, 1.0, 0.0).astype(BF16)
                at = jnp.where(lax.broadcasted_iota(jnp.int32, (SPAN, 128), 0) == row, 1.0, 0.0).astype(BF16)
                l_ref[a, t, :, lanes] = dot(qh_ref[...], at) + dot(ql_ref[...], at)


def values_kernel(a0, na, m_ref, count_ref, dh_ref, dl_ref, bt_ref, l_ref, *refs):
    ins, (up_ref, v_ref) = refs[:6], refs[6:]
    me = position()[0]
    lanes = pl.ds(pl.multiple_of(me * 128, 128), 128)
    live = lax.broadcasted_iota(jnp.int32, (1, 128), 1) % TOPK < count_ref[0]
    for t in range(NT):
        h, cols, part = t // 2, pl.ds(t * TILE, TILE), pl.ds(t % 2 * TILE, TILE)
        up = DECAY * m_ref[a0 * SPAN : (a0 + na) * SPAN, cols] + (ins[h][:, part] + ins[2 + h][:, part] + ins[4 + h][:, part])
        up_ref[:, cols] = up
        zh, zl = split(dot3(up, dh_ref[...], dl_ref[...]))
        for a in range(na):
            rows = slice(a * SPAN, (a + 1) * SPAN)
            got = dot(jnp.concatenate([zh[rows], zl[rows]], axis=0), bt_ref[a0 + a, t, :, lanes])
            v = jnp.sum((got[:SPAN] + got[SPAN:]) * l_ref[a0 + a, t, :, lanes], axis=0, keepdims=True)
            v_ref[4 * a + t : 4 * a + t + 1, :] = jnp.where(live, v, 0.0)


def field(v, l, bt, eh, el):
    high, low = split(l * v)
    got = dot(jnp.concatenate([high, low], axis=0), bt, last=True)
    return dot3(got[:SPAN] + got[SPAN:], eh, el)


def store_rows(buf, out_ref, a0, na, sem):
    cp = pltpu.make_async_copy(buf, out_ref.at[pl.ds(a0 * SPAN, na * SPAN), :], sem)
    cp.start()
    cp.wait()


def keep_kernel(a0, na, up_ref, v_ref, eh_ref, el_ref, bt_ref, l_ref, *refs):
    out_ref, buf, sem = refs[-3:]
    lanes = pl.ds(pl.multiple_of(position()[0] * 128, 128), 128)
    for a in range(na):
        for t in range(NT):
            rows, cols = pl.ds(a * SPAN, SPAN), pl.ds(t * TILE, TILE)
            got = field(v_ref[4 * a + t : 4 * a + t + 1, :], l_ref[a0 + a, t, :, lanes], bt_ref[a0 + a, t, :, lanes], eh_ref[...], el_ref[...])
            buf[rows, cols] = up_ref[rows, cols] - got
    store_rows(buf, out_ref, a0, na, sem)


def update_kernel(a0, na, v0, v1, v2, v3, eh_ref, el_ref, bt_ref, l_ref, *refs):
    out_ref, buf, vals, sem = refs[-4:]
    me = position()[0]
    for i, ref in enumerate((v0, v1, v2, v3)):
        vals[:, pl.ds(pl.multiple_of(((me + (4 - i)) % NX) * 128, 128), 128)] = ref[...] * (1.0 / NX)
    for a in range(na):
        for t in range(NT):
            got = field(vals[4 * a + t : 4 * a + t + 1, :], l_ref[a0 + a, t], bt_ref[a0 + a, t], eh_ref[...], el_ref[...])
            buf[pl.ds(a * SPAN, SPAN), pl.ds(t * TILE, TILE)] = got
    store_rows(buf, out_ref, a0, na, sem)


def from_groups(x):
    return [x] + [move_grp(x, i) for i in (1, 2, 3)]


def per_device(grads, momentum, positions, counts):
    g = grads.reshape(NZ, NY, NC, ROWS, COLS)
    q, four = basis()
    dh, dl = halves_of(four)
    eh, el = halves_of(four.T)
    qh, ql = halves_of(q.T)
    places = from_groups(positions.reshape(NA, NT, 128))
    bt, l = call(
        prep_kernel,
        [vm((NA, NT, TILE, NX * 128), BF16), vm((NA, NT, SPAN, NX * 128))],
        [(x, "v") for x in places + [qh, ql]],
        "prep",
        limit=16,
        cost=(10_000_000, 20_000_000),
    )
    tables = [(bt, "v"), (l, "v")]
    kept = update = None
    for r0, rows in PARTS:
        a0, na = r0 // SPAN, rows // SPAN
        sums = reduce_part(g, r0, rows)
        up, v = call(
            functools.partial(values_kernel, a0, na),
            [vm((rows, COLS)), vm((NT * na, 128))],
            [(momentum[0], "v"), (counts, "s"), (dh, "v"), (dl, "v")] + tables + [(x, "v") for s in sums for x in s],
            "values",
        )
        vs = from_groups(v)
        scratch = [pltpu.VMEM((rows, COLS), F32), pltpu.SemaphoreType.DMA]
        kept = call(
            functools.partial(keep_kernel, a0, na),
            jax.ShapeDtypeStruct((ROWS, COLS), F32),
            [(up, "v"), (v, "v"), (eh, "v"), (el, "v")] + tables,
            "keep",
            scratch,
            onto=kept,
        )
        update = call(
            functools.partial(update_kernel, a0, na),
            jax.ShapeDtypeStruct((ROWS, COLS), F32),
            [(x, "v") for x in vs] + [(eh, "v"), (el, "v")] + tables,
            "update",
            [scratch[0], pltpu.VMEM((NT * na, NX * 128), F32), scratch[1]],
            onto=update,
        )
    return kept[None], update


def solution(mesh):
    in_specs = (
        P("grp", "shard", None, None),
        P("grp", "shard", None),
        P("grp", "shard", None, None),
        P("grp"),
    )
    out_specs = (P("grp", "shard", None), P("shard", None))
    return jax.shard_map(
        per_device, mesh=mesh, in_specs=in_specs, out_specs=out_specs, check_vma=False
    )
```

time: 299 us -> 153 us (0.51)
  waiting for transfers between devices: 199 us -> 56.7 us
  starting transfers between devices: 0.08 us -> 47.3 us
  Pallas kernels: 0 us -> 43.4 us
  other arithmetic: 35.5 us -> 0 us
  local copies, waits for them, and re-layouts: 33.5 us -> 2.94 us
  matrix products: 15.9 us -> 0 us
  between operations: 14.9 us -> 1.91 us
    reduce_scatter x1 -> x0, waiting for transfers between devices: 166 us -> none  [per_device(): lax.psum_scatter(local_grads.astype(jnp.float32), 'shard', scatter_dimens...]
    ppermute x0 -> x41, waiting for transfers between devices: none -> 56.7 us  [the longest x24 55.6 us: along(): return lax.ppermute(x, 'shard', pairs)]
    ppermute x0 -> x41, starting transfers between devices: none -> 47.3 us  [the longest x24 30.5 us: along(): return lax.ppermute(x, 'shard', pairs)]
    pallas_call x0 -> x25, Pallas kernels: none -> 43.4 us  [call(): pl.pallas_call(body, out_shape=outs, in_specs=in_specs, out_specs=ASPEC i...]
    psum x1 -> x0, waiting for transfers between devices: 32.8 us -> none  [per_device(): combined = lax.psum(own_coeffs, 'grp')]
    gather x2 -> x0, local copies, waits for them, and re-layouts: 20.7 us -> none  [per_device(): jnp.take_along_axis(coeffs, places, axis=2)]
    convert_element_type x1 -> x0, other arithmetic: 18.6 us -> none  [per_device(): local_grads.astype(jnp.float32)]
    dot_general x6 -> x0, matrix products: 15.9 us -> none  [the longest x4 9.9 us: to_field(): jnp.einsum('km,abkl,ln->ambn', basis, tiles, basis, precision=lax.Precisi...]
  transfers between devices with their start and end apart: 2 -> 41, of which waited for: 2 -> 11; matrix products, arithmetic and copies ran while one was open for 4% -> 0% of each run, Pallas kernels for 0% -> 25%
where the time goes in v1:
time: 153 us; the launch traced here: 152 us
  waiting for transfers between devices  56.7 us (37%)
  starting transfers between devices  47.3 us (31%)
  Pallas kernels  43.4 us (28%)
  local copies, waits for them, and re-layouts  2.94 us (2%)
  between operations  1.91 us (1%)
    ppermute x24, waiting for transfers between devices, along(): return lax.ppermute(x, 'shard', pairs)  55.6 us
    pallas_call x25, Pallas kernels, call(): pl.pallas_call(body, out_shape=outs, in_specs=in_specs, out_specs=ASPEC i...  43.4 us
    ppermute x24, starting transfers between devices, along(): return lax.ppermute(x, 'shard', pairs)  30.5 us
    ppermute x9, starting transfers between devices, move_grp(): return lax.ppermute(x, 'grp', [(i, (i + d) % NX) for i in range(NX)])  14.7 us
  transfers between devices with their start and end apart: 41, of which 11 were waited for; matrix products, arithmetic and copies ran while one was open for 0% of the time, Pallas kernels for 25%

profile of v1, /device:TPU:0, one launch (start us, length us, event | category | flops | bytes accessed | tf_op | source)
XLA Modules:
  0.0 152.3 jit_solution(1966288748759521861)
XLA Ops:
  0.6 1.4 conv0.3
  2.1 1.4 conv2.3
  3.5 0.5 collective-permute-start.23
  4.1 1.4 conv1.3
  5.6 1.4 conv0.2
  7.0 0.5 collective-permute-start.8
  7.5 1.4 conv3.3
  9.0 1.4 conv2.2
  10.4 0.5 collective-permute-start.7
  10.9 1.4 conv1.2
  12.5 1.4 sum0.3
  13.8 4.2 %collective-permute-start.25 = (f32[4,128,512]{2,1,0:T(8,128)S(1)}, f32[4,128,512]{2,1,0:T(8,128)S(1)}, u32[]{:S(2)}, u32[]{:S(2)}) collective-permute-start(f32[4,128,512]{2,1,0:T(8,128)S(1)} %get-tuple-element.62), channel_id=1, source_target_pairs={{0,24},{1,7},{2,26},{3,1},{4,28},{5,3},{6,30},{7,5},{8,0},{9,15},{... | collective-permute-start | bytes 3145736 | tf_op jit(solution)/shard_map/ppermute | solution.py:135
  18.0 1.4 sum1.3
  19.4 1.4 sum0.2
  20.8 1.2 collective-permute-start.21
  22.1 1.6 %collective-permute-start.10 = (f32[4,128,512]{2,1,0:T(8,128)S(1)}, f32[4,128,512]{2,1,0:T(8,128)S(1)}, u32[]{:S(2)}, u32[]{:S(2)}) collective-permute-start(f32[4,128,512]{2,1,0:T(8,128)S(1)} %get-tuple-element.45), channel_id=1, source_target_pairs={{0,8},{1,3},{2,10},{3,5},{4,12},{5,7},{6,14},{7,1},{8,16},{9,11},{... | collective-permute-start | bytes 3145736 | tf_op jit(solution)/shard_map/ppermute | solution.py:135
  23.7 1.4 conv3.2
  25.1 5.3 %collective-permute-done.25.refs_1_ = f32[4,128,512]{2,1,0:T(8,128)S(1)} collective-permute-done((f32[4,128,512]{2,1,0:T(8,128)S(1)}, f32[4,128,512]{2,1,0:T(8,128)S(1)}, u32[]{:S(2)}, u32[]{:S(2)}) %collective-permute-start.25) | collective-permute-done | bytes 1048608 | tf_op jit(solution)/shard_map/ppermute | solution.py:135
  30.4 3.7 %collective-permute-done.26.refs_2_ = f32[4,128,512]{2,1,0:T(8,128)S(1)} collective-permute-done((f32[4,128,512]{2,1,0:T(8,128)S(1)}, f32[4,128,512]{2,1,0:T(8,128)S(1)}, u32[]{:S(2)}, u32[]{:S(2)}) %collective-permute-start.26) | collective-permute-done | bytes 1048608 | tf_op jit(solution)/shard_map/ppermute | solution.py:135
  34.2 1.4 sum2.3
  35.6 0.5 collective-permute-start.22
  36.1 9.2 %collective-permute-done.21.refs_0_ = f32[4,128,512]{2,1,0:T(8,128)S(1)} collective-permute-done((f32[4,128,512]{2,1,0:T(8,128)S(1)}, f32[4,128,512]{2,1,0:T(8,128)S(1)}, u32[]{:S(2)}, u32[]{:S(2)}) %collective-permute-start.21) | collective-permute-done | bytes 1048608 | tf_op jit(solution)/shard_map/ppermute | solution.py:135
  45.4 11.1 %collective-permute-done.10.refs_2_ = f32[4,128,512]{2,1,0:T(8,128)S(1)} collective-permute-done((f32[4,128,512]{2,1,0:T(8,128)S(1)}, f32[4,128,512]{2,1,0:T(8,128)S(1)}, u32[]{:S(2)}, u32[]{:S(2)}) %collective-permute-start.10) | collective-permute-done | bytes 1048608 | tf_op jit(solution)/shard_map/ppermute | solution.py:135
  56.5 1.4 sum1.2
  58.0 1.4 sum2.2
  59.4 0.7 collective-permute-done.22.refs_1_
  60.1 2.7 %collective-permute-start.6 = (f32[4,128,512]{2,1,0:T(8,128)S(1)}, f32[4,128,512]{2,1,0:T(8,128)S(1)}, u32[]{:S(2)}, u32[]{:S(2)}) collective-permute-start(f32[4,128,512]{2,1,0:T(8,128)S(1)} %get-tuple-element.43), channel_id=1, source_target_pairs={{0,24},{1,7},{2,26},{3,1},{4,28},{5,3},{6,30},{7,5},{8,0},{9,15},{... | collective-permute-start | bytes 3145736 | tf_op jit(solution)/shard_map/ppermute | solution.py:135
  62.7 8.6 %collective-permute-done.27.refs_2_ = f32[4,128,512]{2,1,0:T(8,128)S(1)} collective-permute-done((f32[4,128,512]{2,1,0:T(8,128)S(1)}, f32[4,128,512]{2,1,0:T(8,128)S(1)}, u32[]{:S(2)}, u32[]{:S(2)}) %collective-permute-start.27) | collective-permute-done | bytes 1048608 | tf_op jit(solution)/shard_map/ppermute | solution.py:135
  71.3 1.4 collective-permute-start.11
  72.7 0.7 collective-permute-start.12
  73.3 2.5 %turn.3 = (f32[128,512]{1,0:T(8,128)}, f32[128,512]{1,0:T(8,128)}, f32[128,512]{1,0:T(8,128)S(1)}, f32[128,512]{1,0:T(8,128)S(1)}, f32[128,512]{1,0:T(8,128)S(1)...) custom-call(bf16[4,4,2,256,1024]{4,3,2,1,0:T(8,128)(2,1)} %bitcast.21, ...), custom_call_target="tpu_custom_call" | custom-call | flops 1000000 | bytes 4000000 | tf_op jit(solution)/shard_map/turn/pallas_call | solution.py:105
  75.9 0.7 copy-done.12
  76.6 3.0 %collective-permute-start.31 = (f32[128,512]{1,0:T(8,128)}, f32[128,512]{1,0:T(8,128)}, u32[]{:S(2)}, u32[]{:S(2)}) collective-permute-start(f32[128,512]{1,0:T(8,128)} %get-tuple-element.72), channel_id=1, source_target_pairs={{0,6},{1,25},{2,0},{3,27},{4,2},{5,29},{6,4},{7,31},{8,14},{9,1},{... | collective-permute-start | bytes 786440 | tf_op jit(solution)/shard_map/ppermute | solution.py:135
  79.6 4.1 %collective-permute-done.5.refs_0_ = f32[4,128,512]{2,1,0:T(8,128)S(1)} collective-permute-done((f32[4,128,512]{2,1,0:T(8,128)S(1)}, f32[4,128,512]{2,1,0:T(8,128)S(1)}, u32[]{:S(2)}, u32[]{:S(2)}) %collective-permute-start.5) | collective-permute-done | bytes 1048608 | tf_op jit(solution)/shard_map/ppermute | solution.py:135
  83.8 1.6 %collective-permute-start.32 = (f32[128,512]{1,0:T(8,128)}, f32[128,512]{1,0:T(8,128)}, u32[]{:S(2)}, u32[]{:S(2)}) collective-permute-start(f32[128,512]{1,0:T(8,128)} %get-tuple-element.73), channel_id=1, source_target_pairs={{0,2},{1,9},{2,4},{3,11},{4,6},{5,13},{6,0},{7,15},{8,10},{9,17},{... | collective-permute-start | bytes 786440 | tf_op jit(solution)/shard_map/ppermute | solution.py:135
  85.4 11.2 %collective-permute-done.11.refs_2_ = f32[4,128,512]{2,1,0:T(8,128)S(1)} collective-permute-done((f32[4,128,512]{2,1,0:T(8,128)S(1)}, f32[4,128,512]{2,1,0:T(8,128)S(1)}, u32[]{:S(2)}, u32[]{:S(2)}) %collective-permute-start.11) | collective-permute-done | bytes 1048608 | tf_op jit(solution)/shard_map/ppermute | solution.py:135
  96.6 1.2 collective-permute-done.12.refs_3_
  97.8 2.4 %turn.2 = (f32[128,512]{1,0:T(8,128)}, f32[128,512]{1,0:T(8,128)S(1)}, f32[128,512]{1,0:T(8,128)S(1)}, f32[128,512]{1,0:T(8,128)S(1)}, f32[128,512]{1,0:T(8,128)...) custom-call(bf16[4,4,2,256,1024]{4,3,2,1,0:T(8,128)(2,1)} %bitcast.22, ...), custom_call_target="tpu_custom_call" | custom-call | flops 1000000 | bytes 4000000 | tf_op jit(solution)/shard_map/turn/pallas_call | solution.py:105
  100.2 0.7 copy-done.7
  100.9 0.7 copy-done.9
  101.6 0.7 copy-done.13
  102.4 3.1 %collective-permute-start.15 = (f32[128,512]{1,0:T(8,128)}, f32[128,512]{1,0:T(8,128)}, u32[]{:S(2)}, u32[]{:S(2)}) collective-permute-start(f32[128,512]{1,0:T(8,128)} %get-tuple-element.54), channel_id=1, source_target_pairs={{0,6},{1,25},{2,0},{3,27},{4,2},{5,29},{6,4},{7,31},{8,14},{9,1},{... | collective-permute-start | bytes 786440 | tf_op jit(solution)/shard_map/ppermute | solution.py:135
  105.5 1.6 %collective-permute-start = (s32[4,4,128]{2,1,0:T(4,128)S(1)}, s32[4,4,128]{2,1,0:T(4,128)S(1)}, u32[]{:S(2)}, u32[]{:S(2)}) collective-permute-start(s32[4,4,128]{2,1,0:T(4,128)S(1)} %reshape.10.p0), channel_id=1, source_target_pairs={{0,32},{32,64},{64,96},{96,0},{1,33},{33,65},{65,97},{97,1},{2,34}... | collective-permute-start | bytes 24584 | tf_op jit(solution)/shard_map/ppermute | solution.py:139
  107.1 2.7 %collective-permute-start.1 = (s32[4,4,128]{2,1,0:T(4,128)S(1)}, s32[4,4,128]{2,1,0:T(4,128)S(1)}, u32[]{:S(2)}, u32[]{:S(2)}) collective-permute-start(s32[4,4,128]{2,1,0:T(4,128)S(1)} %reshape.10.p0), channel_id=1, source_target_pairs={{0,64},{32,96},{64,0},{96,32},{1,65},{33,97},{65,1},{97,33},{2,66}... | collective-permute-start | bytes 24584 | tf_op jit(solution)/shard_map/ppermute | solution.py:139
  109.8 0.6 collective-permute-start.29
  110.4 1.1 relay.3
  111.5 2.8 %collective-permute-start.30 = (f32[128,512]{1,0:T(8,128)}, f32[128,512]{1,0:T(8,128)S(1)}, u32[]{:S(2)}, u32[]{:S(2)}) collective-permute-start(f32[128,512]{1,0:T(8,128)} %copy-done.11), channel_id=1, source_target_pairs={{0,6},{1,25},{2,0},{3,27},{4,2},{5,29},{6,4},{7,31},{8,14},{9,1},{... | collective-permute-start | bytes 786440 | tf_op jit(solution)/shard_map/ppermute | solution.py:135
  114.3 2.0 %collective-permute-start.33 = (f32[128,512]{1,0:T(8,128)S(1)}, f32[128,512]{1,0:T(8,128)S(1)}, u32[]{:S(2)}, u32[]{:S(2)}) collective-permute-start(f32[128,512]{1,0:T(8,128)S(1)} %get-tuple-element.74), channel_id=1, source_target_pairs={{0,6},{1,25},{2,0},{3,27},{4,2},{5,29},{6,4},{7,31},{8,14},{9,1},{... | collective-permute-start | bytes 786440 | tf_op jit(solution)/shard_map/ppermute | solution.py:135
  116.3 1.4 collective-permute-start.2
  117.8 1.0 relay.2
  118.8 1.1 collective-permute-done.2.p3
  120.4 2.7 %collective-permute-start.14 = (f32[128,512]{1,0:T(8,128)S(1)}, f32[128,512]{1,0:T(8,128)S(1)}, u32[]{:S(2)}, u32[]{:S(2)}) collective-permute-start(f32[128,512]{1,0:T(8,128)S(1)} %copy-done.8), channel_id=1, source_target_pairs={{0,6},{1,25},{2,0},{3,27},{4,2},{5,29},{6,4},{7,31},{8,14},{9,1},{... | collective-permute-start | bytes 786440 | tf_op jit(solution)/shard_map/ppermute | solution.py:135
  123.2 0.9 collective-permute-start.17
  124.1 1.1 collective-permute-start.18
  125.9 4.3 %prep.1 = (bf16[4,4,256,512]{3,2,1,0:T(8,128)(2,1)S(1)}, f32[4,4,64,512]{3,2,1,0:T(8,128)S(1)}) custom-call(s32[4,4,128]{2,1,0:T(4,128)S(1)} %reshape.10.p0, s32[4,4,128]{2,1,0:T(4,128)S(1)} %collective-permute-done.p1, s32[4,4,128]{2,1,0:T(4,128)S(1)} %collective-permute-done.1.p2, s32[4,4,128]{2,1,0:T(4,128)S(1)} %collective-permute-done.2.p3, ...), custom_call_target="tpu_custom_call" | custom-call | flops 10000000 | bytes 20000000 | tf_op jit(solution)/shard_map/prep/pallas_call | solution.py:105
  130.2 1.0 values.3
  131.3 4.1 %collective-permute-start.39 = (f32[8,128]{1,0:T(8,128)S(1)}, f32[8,128]{1,0:T(8,128)S(1)}, u32[]{:S(2)}, u32[]{:S(2)}) collective-permute-start(f32[8,128]{1,0:T(8,128)S(1)} %get-tuple-element.77.v_ref.v0), channel_id=1, source_target_pairs={{0,64},{32,96},{64,0},{96,32},{1,65},{33,97},{65,1},{97,33},{2,66}... | collective-permute-start | bytes 12296 | tf_op jit(solution)/shard_map/ppermute | solution.py:139
  135.5 1.0 values.2
  136.5 2.1 %collective-permute-start.35 = (f32[8,128]{1,0:T(8,128)S(1)}, f32[8,128]{1,0:T(8,128)S(1)}, u32[]{:S(2)}, u32[]{:S(2)}) collective-permute-start(f32[8,128]{1,0:T(8,128)S(1)} %get-tuple-element.59.v_ref.v0), channel_id=1, source_target_pairs={{0,32},{32,64},{64,96},{96,0},{1,33},{33,65},{65,97},{97,1},{2,34}... | collective-permute-start | bytes 12296 | tf_op jit(solution)/shard_map/ppermute | solution.py:139
  138.7 2.6 %collective-permute-start.37 = (f32[8,128]{1,0:T(8,128)S(1)}, f32[8,128]{1,0:T(8,128)S(1)}, u32[]{:S(2)}, u32[]{:S(2)}) collective-permute-start(f32[8,128]{1,0:T(8,128)S(1)} %get-tuple-element.59.v_ref.v0), channel_id=1, source_target_pairs={{0,96},{32,0},{64,32},{96,64},{1,97},{33,1},{65,33},{97,65},{2,98}... | collective-permute-start | bytes 12296 | tf_op jit(solution)/shard_map/ppermute | solution.py:139
  141.4 1.9 %keep.2.refs_0_ = f32[256,1024]{1,0:T(8,128)} custom-call(f32[128,1024]{1,0:T(8,128)S(1)} %get-tuple-element.76.up_ref, f32[8,128]{1,0:T(8,128)S(1)} %get-tuple-element.77.v_ref.v0, bf16[256,256]{1,0:T(8,128)(2,1)S(1)} %copy-done.1, bf16[256,256]{1,0:T(8,128)(2,1)S(1)} %copy-done.2, bf16[4,4,256,512]{3,2,1,0:T(8,128)(2,1)S(1)} %get-tuple-element.40.bt_ref, ...), custom_call_target="tpu_custom_call" | custom-call | flops 1000000 | bytes 4000000 | tf_op jit(solution)/shard_map/keep/pallas_call | solution.py:105
  143.3 1.9 %keep.3 = f32[256,1024]{1,0:T(8,128)} custom-call(f32[128,1024]{1,0:T(8,128)S(1)} %get-tuple-element.58.up_ref, f32[8,128]{1,0:T(8,128)S(1)} %get-tuple-element.59.v_ref.v0, bf16[256,256]{1,0:T(8,128)(2,1)S(1)} %copy-done.1, bf16[256,256]{1,0:T(8,128)(2,1)S(1)} %copy-done.2, ...), custom_call_target="tpu_custom_call", output_to_operand_aliasing={{}: (6, {})} | custom-call | flops 1000000 | bytes 4000000 | tf_op jit(solution)/shard_map/keep/pallas_call | solution.py:105
  145.2 3.4 %update.2.refs_0_ = f32[256,1024]{1,0:T(8,128)} custom-call(f32[8,128]{1,0:T(8,128)S(1)} %get-tuple-element.77.v_ref.v0, f32[8,128]{1,0:T(8,128)S(1)} %collective-permute-done.38.v1, f32[8,128]{1,0:T(8,128)S(1)} %collective-permute-done.39.v2, f32[8,128]{1,0:T(8,128)S(1)} %collective-permute-done.40.v3, bf16[256,256]{1,0:T(8,128)(2,1)S(1)} %copy-done.1, ...), custom_call_target="tpu_custom_call" | custom-call | flops 1000000 | bytes 4000000 | tf_op jit(solution)/shard_map/update/pallas_call | solution.py:105
  148.7 3.4 %update.3 = f32[256,1024]{1,0:T(8,128)} custom-call(f32[8,128]{1,0:T(8,128)S(1)} %get-tuple-element.59.v_ref.v0, f32[8,128]{1,0:T(8,128)S(1)} %collective-permute-done.35.v1, f32[8,128]{1,0:T(8,128)S(1)} %collective-permute-done.36.v2, f32[8,128]{1,0:T(8,128)S(1)} %collective-permute-done.37.v3, ...), custom_call_target="tpu_custom_call", output_to_operand_aliasing={{}: (8, {})} | custom-call | flops 1000000 | bytes 4000000 | tf_op jit(solution)/shard_map/update/pallas_call | solution.py:105
  (74 shorter events, 1.9 us)
Async XLA Ops:
  2.0 8.4 %collective-permute-start.24 = (f32[2,4,128,512]{3,2,1,0:T(8,128)S(1)}, f32[2,4,128,512]{3,2,1,0:T(8,128)S(1)}, u32[]{:S(2)}, u32[]{:S(2)}) collective-permute-start(f32[2,4,128,512]{3,2,1,0:T(8,128)S(1)} %conv0.3), channel_id=1, source_target_pairs={{0,1},{1,0},{2,3},{3,2},{4,5},{5,4},{6,7},{7,6},{8,9},{9,8},{10,11... | collective-permute-start | bytes 6291464 | tf_op jit(solution)/shard_map/ppermute | solution.py:127
  3.5 8.8 %collective-permute-start.23 = (f32[2,4,128,512]{3,2,1,0:T(8,128)S(1)}, f32[2,4,128,512]{3,2,1,0:T(8,128)S(1)}, u32[]{:S(2)}, u32[]{:S(2)}) collective-permute-start(f32[2,4,128,512]{3,2,1,0:T(8,128)S(1)} %conv2.3), channel_id=1, source_target_pairs={{0,1},{1,0},{2,3},{3,2},{4,5},{5,4},{6,7},{7,6},{8,9},{9,8},{10,11... | collective-permute-start | bytes 6291464 | tf_op jit(solution)/shard_map/ppermute | solution.py:127
  5.5 8.4 %collective-permute-start.20 = (f32[2,4,128,512]{3,2,1,0:T(8,128)S(1)}, f32[2,4,128,512]{3,2,1,0:T(8,128)S(1)}, u32[]{:S(2)}, u32[]{:S(2)}) collective-permute-start(f32[2,4,128,512]{3,2,1,0:T(8,128)S(1)} %conv1.3), channel_id=1, source_target_pairs={{0,1},{1,0},{2,3},{3,2},{4,5},{5,4},{6,7},{7,6},{8,9},{9,8},{10,11... | collective-permute-start | bytes 6291464 | tf_op jit(solution)/shard_map/ppermute | solution.py:127
  7.0 11.1 %collective-permute-start.8 = (f32[2,4,128,512]{3,2,1,0:T(8,128)S(1)}, f32[2,4,128,512]{3,2,1,0:T(8,128)S(1)}, u32[]{:S(2)}, u32[]{:S(2)}) collective-permute-start(f32[2,4,128,512]{3,2,1,0:T(8,128)S(1)} %conv0.2), channel_id=1, source_target_pairs={{0,1},{1,0},{2,3},{3,2},{4,5},{5,4},{6,7},{7,6},{8,9},{9,8},{10,11... | collective-permute-start | bytes 6291464 | tf_op jit(solution)/shard_map/ppermute | solution.py:127
  8.9 12.0 %collective-permute-start.19 = (f32[2,4,128,512]{3,2,1,0:T(8,128)S(1)}, f32[2,4,128,512]{3,2,1,0:T(8,128)S(1)}, u32[]{:S(2)}, u32[]{:S(2)}) collective-permute-start(f32[2,4,128,512]{3,2,1,0:T(8,128)S(1)} %conv3.3), channel_id=1, source_target_pairs={{0,1},{1,0},{2,3},{3,2},{4,5},{5,4},{6,7},{7,6},{8,9},{9,8},{10,11... | collective-permute-start | bytes 6291464 | tf_op jit(solution)/shard_map/ppermute | solution.py:127
  10.4 11.7 %collective-permute-start.7 = (f32[2,4,128,512]{3,2,1,0:T(8,128)S(1)}, f32[2,4,128,512]{3,2,1,0:T(8,128)S(1)}, u32[]{:S(2)}, u32[]{:S(2)}) collective-permute-start(f32[2,4,128,512]{3,2,1,0:T(8,128)S(1)} %conv2.2), channel_id=1, source_target_pairs={{0,1},{1,0},{2,3},{3,2},{4,5},{5,4},{6,7},{7,6},{8,9},{9,8},{10,11... | collective-permute-start | bytes 6291464 | tf_op jit(solution)/shard_map/ppermute | solution.py:127
  12.3 23.3 %collective-permute-start.4 = (f32[2,4,128,512]{3,2,1,0:T(8,128)S(1)}, f32[2,4,128,512]{3,2,1,0:T(8,128)S(1)}, u32[]{:S(2)}, u32[]{:S(2)}) collective-permute-start(f32[2,4,128,512]{3,2,1,0:T(8,128)S(1)} %conv1.2), channel_id=1, source_target_pairs={{0,1},{1,0},{2,3},{3,2},{4,5},{5,4},{6,7},{7,6},{8,9},{9,8},{10,11... | collective-permute-start | bytes 6291464 | tf_op jit(solution)/shard_map/ppermute | solution.py:127
  13.8 16.5 %collective-permute-start.25 = (f32[4,128,512]{2,1,0:T(8,128)S(1)}, f32[4,128,512]{2,1,0:T(8,128)S(1)}, u32[]{:S(2)}, u32[]{:S(2)}) collective-permute-start(f32[4,128,512]{2,1,0:T(8,128)S(1)} %get-tuple-element.62), channel_id=1, source_target_pairs={{0,24},{1,7},{2,26},{3,1},{4,28},{5,3},{6,30},{7,5},{8,0},{9,15},{... | collective-permute-start | bytes 3145736 | tf_op jit(solution)/shard_map/ppermute | solution.py:135
  18.0 16.0 %collective-permute-start.26 = (f32[4,128,512]{2,1,0:T(8,128)S(1)}, f32[4,128,512]{2,1,0:T(8,128)S(1)}, u32[]{:S(2)}, u32[]{:S(2)}) collective-permute-start(f32[4,128,512]{2,1,0:T(8,128)S(1)} %get-tuple-element.63), channel_id=1, source_target_pairs={{0,8},{1,3},{2,10},{3,5},{4,12},{5,7},{6,14},{7,1},{8,16},{9,11},{... | collective-permute-start | bytes 3145736 | tf_op jit(solution)/shard_map/ppermute | solution.py:135
  20.8 24.4 %collective-permute-start.21 = (f32[4,128,512]{2,1,0:T(8,128)S(1)}, f32[4,128,512]{2,1,0:T(8,128)S(1)}, u32[]{:S(2)}, u32[]{:S(2)}) collective-permute-start(f32[4,128,512]{2,1,0:T(8,128)S(1)} %get-tuple-element.60), channel_id=1, source_target_pairs={{0,8},{1,3},{2,10},{3,5},{4,12},{5,7},{6,14},{7,1},{8,16},{9,11},{... | collective-permute-start | bytes 3145736 | tf_op jit(solution)/shard_map/ppermute | solution.py:135
  22.1 34.5 %collective-permute-start.10 = (f32[4,128,512]{2,1,0:T(8,128)S(1)}, f32[4,128,512]{2,1,0:T(8,128)S(1)}, u32[]{:S(2)}, u32[]{:S(2)}) collective-permute-start(f32[4,128,512]{2,1,0:T(8,128)S(1)} %get-tuple-element.45), channel_id=1, source_target_pairs={{0,8},{1,3},{2,10},{3,5},{4,12},{5,7},{6,14},{7,1},{8,16},{9,11},{... | collective-permute-start | bytes 3145736 | tf_op jit(solution)/shard_map/ppermute | solution.py:135
  30.4 46.2 %collective-permute-start.3 = (f32[2,4,128,512]{3,2,1,0:T(8,128)S(1)}, f32[2,4,128,512]{3,2,1,0:T(8,128)S(1)}, u32[]{:S(2)}, u32[]{:S(2)}) collective-permute-start(f32[2,4,128,512]{3,2,1,0:T(8,128)S(1)} %conv3.2), channel_id=1, source_target_pairs={{0,1},{1,0},{2,3},{3,2},{4,5},{5,4},{6,7},{7,6},{8,9},{9,8},{10,11... | collective-permute-start | bytes 6291464 | tf_op jit(solution)/shard_map/ppermute | solution.py:127
  34.0 23.9 %collective-permute-start.9 = (f32[4,128,512]{2,1,0:T(8,128)S(1)}, f32[4,128,512]{2,1,0:T(8,128)S(1)}, u32[]{:S(2)}, u32[]{:S(2)}) collective-permute-start(f32[4,128,512]{2,1,0:T(8,128)S(1)} %get-tuple-element.44), channel_id=1, source_target_pairs={{0,24},{1,7},{2,26},{3,1},{4,28},{5,3},{6,30},{7,5},{8,0},{9,15},{... | collective-permute-start | bytes 3145736 | tf_op jit(solution)/shard_map/ppermute | solution.py:135
  35.6 24.5 %collective-permute-start.22 = (f32[4,128,512]{2,1,0:T(8,128)S(1)}, f32[4,128,512]{2,1,0:T(8,128)S(1)}, u32[]{:S(2)}, u32[]{:S(2)}) collective-permute-start(f32[4,128,512]{2,1,0:T(8,128)S(1)} %get-tuple-element.61), channel_id=1, source_target_pairs={{0,24},{1,7},{2,26},{3,1},{4,28},{5,3},{6,30},{7,5},{8,0},{9,15},{... | collective-permute-start | bytes 3145736 | tf_op jit(solution)/shard_map/ppermute | solution.py:135
  45.3 26.0 %collective-permute-start.27 = (f32[4,128,512]{2,1,0:T(8,128)S(1)}, f32[4,128,512]{2,1,0:T(8,128)S(1)}, u32[]{:S(2)}, u32[]{:S(2)}) collective-permute-start(f32[4,128,512]{2,1,0:T(8,128)S(1)} %get-tuple-element.64), channel_id=1, source_target_pairs={{0,24},{1,7},{2,26},{3,1},{4,28},{5,3},{6,30},{7,5},{8,0},{9,15},{... | collective-permute-start | bytes 3145736 | tf_op jit(solution)/shard_map/ppermute | solution.py:135
  56.5 16.2 %collective-permute-start.28 = (f32[4,128,512]{2,1,0:T(8,128)S(1)}, f32[4,128,512]{2,1,0:T(8,128)S(1)}, u32[]{:S(2)}, u32[]{:S(2)}) collective-permute-start(f32[4,128,512]{2,1,0:T(8,128)S(1)} %get-tuple-element.65), channel_id=1, source_target_pairs={{0,8},{1,3},{2,10},{3,5},{4,12},{5,7},{6,14},{7,1},{8,16},{9,11},{... | collective-permute-start | bytes 3145736 | tf_op jit(solution)/shard_map/ppermute | solution.py:135
  57.9 25.9 %collective-permute-start.5 = (f32[4,128,512]{2,1,0:T(8,128)S(1)}, f32[4,128,512]{2,1,0:T(8,128)S(1)}, u32[]{:S(2)}, u32[]{:S(2)}) collective-permute-start(f32[4,128,512]{2,1,0:T(8,128)S(1)} %get-tuple-element.42), channel_id=1, source_target_pairs={{0,8},{1,3},{2,10},{3,5},{4,12},{5,7},{6,14},{7,1},{8,16},{9,11},{... | collective-permute-start | bytes 3145736 | tf_op jit(solution)/shard_map/ppermute | solution.py:135
  60.1 25.3 %collective-permute-start.6 = (f32[4,128,512]{2,1,0:T(8,128)S(1)}, f32[4,128,512]{2,1,0:T(8,128)S(1)}, u32[]{:S(2)}, u32[]{:S(2)}) collective-permute-start(f32[4,128,512]{2,1,0:T(8,128)S(1)} %get-tuple-element.43), channel_id=1, source_target_pairs={{0,24},{1,7},{2,26},{3,1},{4,28},{5,3},{6,30},{7,5},{8,0},{9,15},{... | collective-permute-start | bytes 3145736 | tf_op jit(solution)/shard_map/ppermute | solution.py:135
  71.3 25.3 %collective-permute-start.11 = (f32[4,128,512]{2,1,0:T(8,128)S(1)}, f32[4,128,512]{2,1,0:T(8,128)S(1)}, u32[]{:S(2)}, u32[]{:S(2)}) collective-permute-start(f32[4,128,512]{2,1,0:T(8,128)S(1)} %get-tuple-element.46), channel_id=1, source_target_pairs={{0,24},{1,7},{2,26},{3,1},{4,28},{5,3},{6,30},{7,5},{8,0},{9,15},{... | collective-permute-start | bytes 3145736 | tf_op jit(solution)/shard_map/ppermute | solution.py:135
  72.7 25.1 %collective-permute-start.12 = (f32[4,128,512]{2,1,0:T(8,128)S(1)}, f32[4,128,512]{2,1,0:T(8,128)S(1)}, u32[]{:S(2)}, u32[]{:S(2)}) collective-permute-start(f32[4,128,512]{2,1,0:T(8,128)S(1)} %get-tuple-element.47), channel_id=1, source_target_pairs={{0,8},{1,3},{2,10},{3,5},{4,12},{5,7},{6,14},{7,1},{8,16},{9,11},{... | collective-permute-start | bytes 3145736 | tf_op jit(solution)/shard_map/ppermute | solution.py:135
  75.9 0.7 copy-start.12
  76.6 23.6 %copy-start.11 = (f32[128,512]{1,0:T(8,128)}, f32[128,512]{1,0:T(8,128)S(1)}, u32[]{:S(2)}) copy-start(f32[128,512]{1,0:T(8,128)S(1)} %get-tuple-element.69) | copy-start | bytes 786436
  76.6 33.2 %collective-permute-start.31 = (f32[128,512]{1,0:T(8,128)}, f32[128,512]{1,0:T(8,128)}, u32[]{:S(2)}, u32[]{:S(2)}) collective-permute-start(f32[128,512]{1,0:T(8,128)} %get-tuple-element.72), channel_id=1, source_target_pairs={{0,6},{1,25},{2,0},{3,27},{4,2},{5,29},{6,4},{7,31},{8,14},{9,1},{... | collective-permute-start | bytes 786440 | tf_op jit(solution)/shard_map/ppermute | solution.py:135
  83.8 21.7 %copy-start.14 = (s32[1,4,16,32]{3,2,1,0:T(8,128)S(1)}, s32[1,4,16,32]{3,2,1,0:T(8,128)}, u32[]{:S(2)}) copy-start(s32[1,4,16,32]{3,2,1,0:T(8,128)} %param.12) | copy-start | bytes 24580
  83.8 26.1 %collective-permute-start.32 = (f32[128,512]{1,0:T(8,128)}, f32[128,512]{1,0:T(8,128)}, u32[]{:S(2)}, u32[]{:S(2)}) collective-permute-start(f32[128,512]{1,0:T(8,128)} %get-tuple-element.73), channel_id=1, source_target_pairs={{0,2},{1,9},{2,4},{3,11},{4,6},{5,13},{6,0},{7,15},{8,10},{9,17},{... | collective-permute-start | bytes 786440 | tf_op jit(solution)/shard_map/ppermute | solution.py:135
  100.2 0.7 copy-start.7
  100.9 0.7 copy-start.9
  101.6 0.7 copy-start.13
  102.3 23.5 %copy-start.5 = (bf16[64,64]{1,0:T(8,128)(2,1)S(1)}, bf16[64,64]{1,0:T(8,128)(2,1)}, u32[]{:S(2)}) copy-start(bf16[64,64]{1,0:T(8,128)(2,1)} %constant.16.clone.qh_ref) | copy-start | bytes 24580
  102.3 23.5 %copy-start.6 = (bf16[64,64]{1,0:T(8,128)(2,1)S(1)}, bf16[64,64]{1,0:T(8,128)(2,1)}, u32[]{:S(2)}) copy-start(bf16[64,64]{1,0:T(8,128)(2,1)} %constant.17.clone.ql_ref) | copy-start | bytes 24580
  102.3 27.8 %copy-start = (f32[1,256,1024]{2,1,0:T(8,128)S(1)}, f32[1,256,1024]{2,1,0:T(8,128)}, u32[]{:S(2)}) copy-start(f32[1,256,1024]{2,1,0:T(8,128)} %param.11) | copy-start | bytes 3145732
  102.3 27.9 %copy-start.3 = (bf16[256,256]{1,0:T(8,128)(2,1)S(1)}, bf16[256,256]{1,0:T(8,128)(2,1)}, u32[]{:S(2)}) copy-start(bf16[256,256]{1,0:T(8,128)(2,1)} %constant.12.clone.dh_ref) | copy-start | bytes 393220
  102.3 27.9 %copy-start.4 = (bf16[256,256]{1,0:T(8,128)(2,1)S(1)}, bf16[256,256]{1,0:T(8,128)(2,1)}, u32[]{:S(2)}) copy-start(bf16[256,256]{1,0:T(8,128)(2,1)} %constant.13.clone.dl_ref) | copy-start | bytes 393220
  102.4 13.9 %collective-permute-start.15 = (f32[128,512]{1,0:T(8,128)}, f32[128,512]{1,0:T(8,128)}, u32[]{:S(2)}, u32[]{:S(2)}) collective-permute-start(f32[128,512]{1,0:T(8,128)} %get-tuple-element.54), channel_id=1, source_target_pairs={{0,6},{1,25},{2,0},{3,27},{4,2},{5,29},{6,4},{7,31},{8,14},{9,1},{... | collective-permute-start | bytes 786440 | tf_op jit(solution)/shard_map/ppermute | solution.py:135
  105.5 14.4 %copy-start.10 = (f32[128,512]{1,0:T(8,128)S(1)}, f32[128,512]{1,0:T(8,128)}, u32[]{:S(2)}) copy-start(f32[128,512]{1,0:T(8,128)} %copy-done.9) | copy-start | bytes 786436
  105.5 14.9 %copy-start.8 = (f32[128,512]{1,0:T(8,128)S(1)}, f32[128,512]{1,0:T(8,128)}, u32[]{:S(2)}) copy-start(f32[128,512]{1,0:T(8,128)} %copy-done.7) | copy-start | bytes 786436
  105.5 6.0 %collective-permute-start = (s32[4,4,128]{2,1,0:T(4,128)S(1)}, s32[4,4,128]{2,1,0:T(4,128)S(1)}, u32[]{:S(2)}, u32[]{:S(2)}) collective-permute-start(s32[4,4,128]{2,1,0:T(4,128)S(1)} %reshape.10.p0), channel_id=1, source_target_pairs={{0,32},{32,64},{64,96},{96,0},{1,33},{33,65},{65,97},{97,1},{2,34}... | collective-permute-start | bytes 24584 | tf_op jit(solution)/shard_map/ppermute | solution.py:139
  107.1 7.2 %collective-permute-start.1 = (s32[4,4,128]{2,1,0:T(4,128)S(1)}, s32[4,4,128]{2,1,0:T(4,128)S(1)}, u32[]{:S(2)}, u32[]{:S(2)}) collective-permute-start(s32[4,4,128]{2,1,0:T(4,128)S(1)} %reshape.10.p0), channel_id=1, source_target_pairs={{0,64},{32,96},{64,0},{96,32},{1,65},{33,97},{65,1},{97,33},{2,66}... | collective-permute-start | bytes 24584 | tf_op jit(solution)/shard_map/ppermute | solution.py:139
  109.8 7.9 %collective-permute-start.16 = (f32[128,512]{1,0:T(8,128)}, f32[128,512]{1,0:T(8,128)S(1)}, u32[]{:S(2)}, u32[]{:S(2)}) collective-permute-start(f32[128,512]{1,0:T(8,128)} %copy-done.13), channel_id=1, source_target_pairs={{0,2},{1,9},{2,4},{3,11},{4,6},{5,13},{6,0},{7,15},{8,10},{9,17},{... | collective-permute-start | bytes 786440 | tf_op jit(solution)/shard_map/ppermute | solution.py:135
  109.8 10.6 %collective-permute-start.29 = (f32[128,512]{1,0:T(8,128)}, f32[128,512]{1,0:T(8,128)S(1)}, u32[]{:S(2)}, u32[]{:S(2)}) collective-permute-start(f32[128,512]{1,0:T(8,128)} %copy-done.12), channel_id=1, source_target_pairs={{0,2},{1,9},{2,4},{3,11},{4,6},{5,13},{6,0},{7,15},{8,10},{9,17},{... | collective-permute-start | bytes 786440 | tf_op jit(solution)/shard_map/ppermute | solution.py:135
  111.5 11.7 %collective-permute-start.30 = (f32[128,512]{1,0:T(8,128)}, f32[128,512]{1,0:T(8,128)S(1)}, u32[]{:S(2)}, u32[]{:S(2)}) collective-permute-start(f32[128,512]{1,0:T(8,128)} %copy-done.11), channel_id=1, source_target_pairs={{0,6},{1,25},{2,0},{3,27},{4,2},{5,29},{6,4},{7,31},{8,14},{9,1},{... | collective-permute-start | bytes 786440 | tf_op jit(solution)/shard_map/ppermute | solution.py:135
  114.3 9.8 %collective-permute-start.33 = (f32[128,512]{1,0:T(8,128)S(1)}, f32[128,512]{1,0:T(8,128)S(1)}, u32[]{:S(2)}, u32[]{:S(2)}) collective-permute-start(f32[128,512]{1,0:T(8,128)S(1)} %get-tuple-element.74), channel_id=1, source_target_pairs={{0,6},{1,25},{2,0},{3,27},{4,2},{5,29},{6,4},{7,31},{8,14},{9,1},{... | collective-permute-start | bytes 786440 | tf_op jit(solution)/shard_map/ppermute | solution.py:135
  116.3 3.7 %collective-permute-start.2 = (s32[4,4,128]{2,1,0:T(4,128)S(1)}, s32[4,4,128]{2,1,0:T(4,128)S(1)}, u32[]{:S(2)}, u32[]{:S(2)}) collective-permute-start(s32[4,4,128]{2,1,0:T(4,128)S(1)} %reshape.10.p0), channel_id=1, source_target_pairs={{0,96},{32,0},{64,32},{96,64},{1,97},{33,1},{65,33},{97,65},{2,98}... | collective-permute-start | bytes 24584 | tf_op jit(solution)/shard_map/ppermute | solution.py:139
  117.7 12.5 %collective-permute-start.34 = (f32[128,512]{1,0:T(8,128)S(1)}, f32[128,512]{1,0:T(8,128)S(1)}, u32[]{:S(2)}, u32[]{:S(2)}) collective-permute-start(f32[128,512]{1,0:T(8,128)S(1)} %get-tuple-element.75), channel_id=1, source_target_pairs={{0,2},{1,9},{2,4},{3,11},{4,6},{5,13},{6,0},{7,15},{8,10},{9,17},{... | collective-permute-start | bytes 786440 | tf_op jit(solution)/shard_map/ppermute | solution.py:135
  119.9 11.4 %collective-permute-start.13 = (f32[128,512]{1,0:T(8,128)S(1)}, f32[128,512]{1,0:T(8,128)S(1)}, u32[]{:S(2)}, u32[]{:S(2)}) collective-permute-start(f32[128,512]{1,0:T(8,128)S(1)} %copy-done.10), channel_id=1, source_target_pairs={{0,2},{1,9},{2,4},{3,11},{4,6},{5,13},{6,0},{7,15},{8,10},{9,17},{... | collective-permute-start | bytes 786440 | tf_op jit(solution)/shard_map/ppermute | solution.py:135
  120.4 15.0 %collective-permute-start.14 = (f32[128,512]{1,0:T(8,128)S(1)}, f32[128,512]{1,0:T(8,128)S(1)}, u32[]{:S(2)}, u32[]{:S(2)}) collective-permute-start(f32[128,512]{1,0:T(8,128)S(1)} %copy-done.8), channel_id=1, source_target_pairs={{0,6},{1,25},{2,0},{3,27},{4,2},{5,29},{6,4},{7,31},{8,14},{9,1},{... | collective-permute-start | bytes 786440 | tf_op jit(solution)/shard_map/ppermute | solution.py:135
  123.2 12.3 %collective-permute-start.17 = (f32[128,512]{1,0:T(8,128)S(1)}, f32[128,512]{1,0:T(8,128)S(1)}, u32[]{:S(2)}, u32[]{:S(2)}) collective-permute-start(f32[128,512]{1,0:T(8,128)S(1)} %get-tuple-element.56), channel_id=1, source_target_pairs={{0,6},{1,25},{2,0},{3,27},{4,2},{5,29},{6,4},{7,31},{8,14},{9,1},{... | collective-permute-start | bytes 786440 | tf_op jit(solution)/shard_map/ppermute | solution.py:135
  124.1 11.4 %collective-permute-start.18 = (f32[128,512]{1,0:T(8,128)S(1)}, f32[128,512]{1,0:T(8,128)S(1)}, u32[]{:S(2)}, u32[]{:S(2)}) collective-permute-start(f32[128,512]{1,0:T(8,128)S(1)} %get-tuple-element.57), channel_id=1, source_target_pairs={{0,2},{1,9},{2,4},{3,11},{4,6},{5,13},{6,0},{7,15},{8,10},{9,17},{... | collective-permute-start | bytes 786440 | tf_op jit(solution)/shard_map/ppermute | solution.py:135
  131.3 7.5 %collective-permute-start.38 = (f32[8,128]{1,0:T(8,128)S(1)}, f32[8,128]{1,0:T(8,128)S(1)}, u32[]{:S(2)}, u32[]{:S(2)}) collective-permute-start(f32[8,128]{1,0:T(8,128)S(1)} %get-tuple-element.77.v_ref.v0), channel_id=1, source_target_pairs={{0,32},{32,64},{64,96},{96,0},{1,33},{33,65},{65,97},{97,1},{2,34}... | collective-permute-start | bytes 12296 | tf_op jit(solution)/shard_map/ppermute | solution.py:139
  131.3 13.8 %collective-permute-start.39 = (f32[8,128]{1,0:T(8,128)S(1)}, f32[8,128]{1,0:T(8,128)S(1)}, u32[]{:S(2)}, u32[]{:S(2)}) collective-permute-start(f32[8,128]{1,0:T(8,128)S(1)} %get-tuple-element.77.v_ref.v0), channel_id=1, source_target_pairs={{0,64},{32,96},{64,0},{96,32},{1,65},{33,97},{65,1},{97,33},{2,66}... | collective-permute-start | bytes 12296 | tf_op jit(solution)/shard_map/ppermute | solution.py:139
  135.4 9.8 %collective-permute-start.40 = (f32[8,128]{1,0:T(8,128)S(1)}, f32[8,128]{1,0:T(8,128)S(1)}, u32[]{:S(2)}, u32[]{:S(2)}) collective-permute-start(f32[8,128]{1,0:T(8,128)S(1)} %get-tuple-element.77.v_ref.v0), channel_id=1, source_target_pairs={{0,96},{32,0},{64,32},{96,64},{1,97},{33,1},{65,33},{97,65},{2,98}... | collective-permute-start | bytes 12296 | tf_op jit(solution)/shard_map/ppermute | solution.py:139
  135.5 5.9 %copy-start.1 = (bf16[256,256]{1,0:T(8,128)(2,1)S(1)}, bf16[256,256]{1,0:T(8,128)(2,1)}, u32[]{:S(2)}) copy-start(bf16[256,256]{1,0:T(8,128)(2,1)} %constant.14.clone.eh_ref) | copy-start | bytes 393220
  135.5 5.9 %copy-start.2 = (bf16[256,256]{1,0:T(8,128)(2,1)S(1)}, bf16[256,256]{1,0:T(8,128)(2,1)}, u32[]{:S(2)}) copy-start(bf16[256,256]{1,0:T(8,128)(2,1)} %constant.15.clone.el_ref) | copy-start | bytes 393220
  136.5 12.1 %collective-permute-start.35 = (f32[8,128]{1,0:T(8,128)S(1)}, f32[8,128]{1,0:T(8,128)S(1)}, u32[]{:S(2)}, u32[]{:S(2)}) collective-permute-start(f32[8,128]{1,0:T(8,128)S(1)} %get-tuple-element.59.v_ref.v0), channel_id=1, source_target_pairs={{0,32},{32,64},{64,96},{96,0},{1,33},{33,65},{65,97},{97,1},{2,34}... | collective-permute-start | bytes 12296 | tf_op jit(solution)/shard_map/ppermute | solution.py:139
  138.6 10.0 %collective-permute-start.36 = (f32[8,128]{1,0:T(8,128)S(1)}, f32[8,128]{1,0:T(8,128)S(1)}, u32[]{:S(2)}, u32[]{:S(2)}) collective-permute-start(f32[8,128]{1,0:T(8,128)S(1)} %get-tuple-element.59.v_ref.v0), channel_id=1, source_target_pairs={{0,64},{32,96},{64,0},{96,32},{1,65},{33,97},{65,1},{97,33},{2,66}... | collective-permute-start | bytes 12296 | tf_op jit(solution)/shard_map/ppermute | solution.py:139
  138.7 9.9 %collective-permute-start.37 = (f32[8,128]{1,0:T(8,128)S(1)}, f32[8,128]{1,0:T(8,128)S(1)}, u32[]{:S(2)}, u32[]{:S(2)}) collective-permute-start(f32[8,128]{1,0:T(8,128)S(1)} %get-tuple-element.59.v_ref.v0), channel_id=1, source_target_pairs={{0,96},{32,0},{64,32},{96,64},{1,97},{33,1},{65,33},{97,65},{2,98}... | collective-permute-start | bytes 12296 | tf_op jit(solution)/shard_map/ppermute | solution.py:139

commit v2 on v0

v2 whole, which is shorter than its diff:
```python
import functools

import jax
import jax.numpy as jnp
import numpy as np
from jax import lax
from jax.experimental import pallas as pl
from jax.experimental.pallas import tpu as pltpu
from jax.sharding import PartitionSpec as P

SPAN = 64
DECAY = 0.999
NZ, NY, NC, NX = 4, 4, 2, 4
ROWS, COLS = 256, 1024
HW = COLS // 2
TOPK = 32
AHEAD = (200_000_000_000, 1_000_000_000)
SLOTS = 8
NA, NT, TILE = ROWS // SPAN, 4, 256
PARTS = ((0, 128), (128, 128))
OFFSETS = ((2, 2), (1, -1), (-1, 1), (0, 0))
F32, BF16 = jnp.float32, jnp.bfloat16


def vm(shape, dtype=F32):
    return pltpu.VMEM(shape, dtype)


VSPEC = pl.BlockSpec(memory_space=pltpu.VMEM)
ASPEC = pl.BlockSpec(memory_space=pl.ANY)


def position():
    s = lax.axis_index("shard")
    return lax.axis_index("grp"), s // (NY * NC), (s // NC) % NY, s % NC


def axes(other=False):
    _, z, y, c = position()
    c = 1 - c if other else c
    return c, jnp.where(c == 0, z, y), jnp.where(c == 0, y, z)


def fetch(g_ref, buf, sems, stage, r0, rows, other):
    core, first, _ = axes(other)
    copies = {}
    for h in range(2):
        mine = (first + (OFFSETS[stage][h] + 4)) % 4
        for s in range(4):
            z, y = jnp.where(core == 0, mine, s), jnp.where(core == 0, s, mine)
            src = g_ref.at[z, y, core, pl.ds(r0, rows), pl.ds(h * HW, HW)]
            copies[h, s] = pltpu.make_async_copy(src, buf.at[h, s], sems.at[h, s])
            copies[h, s].start()
    return copies


def conv_kernel(stages, r0, rows, g_ref, w_ref, buf, sems, wide, wide_sems):
    copies = [fetch(g_ref, buf.at[i], sems.at[i], stage, r0, rows, True) for i, stage in enumerate(stages)]
    out = []
    for i in range(len(stages)):
        for (h, s), cp in copies[i].items():
            cp.wait()
            slot = len(out) % SLOTS
            if len(out) >= SLOTS:
                out[-SLOTS].wait()
            wide[slot] = buf[i, h, s].astype(F32)
            out.append(pltpu.make_async_copy(wide.at[slot], w_ref.at[i, h, s], wide_sems.at[slot]))
            out[-1].start()
    for cp in out[-SLOTS:]:
        cp.wait()


def near_conv_kernel(stages, r0, rows, g_ref, w_ref, buf, sems):
    copies = [fetch(g_ref, buf.at[i], sems.at[i], stage, r0, rows, True) for i, stage in enumerate(stages)]
    for i in range(len(stages)):
        for (h, s), cp in copies[i].items():
            cp.wait()
            w_ref[i, h, s] = buf[i, h, s].astype(F32)


class Terms:
    def __init__(self, stage, r0, rows, g_ref, r_ref, at, messages, staging, near=False):
        (i, first_row), (own, other, more, sems) = at, staging
        self.own, self.other, self.more = own, r_ref.at[i] if near else other, None if messages is None else more
        self.copies = {key: [cp] for key, cp in fetch(g_ref, own, sems.at[0], stage, r0, rows, False).items()}
        for h, s in self.copies:
            src = r_ref.at[i, h, s, pl.ds(r0 - first_row, rows)]
            if not near:
                self.copies[h, s].append(pltpu.make_async_copy(src, other.at[h, s], sems.at[1, h, s]))
            if messages is not None:
                self.copies[h, s].append(pltpu.make_async_copy(messages[h].at[s], more.at[h, s], sems.at[2, h, s]))
            for cp in self.copies[h, s][1:]:
                cp.start()

    def get(self, h, s):
        for cp in self.copies[h, s]:
            cp.wait()
        total = self.own[h, s].astype(F32) + self.other[h, s]
        return total if self.more is None else total + self.more[h, s]


def send_kernel(at, r0, rows, g_ref, *refs):
    (*others, minus, plus), staging = refs[:-4], refs[-4:]
    near = len(others) == 2
    terms = [
        Terms(i, r0, rows, g_ref, others[i % len(others)], at[i], None, [ref.at[i] for ref in staging], near)
        for i in range(2)
    ]
    for i, to in enumerate(((minus, plus), (plus, minus))):
        for h in range(2):
            for s in range(4):
                to[h][i, s] = terms[i].get(h, s)


def pass_kernel(at, r0, rows, g_ref, r_ref, minus, plus, *refs):
    terms = Terms(2, r0, rows, g_ref, r_ref, at, (minus.at[0], plus.at[0]), refs[2:])
    for h in range(2):
        for s in range(4):
            refs[h][s] = terms.get(h, s)


def before_kernel(at, r0, rows, g_ref, r_ref, minus, plus, out_ref, *staging):
    terms = Terms(3, r0, rows, g_ref, r_ref, at, (plus.at[1], minus.at[1]), staging)
    for h in range(2):
        for s in range(4):
            out_ref[h, s] = terms.get(h, s)


def turn_kernel(sum_ref, relay0, relay1, *refs):
    (minus, plus), left, own = refs[0:2], refs[2:4], refs[4:6]
    to = ((minus.at[0], plus.at[0]), (plus.at[1], minus.at[1]), left, own)
    _, _, here = axes()
    for stage in range(4):
        for h in range(2):
            s = (here + (OFFSETS[stage][h] + 4)) % 4
            to[stage][h][...] = sum_ref[h, s] + (relay0, relay1)[h][s]


def relay_kernel(*refs):
    for h in range(2):
        refs[4 + h][...] = refs[h][...] + refs[2 + h][0]


def call(body, outs, args, name, scratch=(), limit=8, cost=(1_000_000, 4_000_000), onto=None, after=()):
    space = {"v": pltpu.VMEM, "h": pltpu.HBM}
    spec = {"v": VSPEC, "h": ASPEC, "a": ASPEC, "s": pl.BlockSpec(memory_space=pltpu.SMEM)}
    vals = [pltpu.with_memory_space_constraint(a, space[kind]) if kind in space else a for a, kind in args]
    in_specs = [spec[kind] for _, kind in args]
    outs = list(outs) if isinstance(outs, (list, tuple)) else [outs]
    aliases = {}
    if onto is not None:
        vals, in_specs, aliases = vals + [onto], in_specs + [ASPEC], {len(vals): 0}
    n_read, n_all, n_out = len(vals), len(vals) + len(after), len(outs)

    def kernel(*refs):
        outs_at = n_all + n_out
        refs[outs_at][...] = jnp.zeros((8, 128), F32)
        body(*refs[:n_read], *refs[n_all:outs_at], *refs[outs_at + 1 :])

    vals, in_specs = vals + list(after), in_specs + [ASPEC] * len(after)
    return pl.pallas_call(
        kernel,
        out_shape=outs + [vm((8, 128))],
        in_specs=in_specs,
        out_specs=[ASPEC if isinstance(o, jax.ShapeDtypeStruct) else VSPEC for o in outs] + [VSPEC],
        scratch_shapes=list(scratch),
        input_output_aliases=aliases,
        compiler_params=pltpu.CompilerParams(vmem_limit_bytes=limit * 2**20),
        cost_estimate=pl.CostEstimate(flops=cost[0], bytes_accessed=cost[1], transcendentals=0),
        name=name,
    )(*vals)


def place(z, y, c):
    return (z % NZ * NY + y % NY) * NC + c % NC


def everywhere():
    return [(z, y, c) for z in range(NZ) for y in range(NY) for c in range(NC)]


def to_other_core(x):
    return lax.ppermute(x, "shard", [(place(z, y, c), place(z, y, c + 1)) for z, y, c in everywhere()])


def along(x, step, second=False):
    pairs = []
    for z, y, c in everywhere():
        to = (z + step, y, c) if (c == 0) != second else (z, y + step, c)
        pairs.append((place(z, y, c), place(*to)))
    return lax.ppermute(x, "shard", pairs)


def swap_grp(x, k):
    return lax.ppermute(x, "grp", [(i, i ^ k) for i in range(NX)])


def other_core(g, stages, r0, rows, after=()):
    n = len(stages)
    shape = (n, 2, 4, rows, HW)
    scratch = [pltpu.VMEM(shape, BF16), pltpu.SemaphoreType.DMA((n, 2, 4))]
    if n == 1:
        body, out = near_conv_kernel, vm(shape)
    else:
        body, out = conv_kernel, jax.ShapeDtypeStruct(shape, F32)
        scratch = scratch + [pltpu.VMEM((SLOTS, rows, HW), F32), pltpu.SemaphoreType.DMA((SLOTS,))]
    body = functools.partial(body, stages, r0, rows)
    w, done = call(body, out, [(g, "h")], f"conv{stages[0]}", scratch, limit=12, after=after)
    got = to_other_core(w)
    return {stage: (got, (i, r0)) for i, stage in enumerate(stages)}, done


class Part:
    def __init__(self, g, r0, rows, got):
        self.g, self.r0, self.rows, self.got = g, r0, rows, got
        self.small = vm((rows, HW))

    def staging(self, *lead):
        shape = lead + (2, 4, self.rows, HW)
        return [pltpu.VMEM(shape, BF16), pltpu.VMEM(shape, F32)]

    def kernel(self, body, at, outs, args, name, scratch, after, kind="a", **kwargs):
        body = functools.partial(body, at, self.r0, self.rows)
        args = [(self.g, "h")] + [(x, kind) for x in args]
        return call(body, outs, args, name, scratch, limit=14, after=after, **kwargs)

    def both(self, out, second):
        return [along(out[0], -1, second), along(out[1], 1, second)]

    def send(self, after=(), **kwargs):
        outs = [vm((2, 4, self.rows, HW))] * 2
        (ra, ia), (rb, ib) = self.got[0], self.got[1]
        scratch = self.staging(2) + [pltpu.VMEM((2, 8, 128), F32), pltpu.SemaphoreType.DMA((2, 3, 2, 4))]
        args, kind = ([ra], "a") if ra is rb else ([ra, rb], "v")
        *out, done = self.kernel(send_kernel, (ia, ib), outs, args, "send", scratch, after, kind, **kwargs)
        self.first = self.both(out, False)
        return done

    def add(self, body, stage, outs, name, after):
        r, at = self.got[stage]
        own, other = self.staging()
        scratch = [own, other, other, pltpu.SemaphoreType.DMA((3, 2, 4))]
        return self.kernel(body, at, outs, [r] + self.first, name, scratch, after)

    def on(self, after=()):
        *out, done = self.add(pass_kernel, 2, [vm((4, self.rows, HW))] * 2, "pass", after)
        self.relay = self.both(out, False)
        return done

    def before(self, after=()):
        self.sums, done = self.add(before_kernel, 3, vm((2, 4, self.rows, HW)), "before", after)
        return done

    def turn(self, after=()):
        outs = [vm((2, self.rows, HW))] * 2 + [self.small] * 4
        *out, done = call(turn_kernel, outs, [(x, "v") for x in [self.sums] + self.relay], "turn", after=after)
        self.first2 = self.both(out, True)
        self.left, self.own = out[2:4], out[4:6]
        return done

    def on2(self, after=()):
        args = [(x, "v") for x in list(self.left) + self.first2]
        *out, done = call(relay_kernel, [self.small] * 2, args, "relay", after=after)
        self.relay2 = self.both(out, True)
        return done

    def terms(self):
        return list(self.own) + self.relay2 + self.first2[::-1]


def split(x):
    high = x.astype(BF16)
    return high, (x - high.astype(F32)).astype(BF16)


def dot(a, b, last=False):
    return lax.dot_general(a, b, (((1,), (1 if last else 0,)), ((), ())), preferred_element_type=F32)


def dot3(x, high, low):
    xh, xl = split(x)
    n = x.shape[0]
    both = dot(jnp.concatenate([xh, xl], axis=0), high)
    return both[:n] + both[n:] + dot(xh, low)


def basis():
    k, n = np.arange(SPAN)[:, None], np.arange(SPAN)[None, :]
    q = np.sqrt(np.where(k == 0, 1.0, 2.0) / SPAN) * np.cos(np.pi * (2 * n + 1) * k / (2 * SPAN))
    return q, np.kron(np.eye(TILE // SPAN), q.T)


def halves_of(m):
    high = m.astype(np.float32).astype(jnp.bfloat16)
    low = (m - high.astype(np.float64)).astype(np.float32).astype(jnp.bfloat16)
    return [jnp.asarray(high), jnp.asarray(low)]


def entries(p, qh_ref, ql_ref):
    block = lax.broadcasted_iota(jnp.int32, (1, 128), 1) // TOPK * SPAN
    hit = lax.broadcasted_iota(jnp.int32, (TILE, 128), 0) == p % SPAN + block
    at = jnp.where(lax.broadcasted_iota(jnp.int32, (SPAN, 128), 0) == p // SPAN, 1.0, 0.0).astype(BF16)
    return jnp.where(hit, 1.0, 0.0), dot(qh_ref[...], at) + dot(ql_ref[...], at)


def own_kernel(p_ref, qh_ref, ql_ref, bt_ref, b_ref, l_ref):
    @pl.loop(0, NA)
    def _(a):
        for t in range(NT):
            hit, l_ref[a, t] = entries(p_ref[a, t : t + 1, :], qh_ref, ql_ref)
            bt_ref[a, t] = hit.astype(BF16)
            b_ref[a, t] = hit.T.astype(BF16)


def tables_kernel(x0, x1, x2, x3, qh_ref, ql_ref, b_ref, l_ref):
    me = position()[0]
    n = NA * NT
    for i, ref in enumerate((x0, x1, x2, x3)):
        place = pl.ds(pl.multiple_of((me ^ i) * 128, 128), 128)
        p = ref[n:, :].astype(jnp.int32)
        block = lax.broadcasted_iota(jnp.int32, (n, 128), 1) // TOPK * SPAN
        cols = jnp.concatenate([p % SPAN + block] * (128 // n), axis=0).astype(F32).T.astype(jnp.int32)
        for k in range(n):
            hit = lax.broadcasted_iota(jnp.int32, (128, TILE), 1) == cols[:, k : k + 1]
            b_ref[k // NT, k % NT, place, :] = jnp.where(hit, 1.0, 0.0).astype(BF16)
            at = lax.broadcasted_iota(jnp.int32, (SPAN, 128), 0) == p[k : k + 1] // SPAN
            at = jnp.where(at, 1.0, 0.0).astype(BF16)
            l_ref[k // NT, k % NT, :, place] = dot(qh_ref[...], at) + dot(ql_ref[...], at)


def values_kernel(r0, rows, m_ref, count_ref, p_ref, dh_ref, dl_ref, bt_ref, l_ref, *refs):
    own, relay, direct, (*before, up_ref, v_ref) = refs[0:2], refs[2:4], refs[4:6], refs[6:]
    for h in range(2):
        got = own[h][...] + relay[h][...] + direct[h][1]
        up_ref[:, pl.ds(h * HW, HW)] = DECAY * m_ref[pl.ds(r0, rows), pl.ds(h * HW, HW)] + got
    live = lax.broadcasted_iota(jnp.int32, (1, 128), 1) % TOPK < count_ref[0]
    a0, n = r0 // SPAN, v_ref.shape[0]
    if before:
        v_ref[: NT * a0, :] = before[0][...]
    for t in range(NT):
        zh, zl = split(dot3(up_ref[:, pl.ds(t * TILE, TILE)], dh_ref[...], dl_ref[...]))
        for i in range(rows // SPAN):
            at = slice(i * SPAN, (i + 1) * SPAN)
            got = dot(jnp.concatenate([zh[at], zl[at]], axis=0), bt_ref[a0 + i, t])
            v = jnp.sum((got[:SPAN] + got[SPAN:]) * l_ref[a0 + i, t], axis=0, keepdims=True)
            row = NT * (a0 + i) + t
            v_ref[row : row + 1, :] = jnp.where(live, v, 0.0)
    if n == 2 * NT * NA:
        for a in range(NA):
            v_ref[NT * (NA + a) : NT * (NA + a + 1), :] = p_ref[a].astype(F32)


def row_fields(a, v_ref, l_ref, b_ref, eh_ref, el_ref):
    got = []
    for t in range(NT):
        high, low = split(l_ref[a, t] * v_ref[NT * a + t : NT * a + t + 1, :])
        both = dot(jnp.concatenate([high, low], axis=0), b_ref[a, t])
        got.append(both[:SPAN] + both[SPAN:])
    return dot3(jnp.concatenate(got, axis=0), eh_ref[...], el_ref[...])


def keep_kernel(up0_ref, up1_ref, v_ref, eh_ref, el_ref, b_ref, l_ref, out_ref, buf, sems):
    copies = []
    for a in range(NA):
        rows = pl.ds(a * SPAN, SPAN)
        got = row_fields(a, v_ref, l_ref, b_ref, eh_ref, el_ref)
        for t in range(NT):
            cols = pl.ds(t * TILE, TILE)
            up_ref, r0 = (up0_ref, 0) if a * SPAN < PARTS[1][0] else (up1_ref, PARTS[1][0])
            buf[rows, cols] = up_ref[pl.ds(a * SPAN - r0, SPAN), cols] - got[t * SPAN : (t + 1) * SPAN]
        copies.append(pltpu.make_async_copy(buf.at[rows], out_ref.at[rows], sems.at[a]))
        copies[-1].start()
    for cp in copies:
        cp.wait()


def update_kernel(v0, v1, v2, v3, eh_ref, el_ref, b_ref, l_ref, out_ref, buf, vals, sems):
    me = position()[0]
    for i, ref in enumerate((v0, v1, v2, v3)):
        vals[:, pl.ds(pl.multiple_of((me ^ i) * 128, 128), 128)] = ref[: NT * NA, :] * (1.0 / NX)
    copies = []
    for a in range(NA):
        rows = pl.ds(a * SPAN, SPAN)
        got = row_fields(a, vals, l_ref, b_ref, eh_ref, el_ref)
        for t in range(NT):
            buf[rows, pl.ds(t * TILE, TILE)] = got[t * SPAN : (t + 1) * SPAN]
        copies.append(pltpu.make_async_copy(buf.at[rows], out_ref.at[rows], sems.at[a]))
        copies[-1].start()
    for cp in copies:
        cp.wait()


def from_groups(x):
    return [x] + [swap_grp(x, k) for k in (1, 2, 3)]


def per_device(grads, momentum, positions, counts):
    g = grads.reshape(NZ, NY, NC, ROWS, COLS)
    q, four = basis()
    dh, dl = halves_of(four)
    eh, el = halves_of(four.T)
    qh, ql = halves_of(q.T)
    places = positions.reshape(NA, NT, 128)
    (a0, a_rows), (b0, b_rows) = PARTS
    got_a, n = other_core(g, (0,), a0, a_rows)
    got, n = other_core(g, (1,), a0, a_rows, [n])
    got_a.update(got)
    got_b, n = other_core(g, (0, 1), b0, b_rows, [n, got_a[0][0]])
    first, last = parts = [Part(g, a0, a_rows, got_a), Part(g, b0, b_rows, got_b)]
    n = first.send([n], cost=AHEAD)
    n = last.send([n])
    got, n = other_core(g, (2, 3), 0, ROWS, [n])
    got_a.update(got)
    got_b.update(got)
    bt, b, l, n = call(
        own_kernel,
        [vm((NA, NT, TILE, 128), BF16), vm((NA, NT, 128, TILE), BF16), vm((NA, NT, SPAN, 128))],
        [(places, "v"), (qh, "v"), (ql, "v")],
        "own",
        cost=AHEAD,
        after=[n] + first.first,
    )
    n = first.on([n])
    n = first.before([n])
    n = last.on([n])
    n = first.turn([n])
    n = last.before([n])
    n = last.turn([n])
    n = first.on2([n])
    n = last.on2([n])
    ups, vs = [], []
    for part in parts:
        n_rows = NT * (part.r0 + part.rows) // SPAN * (2 if part is last else 1)
        up, v, n = call(
            functools.partial(values_kernel, part.r0, part.rows),
            [vm((part.rows, COLS)), vm((n_rows, 128))],
            [(momentum[0], "v"), (counts, "s"), (places, "v"), (dh, "v"), (dl, "v"), (bt, "v"), (l, "v")]
            + [(x, "v") for x in part.terms() + vs],
            "values",
            after=[n],
        )
        ups, vs = ups + [up], [v]
    whole = jax.ShapeDtypeStruct((ROWS, COLS), F32)
    scratch = [pltpu.VMEM((ROWS, COLS), F32), pltpu.SemaphoreType.DMA((NA,))]
    vs = from_groups(v)
    kept, _ = call(keep_kernel, whole, [(x, "v") for x in (*ups, v, eh, el, b, l)], "keep", scratch)
    *tables, _ = call(
        tables_kernel,
        [vm((NA, NT, NX * 128, TILE), BF16), vm((NA, NT, SPAN, NX * 128))],
        [(x, "v") for x in vs + [qh, ql]],
        "tables",
    )
    update, _ = call(
        update_kernel,
        whole,
        [(x, "v") for x in vs + [eh, el] + tables],
        "update",
        [scratch[0], pltpu.VMEM((NT * NA, NX * 128), F32), scratch[1]],
    )
    return kept[None], update


def solution(mesh):
    in_specs = (
        P("grp", "shard", None, None),
        P("grp", "shard", None),
        P("grp", "shard", None, None),
        P("grp"),
    )
    out_specs = (P("grp", "shard", None), P("shard", None))
    return jax.shard_map(
        per_device, mesh=mesh, in_specs=in_specs, out_specs=out_specs, check_vma=False
    )
```

time: 299 us -> 134 us (0.45)
  waiting for transfers between devices: 199 us -> 60.4 us
  Pallas kernels: 0 us -> 42.2 us
  other arithmetic: 35.5 us -> 0 us
  local copies, waits for them, and re-layouts: 33.5 us -> 0.12 us
  starting transfers between devices: 0.08 us -> 29.4 us
  matrix products: 15.9 us -> 0 us
  between operations: 14.9 us -> 1.72 us
    reduce_scatter x1 -> x0, waiting for transfers between devices: 166 us -> none  [per_device(): lax.psum_scatter(local_grads.astype(jnp.float32), 'shard', scatter_dimens...]
    ppermute x0 -> x23, waiting for transfers between devices: none -> 60.4 us  [the longest x16 56.1 us: along(): return lax.ppermute(x, 'shard', pairs)]
    pallas_call x0 -> x20, Pallas kernels: none -> 42.2 us  [call(): pl.pallas_call(kernel, out_shape=outs + [vm((8, 128))], in_specs=in_specs...]
    psum x1 -> x0, waiting for transfers between devices: 32.8 us -> none  [per_device(): combined = lax.psum(own_coeffs, 'grp')]
    ppermute x0 -> x23, starting transfers between devices: none -> 29.4 us  [the longest x16 23.7 us: along(): return lax.ppermute(x, 'shard', pairs)]
    gather x2 -> x0, local copies, waits for them, and re-layouts: 20.7 us -> none  [per_device(): jnp.take_along_axis(coeffs, places, axis=2)]
    convert_element_type x1 -> x0, other arithmetic: 18.6 us -> none  [per_device(): local_grads.astype(jnp.float32)]
    dot_general x6 -> x0, matrix products: 15.9 us -> none  [the longest x4 9.9 us: to_field(): jnp.einsum('km,abkl,ln->ambn', basis, tiles, basis, precision=lax.Precisi...]
  transfers between devices with their start and end apart: 2 -> 23, of which waited for: 2 -> 14; matrix products, arithmetic and copies ran while one was open for 4% -> 0% of each run, Pallas kernels for 0% -> 18%
where the time goes in v2:
time: 134 us
  waiting for transfers between devices  60.4 us (45%)
  Pallas kernels  42.2 us (31%)
  starting transfers between devices  29.4 us (22%)
  between operations  1.72 us (1%)
    ppermute x16, waiting for transfers between devices, along(): return lax.ppermute(x, 'shard', pairs)  56.1 us
    pallas_call x20, Pallas kernels, call(): pl.pallas_call(kernel, out_shape=outs + [vm((8, 128))], in_specs=in_specs...  42.2 us
    ppermute x16, starting transfers between devices, along(): return lax.ppermute(x, 'shard', pairs)  23.7 us
    ppermute x3, starting transfers between devices, swap_grp(): return lax.ppermute(x, 'grp', [(i, i ^ k) for i in range(NX)])  4.7 us
  transfers between devices with their start and end apart: 23, of which 14 were waited for; matrix products, arithmetic and copies ran while one was open for 0% of the time, Pallas kernels for 18%

profile of v2, /device:TPU:0, one launch (start us, length us, event | category | flops | bytes accessed | tf_op | source)
XLA Modules:
  0.0 133.8 jit_solution(7962605936557787152)
XLA Ops:
  0.6 1.4 %conv0.2 = (f32[1,2,4,128,512]{4,3,2,1,0:T(8,128)S(1)}, f32[8,128]{1,0:T(8,128)S(1)}) custom-call(bf16[4,4,2,256,1024]{4,3,2,1,0:T(8,128)(2,1)} %bitcast.7), custom_call_target="tpu_custom_call" | custom-call | flops 1000000 | bytes 4000000 | tf_op jit(solution)/shard_map/conv0/pallas_call | solution.py:161
  2.0 0.1 collective-permute-start
  2.1 1.4 %conv1.1 = (f32[1,2,4,128,512]{4,3,2,1,0:T(8,128)S(1)}, f32[8,128]{1,0:T(8,128)S(1)}) custom-call(bf16[4,4,2,256,1024]{4,3,2,1,0:T(8,128)(2,1)} %bitcast.8, f32[8,128]{1,0:T(8,128)S(1)} %get-tuple-element.59.refs_1_), custom_call_target="tpu_custom_call" | custom-call | flops 1000000 | bytes 4000000 | tf_op jit(solution)/shard_map/conv1/pallas_call | solution.py:161
  3.5 0.5 collective-permute-start.2
  4.1 2.2 %collective-permute-done.refs_2_.refs_1_ = f32[1,2,4,128,512]{4,3,2,1,0:T(8,128)S(1)} collective-permute-done((f32[1,2,4,128,512]{4,3,2,1,0:T(8,128)S(1)}, f32[1,2,4,128,512]{4,3,2,1,0:T(8,128)S(1)}, u32[]{:S(2)}, u32[]{:S(2)}) %collective-permute-start) | collective-permute-done | bytes 2097184 | tf_op jit(solution)/shard_map/ppermute | solution.py:183
  6.3 3.3 %conv0.3 = (f32[2,2,4,128,512]{4,3,2,1,0:T(8,128)}, f32[8,128]{1,0:T(8,128)S(1)}) custom-call(bf16[4,4,2,256,1024]{4,3,2,1,0:T(8,128)(2,1)} %bitcast.9, f32[8,128]{1,0:T(8,128)S(1)} %get-tuple-element.60.refs_1_, f32[1,2,4,128,512]{4,3,2,1,0:T(8,128)S(1)} %collective-permute-done.refs_2_.refs_1_), custom_call_target="tpu_custom_call" | custom-call | flops 1000000 | bytes 4000000 | tf_op jit(solution)/shard_map/conv0/pallas_call | solution.py:161
  9.6 0.2 collective-permute-start.1
  9.8 4.1 %send.2 = (f32[2,4,128,512]{3,2,1,0:T(8,128)}, f32[2,4,128,512]{3,2,1,0:T(8,128)}, f32[8,128]{1,0:T(8,128)S(1)}) custom-call(bf16[4,4,2,256,1024]{4,3,2,1,0:T(8,128)(2,1)} %bitcast.10, f32[1,2,4,128,512]{4,3,2,1,0:T(8,128)S(1)} %collective-permute-done.refs_2_.refs_1_, f32[1,2,4,128,512]{4,3,2,1,0:T(8,128)S(1)} %collective-permute-done.2.refs_2_, ...), custom_call_target="tpu_custom_call" | custom-call | flops 199999995904 | bytes 1000000000 | tf_op jit(solution)/shard_map/send/pallas_call | solution.py:161
  13.9 4.2 %collective-permute-start.3 = (f32[2,4,128,512]{3,2,1,0:T(8,128)}, f32[2,4,128,512]{3,2,1,0:T(8,128)S(1)}, u32[]{:S(2)}, u32[]{:S(2)}) collective-permute-start(f32[2,4,128,512]{3,2,1,0:T(8,128)} %get-tuple-element.68), channel_id=1, source_target_pairs={{0,24},{1,7},{2,26},{3,1},{4,28},{5,3},{6,30},{7,5},{8,0},{9,15},{... | collective-permute-start | bytes 6291464 | tf_op jit(solution)/shard_map/ppermute | solution.py:191
  18.1 0.1 reshape.10.refs_0_.refs_2_
  18.2 0.0 collective-permute-done.1.refs_1_
  18.2 5.3 %send.3 = (f32[2,4,128,512]{3,2,1,0:T(8,128)}, f32[2,4,128,512]{3,2,1,0:T(8,128)}, f32[8,128]{1,0:T(8,128)S(1)}) custom-call(bf16[4,4,2,256,1024]{4,3,2,1,0:T(8,128)(2,1)} %bitcast.11, f32[2,2,4,128,512]{4,3,2,1,0:T(8,128)} %collective-permute-done.1.refs_1_, f32[8,128]{1,0:T(8,128)S(1)} %get-tuple-element.65.refs_2_), custom_call_target="tpu_custom_call" | custom-call | flops 1000000 | bytes 4000000 | tf_op jit(solution)/shard_map/send/pallas_call | solution.py:161
  23.5 0.0 copy-start.5
  23.6 0.0 copy-start.6
  23.6 4.5 %conv2.1 = (f32[2,2,4,256,512]{4,3,2,1,0:T(8,128)}, f32[8,128]{1,0:T(8,128)S(1)}) custom-call(bf16[4,4,2,256,1024]{4,3,2,1,0:T(8,128)(2,1)} %bitcast.12, f32[8,128]{1,0:T(8,128)S(1)} %get-tuple-element.66.refs_1_), custom_call_target="tpu_custom_call" | custom-call | flops 1000000 | bytes 4000000 | tf_op jit(solution)/shard_map/conv2/pallas_call | solution.py:161
  28.0 0.1 collective-permute-start.5
  28.1 3.3 %collective-permute-start.8 = (f32[2,4,128,512]{3,2,1,0:T(8,128)}, f32[2,4,128,512]{3,2,1,0:T(8,128)}, u32[]{:S(2)}, u32[]{:S(2)}) collective-permute-start(f32[2,4,128,512]{3,2,1,0:T(8,128)} %get-tuple-element.78), channel_id=1, source_target_pairs={{0,24},{1,7},{2,26},{3,1},{4,28},{5,3},{6,30},{7,5},{8,0},{9,15},{... | collective-permute-start | bytes 6291464 | tf_op jit(solution)/shard_map/ppermute | solution.py:191
  31.4 0.0 collective-permute-start.9
  31.4 10.5 %collective-permute-done.3.refs_4_.refs_2_ = f32[2,4,128,512]{3,2,1,0:T(8,128)S(1)} collective-permute-done((f32[2,4,128,512]{3,2,1,0:T(8,128)}, f32[2,4,128,512]{3,2,1,0:T(8,128)S(1)}, u32[]{:S(2)}, u32[]{:S(2)}) %collective-permute-start.3) | collective-permute-done | bytes 2097184 | tf_op jit(solution)/shard_map/ppermute | solution.py:191
  42.0 3.7 %collective-permute-done.4.refs_5_.refs_3_ = f32[2,4,128,512]{3,2,1,0:T(8,128)} collective-permute-done((f32[2,4,128,512]{3,2,1,0:T(8,128)}, f32[2,4,128,512]{3,2,1,0:T(8,128)}, u32[]{:S(2)}, u32[]{:S(2)}) %collective-permute-start.4) | collective-permute-done | bytes 2097184 | tf_op jit(solution)/shard_map/ppermute | solution.py:191
  45.7 0.7 own.1
  46.4 0.0 collective-permute-done.5.refs_1_
  46.4 2.5 %pass.2 = (f32[4,128,512]{2,1,0:T(8,128)S(1)}, f32[4,128,512]{2,1,0:T(8,128)S(1)}, f32[8,128]{1,0:T(8,128)S(1)}) custom-call(bf16[4,4,2,256,1024]{4,3,2,1,0:T(8,128)(2,1)} %bitcast.13, f32[2,2,4,256,512]{4,3,2,1,0:T(8,128)} %collective-permute-done.5.refs_1_, f32[2,4,128,512]{3,2,1,0:T(8,128)S(1)} %collective-permute-done.3.refs_4_.refs_2_, ...), custom_call_target="tpu_custom_call" | custom-call | flops 1000000 | bytes 4000000 | tf_op jit(solution)/shard_map/pass/pallas_call | solution.py:161
  49.0 0.1 collective-permute-start.6
  49.0 2.0 %collective-permute-start.7 = (f32[4,128,512]{2,1,0:T(8,128)S(1)}, f32[4,128,512]{2,1,0:T(8,128)S(1)}, u32[]{:S(2)}, u32[]{:S(2)}) collective-permute-start(f32[4,128,512]{2,1,0:T(8,128)S(1)} %get-tuple-element.77), channel_id=1, source_target_pairs={{0,8},{1,3},{2,10},{3,5},{4,12},{5,7},{6,14},{7,1},{8,16},{9,11},{... | collective-permute-start | bytes 3145736 | tf_op jit(solution)/shard_map/ppermute | solution.py:191
  51.1 2.5 %before.2 = (f32[2,4,128,512]{3,2,1,0:T(8,128)S(1)}, f32[8,128]{1,0:T(8,128)S(1)}) custom-call(bf16[4,4,2,256,1024]{4,3,2,1,0:T(8,128)(2,1)} %bitcast.14, f32[2,2,4,256,512]{4,3,2,1,0:T(8,128)} %collective-permute-done.5.refs_1_, f32[2,4,128,512]{3,2,1,0:T(8,128)S(1)} %collective-permute-done.3.refs_4_.refs_2_, ...), custom_call_target="tpu_custom_call" | custom-call | flops 1000000 | bytes 4000000 | tf_op jit(solution)/shard_map/before/pallas_call | solution.py:161
  53.6 10.9 %collective-permute-done.8.refs_2_ = f32[2,4,128,512]{3,2,1,0:T(8,128)} collective-permute-done((f32[2,4,128,512]{3,2,1,0:T(8,128)}, f32[2,4,128,512]{3,2,1,0:T(8,128)}, u32[]{:S(2)}, u32[]{:S(2)}) %collective-permute-start.8) | collective-permute-done | bytes 2097184 | tf_op jit(solution)/shard_map/ppermute | solution.py:191
  64.4 3.7 %collective-permute-done.9.refs_3_ = f32[2,4,128,512]{3,2,1,0:T(8,128)} collective-permute-done((f32[2,4,128,512]{3,2,1,0:T(8,128)}, f32[2,4,128,512]{3,2,1,0:T(8,128)}, u32[]{:S(2)}, u32[]{:S(2)}) %collective-permute-start.9) | collective-permute-done | bytes 2097184 | tf_op jit(solution)/shard_map/ppermute | solution.py:191
  68.1 2.8 %pass.3 = (f32[4,128,512]{2,1,0:T(8,128)S(1)}, f32[4,128,512]{2,1,0:T(8,128)S(1)}, f32[8,128]{1,0:T(8,128)S(1)}) custom-call(bf16[4,4,2,256,1024]{4,3,2,1,0:T(8,128)(2,1)} %bitcast.15, f32[2,2,4,256,512]{4,3,2,1,0:T(8,128)} %collective-permute-done.5.refs_1_, f32[2,4,128,512]{3,2,1,0:T(8,128)} %collective-permute-done.8.refs_2_, ...), custom_call_target="tpu_custom_call" | custom-call | flops 1000000 | bytes 4000000 | tf_op jit(solution)/shard_map/pass/pallas_call | solution.py:161
  70.9 0.1 collective-permute-start.12
  71.0 2.0 %collective-permute-start.13 = (f32[4,128,512]{2,1,0:T(8,128)S(1)}, f32[4,128,512]{2,1,0:T(8,128)S(1)}, u32[]{:S(2)}, u32[]{:S(2)}) collective-permute-start(f32[4,128,512]{2,1,0:T(8,128)S(1)} %get-tuple-element.91), channel_id=1, source_target_pairs={{0,8},{1,3},{2,10},{3,5},{4,12},{5,7},{6,14},{7,1},{8,16},{9,11},{... | collective-permute-start | bytes 3145736 | tf_op jit(solution)/shard_map/ppermute | solution.py:191
  73.0 2.5 %collective-permute-done.6.refs_1_ = f32[4,128,512]{2,1,0:T(8,128)S(1)} collective-permute-done((f32[4,128,512]{2,1,0:T(8,128)S(1)}, f32[4,128,512]{2,1,0:T(8,128)S(1)}, u32[]{:S(2)}, u32[]{:S(2)}) %collective-permute-start.6) | collective-permute-done | bytes 1048608 | tf_op jit(solution)/shard_map/ppermute | solution.py:191
  75.6 3.7 %collective-permute-done.7.refs_2_ = f32[4,128,512]{2,1,0:T(8,128)S(1)} collective-permute-done((f32[4,128,512]{2,1,0:T(8,128)S(1)}, f32[4,128,512]{2,1,0:T(8,128)S(1)}, u32[]{:S(2)}, u32[]{:S(2)}) %collective-permute-start.7) | collective-permute-done | bytes 1048608 | tf_op jit(solution)/shard_map/ppermute | solution.py:191
  79.3 0.2 turn.2
  79.5 3.1 %collective-permute-start.10 = (f32[2,128,512]{2,1,0:T(8,128)S(1)}, f32[2,128,512]{2,1,0:T(8,128)S(1)}, u32[]{:S(2)}, u32[]{:S(2)}) collective-permute-start(f32[2,128,512]{2,1,0:T(8,128)S(1)} %get-tuple-element.86), channel_id=1, source_target_pairs={{0,6},{1,25},{2,0},{3,27},{4,2},{5,29},{6,4},{7,31},{8,14},{9,1},{... | collective-permute-start | bytes 1572872 | tf_op jit(solution)/shard_map/ppermute | solution.py:191
  82.6 2.8 %before.3 = (f32[2,4,128,512]{3,2,1,0:T(8,128)S(1)}, f32[8,128]{1,0:T(8,128)S(1)}) custom-call(bf16[4,4,2,256,1024]{4,3,2,1,0:T(8,128)(2,1)} %bitcast.16, f32[2,2,4,256,512]{4,3,2,1,0:T(8,128)} %collective-permute-done.5.refs_1_, f32[2,4,128,512]{3,2,1,0:T(8,128)} %collective-permute-done.8.refs_2_, f32[2,4,128,512]{3,2,1,0:T(8,128)} %collective-permute-done.9.refs_3_, ...), custom_call_target="tpu_custom_call" | custom-call | flops 1000000 | bytes 4000000 | tf_op jit(solution)/shard_map/before/pallas_call | solution.py:161
  85.4 6.3 %collective-permute-done.12.refs_1_ = f32[4,128,512]{2,1,0:T(8,128)S(1)} collective-permute-done((f32[4,128,512]{2,1,0:T(8,128)S(1)}, f32[4,128,512]{2,1,0:T(8,128)S(1)}, u32[]{:S(2)}, u32[]{:S(2)}) %collective-permute-start.12) | collective-permute-done | bytes 1048608 | tf_op jit(solution)/shard_map/ppermute | solution.py:191
  91.6 4.0 %collective-permute-done.13.refs_2_ = f32[4,128,512]{2,1,0:T(8,128)S(1)} collective-permute-done((f32[4,128,512]{2,1,0:T(8,128)S(1)}, f32[4,128,512]{2,1,0:T(8,128)S(1)}, u32[]{:S(2)}, u32[]{:S(2)}) %collective-permute-start.13) | collective-permute-done | bytes 1048608 | tf_op jit(solution)/shard_map/ppermute | solution.py:191
  95.6 0.3 turn.3
  95.9 0.0 copy-start
  95.9 0.0 copy-start.3
  95.9 0.0 copy-start.4
  95.9 3.6 %collective-permute-start.16 = (f32[2,128,512]{2,1,0:T(8,128)S(1)}, f32[2,128,512]{2,1,0:T(8,128)S(1)}, u32[]{:S(2)}, u32[]{:S(2)}) collective-permute-start(f32[2,128,512]{2,1,0:T(8,128)S(1)} %get-tuple-element.98), channel_id=1, source_target_pairs={{0,6},{1,25},{2,0},{3,27},{4,2},{5,29},{6,4},{7,31},{8,14},{9,1},{... | collective-permute-start | bytes 1572872 | tf_op jit(solution)/shard_map/ppermute | solution.py:191
  99.5 0.0 collective-permute-start.17
  99.5 0.0 collective-permute-done.10.refs_2_.refs_12_
  99.5 0.1 relay.2
  99.6 3.3 %collective-permute-start.14 = (f32[128,512]{1,0:T(8,128)S(1)}, f32[128,512]{1,0:T(8,128)S(1)}, u32[]{:S(2)}, u32[]{:S(2)}) collective-permute-start(f32[128,512]{1,0:T(8,128)S(1)} %get-tuple-element.94), channel_id=1, source_target_pairs={{0,6},{1,25},{2,0},{3,27},{4,2},{5,29},{6,4},{7,31},{8,14},{9,1},{... | collective-permute-start | bytes 786440 | tf_op jit(solution)/shard_map/ppermute | solution.py:191
  102.9 0.0 collective-permute-start.15
  102.9 3.3 %collective-permute-done.16.refs_2_.refs_12_ = f32[2,128,512]{2,1,0:T(8,128)S(1)} collective-permute-done((f32[2,128,512]{2,1,0:T(8,128)S(1)}, f32[2,128,512]{2,1,0:T(8,128)S(1)}, u32[]{:S(2)}, u32[]{:S(2)}) %collective-permute-start.16) | collective-permute-done | bytes 524320 | tf_op jit(solution)/shard_map/ppermute | solution.py:191
  106.2 3.7 %collective-permute-done.17.refs_3_.refs_11_ = f32[2,128,512]{2,1,0:T(8,128)S(1)} collective-permute-done((f32[2,128,512]{2,1,0:T(8,128)S(1)}, f32[2,128,512]{2,1,0:T(8,128)S(1)}, u32[]{:S(2)}, u32[]{:S(2)}) %collective-permute-start.17) | collective-permute-done | bytes 524320 | tf_op jit(solution)/shard_map/ppermute | solution.py:191
  109.9 0.1 relay.3
  110.0 0.1 collective-permute-start.18
  110.1 2.0 %collective-permute-start.19 = (f32[128,512]{1,0:T(8,128)S(1)}, f32[128,512]{1,0:T(8,128)S(1)}, u32[]{:S(2)}, u32[]{:S(2)}) collective-permute-start(f32[128,512]{1,0:T(8,128)S(1)} %get-tuple-element.106), channel_id=1, source_target_pairs={{0,2},{1,9},{2,4},{3,11},{4,6},{5,13},{6,0},{7,15},{8,10},{9,17},{... | collective-permute-start | bytes 786440 | tf_op jit(solution)/shard_map/ppermute | solution.py:191
  112.8 1.1 values.2
  113.9 2.6 %collective-permute-done.18.refs_9_ = f32[128,512]{1,0:T(8,128)S(1)} collective-permute-done((f32[128,512]{1,0:T(8,128)S(1)}, f32[128,512]{1,0:T(8,128)S(1)}, u32[]{:S(2)}, u32[]{:S(2)}) %collective-permute-start.18) | collective-permute-done | bytes 262176 | tf_op jit(solution)/shard_map/ppermute | solution.py:191
  116.4 1.3 collective-permute-done.19.refs_10_
  117.7 1.5 %values.3 = (f32[128,1024]{1,0:T(8,128)S(1)}, f32[32,128]{1,0:T(8,128)S(1)}, f32[8,128]{1,0:T(8,128)}) custom-call(f32[256,1024]{1,0:T(8,128)S(1)} %bitcast.6, s32[1]{0:T(128)S(6)} %copy.12.refs_1_, s32[4,4,128]{2,1,0:T(4,128)S(1)} %reshape.10.refs_0_.refs_2_, bf16[256,256]{1,0:T(8,128)(2,1)S(1)} %copy-done.3, bf16[256,256]{1,0:T(8,128)(2,1)S(1)} %copy-done.4, ...), custom_call_target="tpu_custom_call" | custom-call | flops 1000000 | bytes 4000000 | tf_op jit(solution)/shard_map/values/pallas_call | solution.py:161
  119.2 1.5 %collective-permute-start.20 = (f32[32,128]{1,0:T(8,128)S(1)}, f32[32,128]{1,0:T(8,128)S(1)}, u32[]{:S(2)}, u32[]{:S(2)}) collective-permute-start(f32[32,128]{1,0:T(8,128)S(1)} %get-tuple-element.110.refs_2_.refs_0_), channel_id=1, source_target_pairs={{0,32},{32,0},{64,96},{96,64},{1,33},{33,1},{65,97},{97,65},{2,34}... | collective-permute-start | bytes 49160 | tf_op jit(solution)/shard_map/ppermute | solution.py:195
  120.7 2.7 %collective-permute-start.21 = (f32[32,128]{1,0:T(8,128)S(1)}, f32[32,128]{1,0:T(8,128)S(1)}, u32[]{:S(2)}, u32[]{:S(2)}) collective-permute-start(f32[32,128]{1,0:T(8,128)S(1)} %get-tuple-element.110.refs_2_.refs_0_), channel_id=1, source_target_pairs={{0,64},{32,96},{64,0},{96,32},{1,65},{33,97},{65,1},{97,33},{2,66}... | collective-permute-start | bytes 49160 | tf_op jit(solution)/shard_map/ppermute | solution.py:195
  123.5 0.5 collective-permute-start.22
  123.9 2.4 %keep.1 = (f32[256,1024]{1,0:T(8,128)}, f32[8,128]{1,0:T(8,128)}) custom-call(f32[128,1024]{1,0:T(8,128)S(1)} %get-tuple-element.102.refs_0_, f32[128,1024]{1,0:T(8,128)S(1)} %get-tuple-element.109.refs_1_, f32[32,128]{1,0:T(8,128)S(1)} %get-tuple-element.110.refs_2_.refs_0_, bf16[256,256]{1,0:T(8,128)(2,1)S(1)} %copy-done.1, ...), custom_call_target="tpu_custom_call" | custom-call | flops 1000000 | bytes 4000000 | tf_op jit(solution)/shard_map/keep/pallas_call | solution.py:161
  126.4 2.0 %collective-permute-done.22.refs_3_ = f32[32,128]{1,0:T(8,128)S(1)} collective-permute-done((f32[32,128]{1,0:T(8,128)S(1)}, f32[32,128]{1,0:T(8,128)S(1)}, u32[]{:S(2)}, u32[]{:S(2)}) %collective-permute-start.22) | collective-permute-done | bytes 16416 | tf_op jit(solution)/shard_map/ppermute | solution.py:195
  128.4 2.2 %tables.1 = (bf16[4,4,512,256]{3,2,1,0:T(8,128)(2,1)S(1)}, f32[4,4,64,512]{3,2,1,0:T(8,128)S(1)}, f32[8,128]{1,0:T(8,128)}) custom-call(f32[32,128]{1,0:T(8,128)S(1)} %get-tuple-element.110.refs_2_.refs_0_, f32[32,128]{1,0:T(8,128)S(1)} %collective-permute-done.20.refs_1_, f32[32,128]{1,0:T(8,128)S(1)} %collective-permute-done.21.refs_2_, ...), custom_call_target="tpu_custom_call" | custom-call | flops 1000000 | bytes 4000000 | tf_op jit(solution)/shard_map/tables/pallas_call | solution.py:161
  130.6 3.0 %update.1 = (f32[256,1024]{1,0:T(8,128)}, f32[8,128]{1,0:T(8,128)}) custom-call(f32[32,128]{1,0:T(8,128)S(1)} %get-tuple-element.110.refs_2_.refs_0_, f32[32,128]{1,0:T(8,128)S(1)} %collective-permute-done.20.refs_1_, f32[32,128]{1,0:T(8,128)S(1)} %collective-permute-done.21.refs_2_, f32[32,128]{1,0:T(8,128)S(1)} %collective-permute-done.22.refs_3_, ...), custom_call_target="tpu_custom_call" | custom-call | flops 1000000 | bytes 4000000 | tf_op jit(solution)/shard_map/update/pallas_call | solution.py:161
  (19 shorter events, 0.0 us)
Async XLA Ops:
  2.0 4.2 %collective-permute-start = (f32[1,2,4,128,512]{4,3,2,1,0:T(8,128)S(1)}, f32[1,2,4,128,512]{4,3,2,1,0:T(8,128)S(1)}, u32[]{:S(2)}, u32[]{:S(2)}) collective-permute-start(f32[1,2,4,128,512]{4,3,2,1,0:T(8,128)S(1)} %get-tuple-element.61), channel_id=1, source_target_pairs={{0,1},{1,0},{2,3},{3,2},{4,5},{5,4},{6,7},{7,6},{8,9},{9,8},{10,11... | collective-permute-start | bytes 6291464 | tf_op jit(solution)/shard_map/ppermute | solution.py:183
  3.5 6.3 %collective-permute-start.2 = (f32[1,2,4,128,512]{4,3,2,1,0:T(8,128)S(1)}, f32[1,2,4,128,512]{4,3,2,1,0:T(8,128)S(1)}, u32[]{:S(2)}, u32[]{:S(2)}) collective-permute-start(f32[1,2,4,128,512]{4,3,2,1,0:T(8,128)S(1)} %get-tuple-element.63), channel_id=1, source_target_pairs={{0,1},{1,0},{2,3},{3,2},{4,5},{5,4},{6,7},{7,6},{8,9},{9,8},{10,11... | collective-permute-start | bytes 6291464 | tf_op jit(solution)/shard_map/ppermute | solution.py:183
  9.6 8.6 %collective-permute-start.1 = (f32[2,2,4,128,512]{4,3,2,1,0:T(8,128)}, f32[2,2,4,128,512]{4,3,2,1,0:T(8,128)}, u32[]{:S(2)}, u32[]{:S(2)}) collective-permute-start(f32[2,2,4,128,512]{4,3,2,1,0:T(8,128)} %get-tuple-element.62), channel_id=1, source_target_pairs={{0,1},{1,0},{2,3},{3,2},{4,5},{5,4},{6,7},{7,6},{8,9},{9,8},{10,11... | collective-permute-start | bytes 12582920 | tf_op jit(solution)/shard_map/ppermute | solution.py:183
  9.8 8.3 %copy-start.7 = (s32[1,4,16,32]{3,2,1,0:T(8,128)S(1)}, s32[1,4,16,32]{3,2,1,0:T(8,128)}, u32[]{:S(2)}) copy-start(s32[1,4,16,32]{3,2,1,0:T(8,128)} %param.12) | copy-start | bytes 24580
  13.9 28.1 %collective-permute-start.3 = (f32[2,4,128,512]{3,2,1,0:T(8,128)}, f32[2,4,128,512]{3,2,1,0:T(8,128)S(1)}, u32[]{:S(2)}, u32[]{:S(2)}) collective-permute-start(f32[2,4,128,512]{3,2,1,0:T(8,128)} %get-tuple-element.68), channel_id=1, source_target_pairs={{0,24},{1,7},{2,26},{3,1},{4,28},{5,3},{6,30},{7,5},{8,0},{9,15},{... | collective-permute-start | bytes 6291464 | tf_op jit(solution)/shard_map/ppermute | solution.py:191
  18.1 27.6 %collective-permute-start.4 = (f32[2,4,128,512]{3,2,1,0:T(8,128)}, f32[2,4,128,512]{3,2,1,0:T(8,128)}, u32[]{:S(2)}, u32[]{:S(2)}) collective-permute-start(f32[2,4,128,512]{3,2,1,0:T(8,128)} %get-tuple-element.69), channel_id=1, source_target_pairs={{0,8},{1,3},{2,10},{3,5},{4,12},{5,7},{6,14},{7,1},{8,16},{9,11},{... | collective-permute-start | bytes 6291464 | tf_op jit(solution)/shard_map/ppermute | solution.py:191
  23.5 22.1 %copy-start.5 = (bf16[64,64]{1,0:T(8,128)(2,1)S(1)}, bf16[64,64]{1,0:T(8,128)(2,1)}, u32[]{:S(2)}) copy-start(bf16[64,64]{1,0:T(8,128)(2,1)} %constant.16.clone.refs_1_.refs_4_) | copy-start | bytes 24580
  23.6 22.1 %copy-start.6 = (bf16[64,64]{1,0:T(8,128)(2,1)S(1)}, bf16[64,64]{1,0:T(8,128)(2,1)}, u32[]{:S(2)}) copy-start(bf16[64,64]{1,0:T(8,128)(2,1)} %constant.17.clone.refs_2_.refs_5_) | copy-start | bytes 24580
  28.0 18.4 %collective-permute-start.5 = (f32[2,2,4,256,512]{4,3,2,1,0:T(8,128)}, f32[2,2,4,256,512]{4,3,2,1,0:T(8,128)}, u32[]{:S(2)}, u32[]{:S(2)}) collective-permute-start(f32[2,2,4,256,512]{4,3,2,1,0:T(8,128)} %get-tuple-element.72), channel_id=1, source_target_pairs={{0,1},{1,0},{2,3},{3,2},{4,5},{5,4},{6,7},{7,6},{8,9},{9,8},{10,11... | collective-permute-start | bytes 25165832 | tf_op jit(solution)/shard_map/ppermute | solution.py:183
  28.1 36.3 %collective-permute-start.8 = (f32[2,4,128,512]{3,2,1,0:T(8,128)}, f32[2,4,128,512]{3,2,1,0:T(8,128)}, u32[]{:S(2)}, u32[]{:S(2)}) collective-permute-start(f32[2,4,128,512]{3,2,1,0:T(8,128)} %get-tuple-element.78), channel_id=1, source_target_pairs={{0,24},{1,7},{2,26},{3,1},{4,28},{5,3},{6,30},{7,5},{8,0},{9,15},{... | collective-permute-start | bytes 6291464 | tf_op jit(solution)/shard_map/ppermute | solution.py:191
  31.4 36.7 %collective-permute-start.9 = (f32[2,4,128,512]{3,2,1,0:T(8,128)}, f32[2,4,128,512]{3,2,1,0:T(8,128)}, u32[]{:S(2)}, u32[]{:S(2)}) collective-permute-start(f32[2,4,128,512]{3,2,1,0:T(8,128)} %get-tuple-element.79), channel_id=1, source_target_pairs={{0,8},{1,3},{2,10},{3,5},{4,12},{5,7},{6,14},{7,1},{8,16},{9,11},{... | collective-permute-start | bytes 6291464 | tf_op jit(solution)/shard_map/ppermute | solution.py:191
  49.0 26.6 %collective-permute-start.6 = (f32[4,128,512]{2,1,0:T(8,128)S(1)}, f32[4,128,512]{2,1,0:T(8,128)S(1)}, u32[]{:S(2)}, u32[]{:S(2)}) collective-permute-start(f32[4,128,512]{2,1,0:T(8,128)S(1)} %get-tuple-element.76), channel_id=1, source_target_pairs={{0,24},{1,7},{2,26},{3,1},{4,28},{5,3},{6,30},{7,5},{8,0},{9,15},{... | collective-permute-start | bytes 3145736 | tf_op jit(solution)/shard_map/ppermute | solution.py:191
  49.0 30.2 %collective-permute-start.7 = (f32[4,128,512]{2,1,0:T(8,128)S(1)}, f32[4,128,512]{2,1,0:T(8,128)S(1)}, u32[]{:S(2)}, u32[]{:S(2)}) collective-permute-start(f32[4,128,512]{2,1,0:T(8,128)S(1)} %get-tuple-element.77), channel_id=1, source_target_pairs={{0,8},{1,3},{2,10},{3,5},{4,12},{5,7},{6,14},{7,1},{8,16},{9,11},{... | collective-permute-start | bytes 3145736 | tf_op jit(solution)/shard_map/ppermute | solution.py:191
  70.9 20.7 %collective-permute-start.12 = (f32[4,128,512]{2,1,0:T(8,128)S(1)}, f32[4,128,512]{2,1,0:T(8,128)S(1)}, u32[]{:S(2)}, u32[]{:S(2)}) collective-permute-start(f32[4,128,512]{2,1,0:T(8,128)S(1)} %get-tuple-element.90), channel_id=1, source_target_pairs={{0,24},{1,7},{2,26},{3,1},{4,28},{5,3},{6,30},{7,5},{8,0},{9,15},{... | collective-permute-start | bytes 3145736 | tf_op jit(solution)/shard_map/ppermute | solution.py:191
  71.0 24.6 %collective-permute-start.13 = (f32[4,128,512]{2,1,0:T(8,128)S(1)}, f32[4,128,512]{2,1,0:T(8,128)S(1)}, u32[]{:S(2)}, u32[]{:S(2)}) collective-permute-start(f32[4,128,512]{2,1,0:T(8,128)S(1)} %get-tuple-element.91), channel_id=1, source_target_pairs={{0,8},{1,3},{2,10},{3,5},{4,12},{5,7},{6,14},{7,1},{8,16},{9,11},{... | collective-permute-start | bytes 3145736 | tf_op jit(solution)/shard_map/ppermute | solution.py:191
  79.5 20.1 %collective-permute-start.10 = (f32[2,128,512]{2,1,0:T(8,128)S(1)}, f32[2,128,512]{2,1,0:T(8,128)S(1)}, u32[]{:S(2)}, u32[]{:S(2)}) collective-permute-start(f32[2,128,512]{2,1,0:T(8,128)S(1)} %get-tuple-element.86), channel_id=1, source_target_pairs={{0,6},{1,25},{2,0},{3,27},{4,2},{5,29},{6,4},{7,31},{8,14},{9,1},{... | collective-permute-start | bytes 1572872 | tf_op jit(solution)/shard_map/ppermute | solution.py:191
  82.6 17.0 %collective-permute-start.11 = (f32[2,128,512]{2,1,0:T(8,128)S(1)}, f32[2,128,512]{2,1,0:T(8,128)S(1)}, u32[]{:S(2)}, u32[]{:S(2)}) collective-permute-start(f32[2,128,512]{2,1,0:T(8,128)S(1)} %get-tuple-element.87), channel_id=1, source_target_pairs={{0,2},{1,9},{2,4},{3,11},{4,6},{5,13},{6,0},{7,15},{8,10},{9,17},{... | collective-permute-start | bytes 1572872 | tf_op jit(solution)/shard_map/ppermute | solution.py:191
  95.9 16.9 %copy-start = (f32[1,256,1024]{2,1,0:T(8,128)S(1)}, f32[1,256,1024]{2,1,0:T(8,128)}, u32[]{:S(2)}) copy-start(f32[1,256,1024]{2,1,0:T(8,128)} %param.11) | copy-start | bytes 3145732
  95.9 16.9 %copy-start.3 = (bf16[256,256]{1,0:T(8,128)(2,1)S(1)}, bf16[256,256]{1,0:T(8,128)(2,1)}, u32[]{:S(2)}) copy-start(bf16[256,256]{1,0:T(8,128)(2,1)} %constant.12.clone.refs_3_) | copy-start | bytes 393220
  95.9 16.9 %copy-start.4 = (bf16[256,256]{1,0:T(8,128)(2,1)S(1)}, bf16[256,256]{1,0:T(8,128)(2,1)}, u32[]{:S(2)}) copy-start(bf16[256,256]{1,0:T(8,128)(2,1)} %constant.13.clone.refs_4_) | copy-start | bytes 393220
  95.9 10.3 %collective-permute-start.16 = (f32[2,128,512]{2,1,0:T(8,128)S(1)}, f32[2,128,512]{2,1,0:T(8,128)S(1)}, u32[]{:S(2)}, u32[]{:S(2)}) collective-permute-start(f32[2,128,512]{2,1,0:T(8,128)S(1)} %get-tuple-element.98), channel_id=1, source_target_pairs={{0,6},{1,25},{2,0},{3,27},{4,2},{5,29},{6,4},{7,31},{8,14},{9,1},{... | collective-permute-start | bytes 1572872 | tf_op jit(solution)/shard_map/ppermute | solution.py:191
  99.5 10.4 %collective-permute-start.17 = (f32[2,128,512]{2,1,0:T(8,128)S(1)}, f32[2,128,512]{2,1,0:T(8,128)S(1)}, u32[]{:S(2)}, u32[]{:S(2)}) collective-permute-start(f32[2,128,512]{2,1,0:T(8,128)S(1)} %get-tuple-element.99), channel_id=1, source_target_pairs={{0,2},{1,9},{2,4},{3,11},{4,6},{5,13},{6,0},{7,15},{8,10},{9,17},{... | collective-permute-start | bytes 1572872 | tf_op jit(solution)/shard_map/ppermute | solution.py:191
  99.6 13.1 %collective-permute-start.14 = (f32[128,512]{1,0:T(8,128)S(1)}, f32[128,512]{1,0:T(8,128)S(1)}, u32[]{:S(2)}, u32[]{:S(2)}) collective-permute-start(f32[128,512]{1,0:T(8,128)S(1)} %get-tuple-element.94), channel_id=1, source_target_pairs={{0,6},{1,25},{2,0},{3,27},{4,2},{5,29},{6,4},{7,31},{8,14},{9,1},{... | collective-permute-start | bytes 786440 | tf_op jit(solution)/shard_map/ppermute | solution.py:191
  102.9 9.8 %collective-permute-start.15 = (f32[128,512]{1,0:T(8,128)S(1)}, f32[128,512]{1,0:T(8,128)S(1)}, u32[]{:S(2)}, u32[]{:S(2)}) collective-permute-start(f32[128,512]{1,0:T(8,128)S(1)} %get-tuple-element.95), channel_id=1, source_target_pairs={{0,2},{1,9},{2,4},{3,11},{4,6},{5,13},{6,0},{7,15},{8,10},{9,17},{... | collective-permute-start | bytes 786440 | tf_op jit(solution)/shard_map/ppermute | solution.py:191
  110.0 6.4 %collective-permute-start.18 = (f32[128,512]{1,0:T(8,128)S(1)}, f32[128,512]{1,0:T(8,128)S(1)}, u32[]{:S(2)}, u32[]{:S(2)}) collective-permute-start(f32[128,512]{1,0:T(8,128)S(1)} %get-tuple-element.105), channel_id=1, source_target_pairs={{0,6},{1,25},{2,0},{3,27},{4,2},{5,29},{6,4},{7,31},{8,14},{9,1},{... | collective-permute-start | bytes 786440 | tf_op jit(solution)/shard_map/ppermute | solution.py:191
  110.1 7.7 %collective-permute-start.19 = (f32[128,512]{1,0:T(8,128)S(1)}, f32[128,512]{1,0:T(8,128)S(1)}, u32[]{:S(2)}, u32[]{:S(2)}) collective-permute-start(f32[128,512]{1,0:T(8,128)S(1)} %get-tuple-element.106), channel_id=1, source_target_pairs={{0,2},{1,9},{2,4},{3,11},{4,6},{5,13},{6,0},{7,15},{8,10},{9,17},{... | collective-permute-start | bytes 786440 | tf_op jit(solution)/shard_map/ppermute | solution.py:191
  117.7 6.2 %copy-start.1 = (bf16[256,256]{1,0:T(8,128)(2,1)S(1)}, bf16[256,256]{1,0:T(8,128)(2,1)}, u32[]{:S(2)}) copy-start(bf16[256,256]{1,0:T(8,128)(2,1)} %constant.14.clone.refs_3_.refs_4_) | copy-start | bytes 393220
  117.7 6.2 %copy-start.2 = (bf16[256,256]{1,0:T(8,128)(2,1)S(1)}, bf16[256,256]{1,0:T(8,128)(2,1)}, u32[]{:S(2)}) copy-start(bf16[256,256]{1,0:T(8,128)(2,1)} %constant.15.clone.refs_4_.refs_5_) | copy-start | bytes 393220
  119.2 7.1 %collective-permute-start.20 = (f32[32,128]{1,0:T(8,128)S(1)}, f32[32,128]{1,0:T(8,128)S(1)}, u32[]{:S(2)}, u32[]{:S(2)}) collective-permute-start(f32[32,128]{1,0:T(8,128)S(1)} %get-tuple-element.110.refs_2_.refs_0_), channel_id=1, source_target_pairs={{0,32},{32,0},{64,96},{96,64},{1,33},{33,1},{65,97},{97,65},{2,34}... | collective-permute-start | bytes 49160 | tf_op jit(solution)/shard_map/ppermute | solution.py:195
  120.7 5.6 %collective-permute-start.21 = (f32[32,128]{1,0:T(8,128)S(1)}, f32[32,128]{1,0:T(8,128)S(1)}, u32[]{:S(2)}, u32[]{:S(2)}) collective-permute-start(f32[32,128]{1,0:T(8,128)S(1)} %get-tuple-element.110.refs_2_.refs_0_), channel_id=1, source_target_pairs={{0,64},{32,96},{64,0},{96,32},{1,65},{33,97},{65,1},{97,33},{2,66}... | collective-permute-start | bytes 49160 | tf_op jit(solution)/shard_map/ppermute | solution.py:195
  123.5 4.9 %collective-permute-start.22 = (f32[32,128]{1,0:T(8,128)S(1)}, f32[32,128]{1,0:T(8,128)S(1)}, u32[]{:S(2)}, u32[]{:S(2)}) collective-permute-start(f32[32,128]{1,0:T(8,128)S(1)} %get-tuple-element.110.refs_2_.refs_0_), channel_id=1, source_target_pairs={{0,96},{32,64},{64,32},{96,0},{1,97},{33,65},{65,33},{97,1},{2,98}... | collective-permute-start | bytes 49160 | tf_op jit(solution)/shard_map/ppermute | solution.py:195

commit v3 on v2

--- a/solution.py
+++ b/solution.py
@@ -100,16 +100,21 @@
 
 
 def send_kernel(at, r0, rows, g_ref, *refs):
-    (*others, minus, plus), staging = refs[:-4], refs[-4:]
+    (*others, minus, plus), staging, (made, made_sems) = refs[:-6], refs[-6:-2], refs[-2:]
     near = len(others) == 2
     terms = [
         Terms(i, r0, rows, g_ref, others[i % len(others)], at[i], None, [ref.at[i] for ref in staging], near)
         for i in range(2)
     ]
+    copies = []
     for i, to in enumerate(((minus, plus), (plus, minus))):
         for h in range(2):
             for s in range(4):
-                to[h][i, s] = terms[i].get(h, s)
+                made[i, h, s] = terms[i].get(h, s)
+                copies.append(pltpu.make_async_copy(made.at[i, h, s], to[h].at[i, s], made_sems.at[i, h, s]))
+                copies[-1].start()
+    for cp in copies:
+        cp.wait()
 
 
 def pass_kernel(at, r0, rows, g_ref, r_ref, minus, plus, *refs):
@@ -228,9 +233,11 @@
         return [along(out[0], -1, second), along(out[1], 1, second)]
 
     def send(self, after=(), **kwargs):
-        outs = [vm((2, 4, self.rows, HW))] * 2
+        outs = [jax.ShapeDtypeStruct((2, 4, self.rows, HW), F32)] * 2
         (ra, ia), (rb, ib) = self.got[0], self.got[1]
-        scratch = self.staging(2) + [pltpu.VMEM((2, 8, 128), F32), pltpu.SemaphoreType.DMA((2, 3, 2, 4))]
+        scratch = self.staging(2)
+        scratch += [pltpu.VMEM((2, 8, 128), F32), pltpu.SemaphoreType.DMA((2, 3, 2, 4))]
+        scratch += [scratch[1], pltpu.SemaphoreType.DMA((2, 2, 4))]
         args, kind = ([ra], "a") if ra is rb else ([ra, rb], "v")
         *out, done = self.kernel(send_kernel, (ia, ib), outs, args, "send", scratch, after, kind, **kwargs)
         self.first = self.both(out, False)
@@ -317,7 +324,7 @@
     n = NA * NT
     for i, ref in enumerate((x0, x1, x2, x3)):
         place = pl.ds(pl.multiple_of((me ^ i) * 128, 128), 128)
-        p = ref[n:, :].astype(jnp.int32)
+        p = ref[...]
         block = lax.broadcasted_iota(jnp.int32, (n, 128), 1) // TOPK * SPAN
         cols = jnp.concatenate([p % SPAN + block] * (128 // n), axis=0).astype(F32).T.astype(jnp.int32)
         for k in range(n):
@@ -328,13 +335,18 @@
             l_ref[k // NT, k % NT, :, place] = dot(qh_ref[...], at) + dot(ql_ref[...], at)
 
 
-def values_kernel(r0, rows, m_ref, count_ref, p_ref, dh_ref, dl_ref, bt_ref, l_ref, *refs):
+def copy_kernel(x_ref, o_ref):
+    for a in range(NA):
+        o_ref[NT * a : NT * (a + 1), :] = x_ref[a]
+
+
+def values_kernel(r0, rows, m_ref, count_ref, dh_ref, dl_ref, bt_ref, l_ref, *refs):
     own, relay, direct, (*before, up_ref, v_ref) = refs[0:2], refs[2:4], refs[4:6], refs[6:]
     for h in range(2):
         got = own[h][...] + relay[h][...] + direct[h][1]
         up_ref[:, pl.ds(h * HW, HW)] = DECAY * m_ref[pl.ds(r0, rows), pl.ds(h * HW, HW)] + got
     live = lax.broadcasted_iota(jnp.int32, (1, 128), 1) % TOPK < count_ref[0]
-    a0, n = r0 // SPAN, v_ref.shape[0]
+    a0 = r0 // SPAN
     if before:
         v_ref[: NT * a0, :] = before[0][...]
     for t in range(NT):
@@ -345,9 +357,6 @@
             v = jnp.sum((got[:SPAN] + got[SPAN:]) * l_ref[a0 + i, t], axis=0, keepdims=True)
             row = NT * (a0 + i) + t
             v_ref[row : row + 1, :] = jnp.where(live, v, 0.0)
-    if n == 2 * NT * NA:
-        for a in range(NA):
-            v_ref[NT * (NA + a) : NT * (NA + a + 1), :] = p_ref[a].astype(F32)
 
 
 def row_fields(a, v_ref, l_ref, b_ref, eh_ref, el_ref):
@@ -377,7 +386,7 @@
 def update_kernel(v0, v1, v2, v3, eh_ref, el_ref, b_ref, l_ref, out_ref, buf, vals, sems):
     me = position()[0]
     for i, ref in enumerate((v0, v1, v2, v3)):
-        vals[:, pl.ds(pl.multiple_of((me ^ i) * 128, 128), 128)] = ref[: NT * NA, :] * (1.0 / NX)
+        vals[:, pl.ds(pl.multiple_of((me ^ i) * 128, 128), 128)] = ref[...] * (1.0 / NX)
     copies = []
     for a in range(NA):
         rows = pl.ds(a * SPAN, SPAN)
@@ -412,6 +421,14 @@
     got, n = other_core(g, (2, 3), 0, ROWS, [n])
     got_a.update(got)
     got_b.update(got)
+    spread, n = call(copy_kernel, vm((NT * NA, 128), jnp.int32), [(places, "v")], "places", after=[n])
+    *tables, n = call(
+        tables_kernel,
+        [vm((NA, NT, NX * 128, TILE), BF16), vm((NA, NT, SPAN, NX * 128))],
+        [(x, "v") for x in from_groups(spread) + [qh, ql]],
+        "tables",
+        after=[n],
+    )
     bt, b, l, n = call(
         own_kernel,
         [vm((NA, NT, TILE, 128), BF16), vm((NA, NT, 128, TILE), BF16), vm((NA, NT, SPAN, 128))],
@@ -430,11 +447,11 @@
     n = last.on2([n])
     ups, vs = [], []
     for part in parts:
-        n_rows = NT * (part.r0 + part.rows) // SPAN * (2 if part is last else 1)
+        n_rows = NT * (part.r0 + part.rows) // SPAN
         up, v, n = call(
             functools.partial(values_kernel, part.r0, part.rows),
             [vm((part.rows, COLS)), vm((n_rows, 128))],
-            [(momentum[0], "v"), (counts, "s"), (places, "v"), (dh, "v"), (dl, "v"), (bt, "v"), (l, "v")]
+            [(momentum[0], "v"), (counts, "s"), (dh, "v"), (dl, "v"), (bt, "v"), (l, "v")]
             + [(x, "v") for x in part.terms() + vs],
             "values",
             after=[n],
@@ -444,12 +461,6 @@
     scratch = [pltpu.VMEM((ROWS, COLS), F32), pltpu.SemaphoreType.DMA((NA,))]
     vs = from_groups(v)
     kept, _ = call(keep_kernel, whole, [(x, "v") for x in (*ups, v, eh, el, b, l)], "keep", scratch)
-    *tables, _ = call(
-        tables_kernel,
-        [vm((NA, NT, NX * 128, TILE), BF16), vm((NA, NT, SPAN, NX * 128))],
-        [(x, "v") for x in vs + [qh, ql]],
-        "tables",
-    )
     update, _ = call(
         update_kernel,
         whole,

time: 134 us -> 131 us (0.978)
  waiting for transfers between devices: 60.4 us -> 51.4 us
  starting transfers between devices: 29.4 us -> 36.5 us
    ppermute x16, waiting for transfers between devices: 56.1 us -> 45.3 us  [along(): return lax.ppermute(x, 'shard', pairs)]
    ppermute x3 -> x6, starting transfers between devices: 4.7 us -> 9.48 us  [swap_grp(): return lax.ppermute(x, 'grp', [(i, i ^ k) for i in range(NX)])]
    ppermute x16, starting transfers between devices: 23.7 us -> 26.2 us  [along(): return lax.ppermute(x, 'shard', pairs)]
    ppermute x3 -> x6, waiting for transfers between devices: 2.04 us -> 3.91 us  [swap_grp(): return lax.ppermute(x, 'grp', [(i, i ^ k) for i in range(NX)])]
    pallas_call x20 -> x21, Pallas kernels: 42.2 us -> 41.1 us  [call(): pl.pallas_call(kernel, out_shape=outs + [vm((8, 128))], in_specs=in_specs...]
  transfers between devices with their start and end apart: 23 -> 26, of which waited for: 14 -> 14; matrix products, arithmetic and copies ran while one was open for 0% -> 0% of each run, Pallas kernels for 18% -> 20%
where the time goes in v3:
time: 131 us
  waiting for transfers between devices  51.4 us (39%)
  Pallas kernels  41.1 us (31%)
  starting transfers between devices  36.5 us (28%)
  between operations  1.73 us (1%)
    ppermute x16, waiting for transfers between devices, along(): return lax.ppermute(x, 'shard', pairs)  45.3 us
    pallas_call x21, Pallas kernels, call(): pl.pallas_call(kernel, out_shape=outs + [vm((8, 128))], in_specs=in_specs...  41.1 us
    ppermute x16, starting transfers between devices, along(): return lax.ppermute(x, 'shard', pairs)  26.2 us
    ppermute x6, starting transfers between devices, swap_grp(): return lax.ppermute(x, 'grp', [(i, i ^ k) for i in range(NX)])  9.48 us
    ppermute x6, waiting for transfers between devices, swap_grp(): return lax.ppermute(x, 'grp', [(i, i ^ k) for i in range(NX)])  3.91 us
  transfers between devices with their start and end apart: 26, of which 14 were waited for; matrix products, arithmetic and copies ran while one was open for 0% of the time, Pallas kernels for 20%

profile of v3, /device:TPU:0, one launch (start us, length us, event | category | flops | bytes accessed | tf_op | source)
XLA Modules:
  0.0 130.9 jit_solution(16873273919509371849)
XLA Ops:
  0.6 1.4 %conv0.2 = (f32[1,2,4,128,512]{4,3,2,1,0:T(8,128)S(1)}, f32[8,128]{1,0:T(8,128)S(1)}) custom-call(bf16[4,4,2,256,1024]{4,3,2,1,0:T(8,128)(2,1)} %bitcast.7), custom_call_target="tpu_custom_call" | custom-call | flops 1000000 | bytes 4000000 | tf_op jit(solution)/shard_map/conv0/pallas_call | solution.py:166
  2.0 0.1 collective-permute-start
  2.1 1.4 %conv1.1 = (f32[1,2,4,128,512]{4,3,2,1,0:T(8,128)S(1)}, f32[8,128]{1,0:T(8,128)S(1)}) custom-call(bf16[4,4,2,256,1024]{4,3,2,1,0:T(8,128)(2,1)} %bitcast.8, f32[8,128]{1,0:T(8,128)S(1)} %get-tuple-element.62.refs_1_), custom_call_target="tpu_custom_call" | custom-call | flops 1000000 | bytes 4000000 | tf_op jit(solution)/shard_map/conv1/pallas_call | solution.py:166
  3.5 0.5 collective-permute-start.2
  4.1 2.2 %collective-permute-done.refs_2_.refs_1_ = f32[1,2,4,128,512]{4,3,2,1,0:T(8,128)S(1)} collective-permute-done((f32[1,2,4,128,512]{4,3,2,1,0:T(8,128)S(1)}, f32[1,2,4,128,512]{4,3,2,1,0:T(8,128)S(1)}, u32[]{:S(2)}, u32[]{:S(2)}) %collective-permute-start) | collective-permute-done | bytes 2097184 | tf_op jit(solution)/shard_map/ppermute | solution.py:188
  6.3 3.3 %conv0.3 = (f32[2,2,4,128,512]{4,3,2,1,0:T(8,128)}, f32[8,128]{1,0:T(8,128)S(1)}) custom-call(bf16[4,4,2,256,1024]{4,3,2,1,0:T(8,128)(2,1)} %bitcast.9, f32[8,128]{1,0:T(8,128)S(1)} %get-tuple-element.63.refs_1_, f32[1,2,4,128,512]{4,3,2,1,0:T(8,128)S(1)} %collective-permute-done.refs_2_.refs_1_), custom_call_target="tpu_custom_call" | custom-call | flops 1000000 | bytes 4000000 | tf_op jit(solution)/shard_map/conv0/pallas_call | solution.py:166
  9.6 0.2 collective-permute-start.1
  9.8 3.6 %send.2 = (f32[2,4,128,512]{3,2,1,0:T(8,128)}, f32[2,4,128,512]{3,2,1,0:T(8,128)}, f32[8,128]{1,0:T(8,128)S(1)}) custom-call(bf16[4,4,2,256,1024]{4,3,2,1,0:T(8,128)(2,1)} %bitcast.10, f32[1,2,4,128,512]{4,3,2,1,0:T(8,128)S(1)} %collective-permute-done.refs_2_.refs_1_, f32[1,2,4,128,512]{4,3,2,1,0:T(8,128)S(1)} %collective-permute-done.2.refs_2_, ...), custom_call_target="tpu_custom_call" | custom-call | flops 199999995904 | bytes 1000000000 | tf_op jit(solution)/shard_map/send/pallas_call | solution.py:166
  13.4 4.2 %collective-permute-start.6 = (f32[2,4,128,512]{3,2,1,0:T(8,128)}, f32[2,4,128,512]{3,2,1,0:T(8,128)S(1)}, u32[]{:S(2)}, u32[]{:S(2)}) collective-permute-start(f32[2,4,128,512]{3,2,1,0:T(8,128)} %get-tuple-element.74), channel_id=1, source_target_pairs={{0,24},{1,7},{2,26},{3,1},{4,28},{5,3},{6,30},{7,5},{8,0},{9,15},{... | collective-permute-start | bytes 6291464 | tf_op jit(solution)/shard_map/ppermute | solution.py:196
  17.6 0.0 collective-permute-start.7
  17.6 0.1 reshape.10.refs_0_
  17.6 0.0 collective-permute-done.1.refs_1_
  17.6 5.2 %send.3 = (f32[2,4,128,512]{3,2,1,0:T(8,128)}, f32[2,4,128,512]{3,2,1,0:T(8,128)}, f32[8,128]{1,0:T(8,128)S(1)}) custom-call(bf16[4,4,2,256,1024]{4,3,2,1,0:T(8,128)(2,1)} %bitcast.11, f32[2,2,4,128,512]{4,3,2,1,0:T(8,128)} %collective-permute-done.1.refs_1_, f32[8,128]{1,0:T(8,128)S(1)} %get-tuple-element.68.refs_2_), custom_call_target="tpu_custom_call" | custom-call | flops 1000000 | bytes 4000000 | tf_op jit(solution)/shard_map/send/pallas_call | solution.py:166
  22.9 0.0 copy-start.5
  22.9 0.0 copy-start.6
  22.9 4.5 %conv2.1 = (f32[2,2,4,256,512]{4,3,2,1,0:T(8,128)}, f32[8,128]{1,0:T(8,128)S(1)}) custom-call(bf16[4,4,2,256,1024]{4,3,2,1,0:T(8,128)(2,1)} %bitcast.12, f32[8,128]{1,0:T(8,128)S(1)} %get-tuple-element.69.refs_1_), custom_call_target="tpu_custom_call" | custom-call | flops 1000000 | bytes 4000000 | tf_op jit(solution)/shard_map/conv2/pallas_call | solution.py:166
  27.4 1.6 %collective-permute-start.3 = (s32[16,128]{1,0:T(8,128)S(1)}, s32[16,128]{1,0:T(8,128)S(1)}, u32[]{:S(2)}, u32[]{:S(2)}) collective-permute-start(s32[16,128]{1,0:T(8,128)S(1)} %get-tuple-element.71.refs_0_), channel_id=1, source_target_pairs={{0,32},{32,0},{64,96},{96,64},{1,33},{33,1},{65,97},{97,65},{2,34}... | collective-permute-start | bytes 24584 | tf_op jit(solution)/shard_map/ppermute | solution.py:200
  29.0 2.7 %collective-permute-start.4 = (s32[16,128]{1,0:T(8,128)S(1)}, s32[16,128]{1,0:T(8,128)S(1)}, u32[]{:S(2)}, u32[]{:S(2)}) collective-permute-start(s32[16,128]{1,0:T(8,128)S(1)} %get-tuple-element.71.refs_0_), channel_id=1, source_target_pairs={{0,64},{32,96},{64,0},{96,32},{1,65},{33,97},{65,1},{97,33},{2,66}... | collective-permute-start | bytes 24584 | tf_op jit(solution)/shard_map/ppermute | solution.py:200
  31.7 0.5 collective-permute-start.5
  32.2 1.9 %collective-permute-done.4.refs_2_ = s32[16,128]{1,0:T(8,128)S(1)} collective-permute-done((s32[16,128]{1,0:T(8,128)S(1)}, s32[16,128]{1,0:T(8,128)S(1)}, u32[]{:S(2)}, u32[]{:S(2)}) %collective-permute-start.4) | collective-permute-done | bytes 8224 | tf_op jit(solution)/shard_map/ppermute | solution.py:200
  34.1 3.6 %collective-permute-start.11 = (f32[2,4,128,512]{3,2,1,0:T(8,128)}, f32[2,4,128,512]{3,2,1,0:T(8,128)}, u32[]{:S(2)}, u32[]{:S(2)}) collective-permute-start(f32[2,4,128,512]{3,2,1,0:T(8,128)} %get-tuple-element.84), channel_id=1, source_target_pairs={{0,24},{1,7},{2,26},{3,1},{4,28},{5,3},{6,30},{7,5},{8,0},{9,15},{... | collective-permute-start | bytes 6291464 | tf_op jit(solution)/shard_map/ppermute | solution.py:196
  37.8 0.0 collective-permute-done.5.refs_3_
  37.8 0.3 collective-permute-start.12
  38.1 1.8 %tables.1 = (bf16[4,4,512,256]{3,2,1,0:T(8,128)(2,1)S(1)}, f32[4,4,64,512]{3,2,1,0:T(8,128)S(1)}, f32[8,128]{1,0:T(8,128)S(1)}) custom-call(s32[16,128]{1,0:T(8,128)S(1)} %get-tuple-element.71.refs_0_, s32[16,128]{1,0:T(8,128)S(1)} %collective-permute-done.3.refs_1_, s32[16,128]{1,0:T(8,128)S(1)} %collective-permute-done.4.refs_2_, ...), custom_call_target="tpu_custom_call" | custom-call | flops 1000000 | bytes 4000000 | tf_op jit(solution)/shard_map/tables/pallas_call | solution.py:166
  39.9 1.5 %collective-permute-done.6.refs_4_.refs_2_ = f32[2,4,128,512]{3,2,1,0:T(8,128)S(1)} collective-permute-done((f32[2,4,128,512]{3,2,1,0:T(8,128)}, f32[2,4,128,512]{3,2,1,0:T(8,128)S(1)}, u32[]{:S(2)}, u32[]{:S(2)}) %collective-permute-start.6) | collective-permute-done | bytes 2097184 | tf_op jit(solution)/shard_map/ppermute | solution.py:196
  41.4 3.7 %collective-permute-done.7.refs_5_.refs_3_ = f32[2,4,128,512]{3,2,1,0:T(8,128)} collective-permute-done((f32[2,4,128,512]{3,2,1,0:T(8,128)}, f32[2,4,128,512]{3,2,1,0:T(8,128)}, u32[]{:S(2)}, u32[]{:S(2)}) %collective-permute-start.7) | collective-permute-done | bytes 2097184 | tf_op jit(solution)/shard_map/ppermute | solution.py:196
  45.1 0.7 own.1
  45.9 2.5 %pass.2 = (f32[4,128,512]{2,1,0:T(8,128)S(1)}, f32[4,128,512]{2,1,0:T(8,128)S(1)}, f32[8,128]{1,0:T(8,128)S(1)}) custom-call(bf16[4,4,2,256,1024]{4,3,2,1,0:T(8,128)(2,1)} %bitcast.13, f32[2,2,4,256,512]{4,3,2,1,0:T(8,128)} %collective-permute-done.8.refs_1_, f32[2,4,128,512]{3,2,1,0:T(8,128)S(1)} %collective-permute-done.6.refs_4_.refs_2_, ...), custom_call_target="tpu_custom_call" | custom-call | flops 1000000 | bytes 4000000 | tf_op jit(solution)/shard_map/pass/pallas_call | solution.py:166
  48.4 1.3 %collective-permute-start.10 = (f32[4,128,512]{2,1,0:T(8,128)S(1)}, f32[4,128,512]{2,1,0:T(8,128)S(1)}, u32[]{:S(2)}, u32[]{:S(2)}) collective-permute-start(f32[4,128,512]{2,1,0:T(8,128)S(1)} %get-tuple-element.83), channel_id=1, source_target_pairs={{0,8},{1,3},{2,10},{3,5},{4,12},{5,7},{6,14},{7,1},{8,16},{9,11},{... | collective-permute-start | bytes 3145736 | tf_op jit(solution)/shard_map/ppermute | solution.py:196
  49.8 2.2 %collective-permute-start.9 = (f32[4,128,512]{2,1,0:T(8,128)S(1)}, f32[4,128,512]{2,1,0:T(8,128)S(1)}, u32[]{:S(2)}, u32[]{:S(2)}) collective-permute-start(f32[4,128,512]{2,1,0:T(8,128)S(1)} %get-tuple-element.82), channel_id=1, source_target_pairs={{0,24},{1,7},{2,26},{3,1},{4,28},{5,3},{6,30},{7,5},{8,0},{9,15},{... | collective-permute-start | bytes 3145736 | tf_op jit(solution)/shard_map/ppermute | solution.py:196
  52.0 2.5 %before.2 = (f32[2,4,128,512]{3,2,1,0:T(8,128)S(1)}, f32[8,128]{1,0:T(8,128)S(1)}) custom-call(bf16[4,4,2,256,1024]{4,3,2,1,0:T(8,128)(2,1)} %bitcast.14, f32[2,2,4,256,512]{4,3,2,1,0:T(8,128)} %collective-permute-done.8.refs_1_, f32[2,4,128,512]{3,2,1,0:T(8,128)S(1)} %collective-permute-done.6.refs_4_.refs_2_, ...), custom_call_target="tpu_custom_call" | custom-call | flops 1000000 | bytes 4000000 | tf_op jit(solution)/shard_map/before/pallas_call | solution.py:166
  54.5 9.4 %collective-permute-done.11.refs_2_ = f32[2,4,128,512]{3,2,1,0:T(8,128)} collective-permute-done((f32[2,4,128,512]{3,2,1,0:T(8,128)}, f32[2,4,128,512]{3,2,1,0:T(8,128)}, u32[]{:S(2)}, u32[]{:S(2)}) %collective-permute-start.11) | collective-permute-done | bytes 2097184 | tf_op jit(solution)/shard_map/ppermute | solution.py:196
  63.9 3.7 %collective-permute-done.12.refs_3_ = f32[2,4,128,512]{3,2,1,0:T(8,128)} collective-permute-done((f32[2,4,128,512]{3,2,1,0:T(8,128)}, f32[2,4,128,512]{3,2,1,0:T(8,128)}, u32[]{:S(2)}, u32[]{:S(2)}) %collective-permute-start.12) | collective-permute-done | bytes 2097184 | tf_op jit(solution)/shard_map/ppermute | solution.py:196
  67.6 2.8 %pass.3 = (f32[4,128,512]{2,1,0:T(8,128)S(1)}, f32[4,128,512]{2,1,0:T(8,128)S(1)}, f32[8,128]{1,0:T(8,128)S(1)}) custom-call(bf16[4,4,2,256,1024]{4,3,2,1,0:T(8,128)(2,1)} %bitcast.15, f32[2,2,4,256,512]{4,3,2,1,0:T(8,128)} %collective-permute-done.8.refs_1_, f32[2,4,128,512]{3,2,1,0:T(8,128)} %collective-permute-done.11.refs_2_, ...), custom_call_target="tpu_custom_call" | custom-call | flops 1000000 | bytes 4000000 | tf_op jit(solution)/shard_map/pass/pallas_call | solution.py:166
  70.4 0.1 collective-permute-start.15
  70.5 2.0 %collective-permute-start.16 = (f32[4,128,512]{2,1,0:T(8,128)S(1)}, f32[4,128,512]{2,1,0:T(8,128)S(1)}, u32[]{:S(2)}, u32[]{:S(2)}) collective-permute-start(f32[4,128,512]{2,1,0:T(8,128)S(1)} %get-tuple-element.97), channel_id=1, source_target_pairs={{0,8},{1,3},{2,10},{3,5},{4,12},{5,7},{6,14},{7,1},{8,16},{9,11},{... | collective-permute-start | bytes 3145736 | tf_op jit(solution)/shard_map/ppermute | solution.py:196
  72.5 6.2 %collective-permute-done.10.refs_2_ = f32[4,128,512]{2,1,0:T(8,128)S(1)} collective-permute-done((f32[4,128,512]{2,1,0:T(8,128)S(1)}, f32[4,128,512]{2,1,0:T(8,128)S(1)}, u32[]{:S(2)}, u32[]{:S(2)}) %collective-permute-start.10) | collective-permute-done | bytes 1048608 | tf_op jit(solution)/shard_map/ppermute | solution.py:196
  78.7 0.2 turn.2
  78.9 3.3 %collective-permute-start.13 = (f32[2,128,512]{2,1,0:T(8,128)S(1)}, f32[2,128,512]{2,1,0:T(8,128)S(1)}, u32[]{:S(2)}, u32[]{:S(2)}) collective-permute-start(f32[2,128,512]{2,1,0:T(8,128)S(1)} %get-tuple-element.92), channel_id=1, source_target_pairs={{0,6},{1,25},{2,0},{3,27},{4,2},{5,29},{6,4},{7,31},{8,14},{9,1},{... | collective-permute-start | bytes 1572872 | tf_op jit(solution)/shard_map/ppermute | solution.py:196
  82.2 2.8 %before.3 = (f32[2,4,128,512]{3,2,1,0:T(8,128)S(1)}, f32[8,128]{1,0:T(8,128)S(1)}) custom-call(bf16[4,4,2,256,1024]{4,3,2,1,0:T(8,128)(2,1)} %bitcast.16, f32[2,2,4,256,512]{4,3,2,1,0:T(8,128)} %collective-permute-done.8.refs_1_, f32[2,4,128,512]{3,2,1,0:T(8,128)} %collective-permute-done.11.refs_2_, f32[2,4,128,512]{3,2,1,0:T(8,128)} %collective-permute-done.12.refs_3_, ...), custom_call_target="tpu_custom_call" | custom-call | flops 1000000 | bytes 4000000 | tf_op jit(solution)/shard_map/before/pallas_call | solution.py:166
  85.0 5.9 %collective-permute-done.15.refs_1_ = f32[4,128,512]{2,1,0:T(8,128)S(1)} collective-permute-done((f32[4,128,512]{2,1,0:T(8,128)S(1)}, f32[4,128,512]{2,1,0:T(8,128)S(1)}, u32[]{:S(2)}, u32[]{:S(2)}) %collective-permute-start.15) | collective-permute-done | bytes 1048608 | tf_op jit(solution)/shard_map/ppermute | solution.py:196
  90.9 4.0 %collective-permute-done.16.refs_2_ = f32[4,128,512]{2,1,0:T(8,128)S(1)} collective-permute-done((f32[4,128,512]{2,1,0:T(8,128)S(1)}, f32[4,128,512]{2,1,0:T(8,128)S(1)}, u32[]{:S(2)}, u32[]{:S(2)}) %collective-permute-start.16) | collective-permute-done | bytes 1048608 | tf_op jit(solution)/shard_map/ppermute | solution.py:196
  94.9 0.3 turn.3
  95.2 0.0 copy-start
  95.2 0.0 copy-start.3
  95.2 0.0 copy-start.4
  95.2 3.8 %collective-permute-start.19 = (f32[2,128,512]{2,1,0:T(8,128)S(1)}, f32[2,128,512]{2,1,0:T(8,128)S(1)}, u32[]{:S(2)}, u32[]{:S(2)}) collective-permute-start(f32[2,128,512]{2,1,0:T(8,128)S(1)} %get-tuple-element.104), channel_id=1, source_target_pairs={{0,6},{1,25},{2,0},{3,27},{4,2},{5,29},{6,4},{7,31},{8,14},{9,1},{... | collective-permute-start | bytes 1572872 | tf_op jit(solution)/shard_map/ppermute | solution.py:196
  99.0 0.1 relay.2
  99.1 3.3 %collective-permute-start.17 = (f32[128,512]{1,0:T(8,128)S(1)}, f32[128,512]{1,0:T(8,128)S(1)}, u32[]{:S(2)}, u32[]{:S(2)}) collective-permute-start(f32[128,512]{1,0:T(8,128)S(1)} %get-tuple-element.100), channel_id=1, source_target_pairs={{0,6},{1,25},{2,0},{3,27},{4,2},{5,29},{6,4},{7,31},{8,14},{9,1},{... | collective-permute-start | bytes 786440 | tf_op jit(solution)/shard_map/ppermute | solution.py:196
  102.4 3.3 %collective-permute-done.19.refs_2_.refs_11_ = f32[2,128,512]{2,1,0:T(8,128)S(1)} collective-permute-done((f32[2,128,512]{2,1,0:T(8,128)S(1)}, f32[2,128,512]{2,1,0:T(8,128)S(1)}, u32[]{:S(2)}, u32[]{:S(2)}) %collective-permute-start.19) | collective-permute-done | bytes 524320 | tf_op jit(solution)/shard_map/ppermute | solution.py:196
  105.7 3.7 %collective-permute-done.20.refs_3_.refs_10_ = f32[2,128,512]{2,1,0:T(8,128)S(1)} collective-permute-done((f32[2,128,512]{2,1,0:T(8,128)S(1)}, f32[2,128,512]{2,1,0:T(8,128)S(1)}, u32[]{:S(2)}, u32[]{:S(2)}) %collective-permute-start.20) | collective-permute-done | bytes 524320 | tf_op jit(solution)/shard_map/ppermute | solution.py:196
  109.4 0.1 relay.3
  109.5 0.1 collective-permute-start.21
  109.5 2.0 %collective-permute-start.22 = (f32[128,512]{1,0:T(8,128)S(1)}, f32[128,512]{1,0:T(8,128)S(1)}, u32[]{:S(2)}, u32[]{:S(2)}) collective-permute-start(f32[128,512]{1,0:T(8,128)S(1)} %get-tuple-element.112), channel_id=1, source_target_pairs={{0,2},{1,9},{2,4},{3,11},{4,6},{5,13},{6,0},{7,15},{8,10},{9,17},{... | collective-permute-start | bytes 786440 | tf_op jit(solution)/shard_map/ppermute | solution.py:196
  112.3 1.1 values.2
  113.3 2.6 %collective-permute-done.21.refs_8_ = f32[128,512]{1,0:T(8,128)S(1)} collective-permute-done((f32[128,512]{1,0:T(8,128)S(1)}, f32[128,512]{1,0:T(8,128)S(1)}, u32[]{:S(2)}, u32[]{:S(2)}) %collective-permute-start.21) | collective-permute-done | bytes 262176 | tf_op jit(solution)/shard_map/ppermute | solution.py:196
  115.9 1.3 collective-permute-done.22.refs_9_
  117.2 1.5 %values.3 = (f32[128,1024]{1,0:T(8,128)S(1)}, f32[16,128]{1,0:T(8,128)S(1)}, f32[8,128]{1,0:T(8,128)}) custom-call(f32[256,1024]{1,0:T(8,128)S(1)} %bitcast.6, s32[1]{0:T(128)S(6)} %copy.12.refs_1_, bf16[256,256]{1,0:T(8,128)(2,1)S(1)} %copy-done.3, bf16[256,256]{1,0:T(8,128)(2,1)S(1)} %copy-done.4, bf16[4,4,256,128]{3,2,1,0:T(8,128)(2,1)S(1)} %get-tuple-element.76.refs_4_, ...), custom_call_target="tpu_custom_call" | custom-call | flops 1000000 | bytes 4000000 | tf_op jit(solution)/shard_map/values/pallas_call | solution.py:166
  118.7 1.5 %collective-permute-start.23 = (f32[16,128]{1,0:T(8,128)S(1)}, f32[16,128]{1,0:T(8,128)S(1)}, u32[]{:S(2)}, u32[]{:S(2)}) collective-permute-start(f32[16,128]{1,0:T(8,128)S(1)} %get-tuple-element.116.refs_2_.refs_0_), channel_id=1, source_target_pairs={{0,32},{32,0},{64,96},{96,64},{1,33},{33,1},{65,97},{97,65},{2,34}... | collective-permute-start | bytes 24584 | tf_op jit(solution)/shard_map/ppermute | solution.py:200
  120.2 2.7 %collective-permute-start.24 = (f32[16,128]{1,0:T(8,128)S(1)}, f32[16,128]{1,0:T(8,128)S(1)}, u32[]{:S(2)}, u32[]{:S(2)}) collective-permute-start(f32[16,128]{1,0:T(8,128)S(1)} %get-tuple-element.116.refs_2_.refs_0_), channel_id=1, source_target_pairs={{0,64},{32,96},{64,0},{96,32},{1,65},{33,97},{65,1},{97,33},{2,66}... | collective-permute-start | bytes 24584 | tf_op jit(solution)/shard_map/ppermute | solution.py:200
  122.9 0.5 collective-permute-start.25
  123.4 2.4 %keep.1 = (f32[256,1024]{1,0:T(8,128)}, f32[8,128]{1,0:T(8,128)}) custom-call(f32[128,1024]{1,0:T(8,128)S(1)} %get-tuple-element.108.refs_0_, f32[128,1024]{1,0:T(8,128)S(1)} %get-tuple-element.115.refs_1_, f32[16,128]{1,0:T(8,128)S(1)} %get-tuple-element.116.refs_2_.refs_0_, bf16[256,256]{1,0:T(8,128)(2,1)S(1)} %copy-done.1, ...), custom_call_target="tpu_custom_call" | custom-call | flops 1000000 | bytes 4000000 | tf_op jit(solution)/shard_map/keep/pallas_call | solution.py:166
  125.8 2.0 %collective-permute-done.25.refs_3_ = f32[16,128]{1,0:T(8,128)S(1)} collective-permute-done((f32[16,128]{1,0:T(8,128)S(1)}, f32[16,128]{1,0:T(8,128)S(1)}, u32[]{:S(2)}, u32[]{:S(2)}) %collective-permute-start.25) | collective-permute-done | bytes 8224 | tf_op jit(solution)/shard_map/ppermute | solution.py:200
  127.8 3.0 %update.1 = (f32[256,1024]{1,0:T(8,128)}, f32[8,128]{1,0:T(8,128)}) custom-call(f32[16,128]{1,0:T(8,128)S(1)} %get-tuple-element.116.refs_2_.refs_0_, f32[16,128]{1,0:T(8,128)S(1)} %collective-permute-done.23.refs_1_, f32[16,128]{1,0:T(8,128)S(1)} %collective-permute-done.24.refs_2_, f32[16,128]{1,0:T(8,128)S(1)} %collective-permute-done.25.refs_3_, ...), custom_call_target="tpu_custom_call" | custom-call | flops 1000000 | bytes 4000000 | tf_op jit(solution)/shard_map/update/pallas_call | solution.py:166
  (26 shorter events, 0.1 us)
Async XLA Ops:
  2.0 4.2 %collective-permute-start = (f32[1,2,4,128,512]{4,3,2,1,0:T(8,128)S(1)}, f32[1,2,4,128,512]{4,3,2,1,0:T(8,128)S(1)}, u32[]{:S(2)}, u32[]{:S(2)}) collective-permute-start(f32[1,2,4,128,512]{4,3,2,1,0:T(8,128)S(1)} %get-tuple-element.64), channel_id=1, source_target_pairs={{0,1},{1,0},{2,3},{3,2},{4,5},{5,4},{6,7},{7,6},{8,9},{9,8},{10,11... | collective-permute-start | bytes 6291464 | tf_op jit(solution)/shard_map/ppermute | solution.py:188
  3.5 6.3 %collective-permute-start.2 = (f32[1,2,4,128,512]{4,3,2,1,0:T(8,128)S(1)}, f32[1,2,4,128,512]{4,3,2,1,0:T(8,128)S(1)}, u32[]{:S(2)}, u32[]{:S(2)}) collective-permute-start(f32[1,2,4,128,512]{4,3,2,1,0:T(8,128)S(1)} %get-tuple-element.66), channel_id=1, source_target_pairs={{0,1},{1,0},{2,3},{3,2},{4,5},{5,4},{6,7},{7,6},{8,9},{9,8},{10,11... | collective-permute-start | bytes 6291464 | tf_op jit(solution)/shard_map/ppermute | solution.py:188
  9.6 8.1 %collective-permute-start.1 = (f32[2,2,4,128,512]{4,3,2,1,0:T(8,128)}, f32[2,2,4,128,512]{4,3,2,1,0:T(8,128)}, u32[]{:S(2)}, u32[]{:S(2)}) collective-permute-start(f32[2,2,4,128,512]{4,3,2,1,0:T(8,128)} %get-tuple-element.65), channel_id=1, source_target_pairs={{0,1},{1,0},{2,3},{3,2},{4,5},{5,4},{6,7},{7,6},{8,9},{9,8},{10,11... | collective-permute-start | bytes 12582920 | tf_op jit(solution)/shard_map/ppermute | solution.py:188
  9.8 7.8 %copy-start.7 = (s32[1,4,16,32]{3,2,1,0:T(8,128)S(1)}, s32[1,4,16,32]{3,2,1,0:T(8,128)}, u32[]{:S(2)}) copy-start(s32[1,4,16,32]{3,2,1,0:T(8,128)} %param.12) | copy-start | bytes 24580
  13.4 28.1 %collective-permute-start.6 = (f32[2,4,128,512]{3,2,1,0:T(8,128)}, f32[2,4,128,512]{3,2,1,0:T(8,128)S(1)}, u32[]{:S(2)}, u32[]{:S(2)}) collective-permute-start(f32[2,4,128,512]{3,2,1,0:T(8,128)} %get-tuple-element.74), channel_id=1, source_target_pairs={{0,24},{1,7},{2,26},{3,1},{4,28},{5,3},{6,30},{7,5},{8,0},{9,15},{... | collective-permute-start | bytes 6291464 | tf_op jit(solution)/shard_map/ppermute | solution.py:196
  17.6 27.6 %collective-permute-start.7 = (f32[2,4,128,512]{3,2,1,0:T(8,128)}, f32[2,4,128,512]{3,2,1,0:T(8,128)}, u32[]{:S(2)}, u32[]{:S(2)}) collective-permute-start(f32[2,4,128,512]{3,2,1,0:T(8,128)} %get-tuple-element.75), channel_id=1, source_target_pairs={{0,8},{1,3},{2,10},{3,5},{4,12},{5,7},{6,14},{7,1},{8,16},{9,11},{... | collective-permute-start | bytes 6291464 | tf_op jit(solution)/shard_map/ppermute | solution.py:196
  22.9 15.2 %copy-start.5 = (bf16[64,64]{1,0:T(8,128)(2,1)S(1)}, bf16[64,64]{1,0:T(8,128)(2,1)}, u32[]{:S(2)}) copy-start(bf16[64,64]{1,0:T(8,128)(2,1)} %constant.16.clone.refs_4_.refs_1_) | copy-start | bytes 24580
  22.9 15.2 %copy-start.6 = (bf16[64,64]{1,0:T(8,128)(2,1)S(1)}, bf16[64,64]{1,0:T(8,128)(2,1)}, u32[]{:S(2)}) copy-start(bf16[64,64]{1,0:T(8,128)(2,1)} %constant.17.clone.refs_5_.refs_2_) | copy-start | bytes 24580
  27.4 4.8 %collective-permute-start.3 = (s32[16,128]{1,0:T(8,128)S(1)}, s32[16,128]{1,0:T(8,128)S(1)}, u32[]{:S(2)}, u32[]{:S(2)}) collective-permute-start(s32[16,128]{1,0:T(8,128)S(1)} %get-tuple-element.71.refs_0_), channel_id=1, source_target_pairs={{0,32},{32,0},{64,96},{96,64},{1,33},{33,1},{65,97},{97,65},{2,34}... | collective-permute-start | bytes 24584 | tf_op jit(solution)/shard_map/ppermute | solution.py:200
  29.0 5.2 %collective-permute-start.4 = (s32[16,128]{1,0:T(8,128)S(1)}, s32[16,128]{1,0:T(8,128)S(1)}, u32[]{:S(2)}, u32[]{:S(2)}) collective-permute-start(s32[16,128]{1,0:T(8,128)S(1)} %get-tuple-element.71.refs_0_), channel_id=1, source_target_pairs={{0,64},{32,96},{64,0},{96,32},{1,65},{33,97},{65,1},{97,33},{2,66}... | collective-permute-start | bytes 24584 | tf_op jit(solution)/shard_map/ppermute | solution.py:200
  31.7 6.0 %collective-permute-start.5 = (s32[16,128]{1,0:T(8,128)S(1)}, s32[16,128]{1,0:T(8,128)S(1)}, u32[]{:S(2)}, u32[]{:S(2)}) collective-permute-start(s32[16,128]{1,0:T(8,128)S(1)} %get-tuple-element.71.refs_0_), channel_id=1, source_target_pairs={{0,96},{32,64},{64,32},{96,0},{1,97},{33,65},{65,33},{97,1},{2,98}... | collective-permute-start | bytes 24584 | tf_op jit(solution)/shard_map/ppermute | solution.py:200
  32.2 13.7 %collective-permute-start.8 = (f32[2,2,4,256,512]{4,3,2,1,0:T(8,128)}, f32[2,2,4,256,512]{4,3,2,1,0:T(8,128)}, u32[]{:S(2)}, u32[]{:S(2)}) collective-permute-start(f32[2,2,4,256,512]{4,3,2,1,0:T(8,128)} %get-tuple-element.78), channel_id=1, source_target_pairs={{0,1},{1,0},{2,3},{3,2},{4,5},{5,4},{6,7},{7,6},{8,9},{9,8},{10,11... | collective-permute-start | bytes 25165832 | tf_op jit(solution)/shard_map/ppermute | solution.py:188
  34.1 29.8 %collective-permute-start.11 = (f32[2,4,128,512]{3,2,1,0:T(8,128)}, f32[2,4,128,512]{3,2,1,0:T(8,128)}, u32[]{:S(2)}, u32[]{:S(2)}) collective-permute-start(f32[2,4,128,512]{3,2,1,0:T(8,128)} %get-tuple-element.84), channel_id=1, source_target_pairs={{0,24},{1,7},{2,26},{3,1},{4,28},{5,3},{6,30},{7,5},{8,0},{9,15},{... | collective-permute-start | bytes 6291464 | tf_op jit(solution)/shard_map/ppermute | solution.py:196
  37.8 29.8 %collective-permute-start.12 = (f32[2,4,128,512]{3,2,1,0:T(8,128)}, f32[2,4,128,512]{3,2,1,0:T(8,128)}, u32[]{:S(2)}, u32[]{:S(2)}) collective-permute-start(f32[2,4,128,512]{3,2,1,0:T(8,128)} %get-tuple-element.85), channel_id=1, source_target_pairs={{0,8},{1,3},{2,10},{3,5},{4,12},{5,7},{6,14},{7,1},{8,16},{9,11},{... | collective-permute-start | bytes 6291464 | tf_op jit(solution)/shard_map/ppermute | solution.py:196
  48.4 30.3 %collective-permute-start.10 = (f32[4,128,512]{2,1,0:T(8,128)S(1)}, f32[4,128,512]{2,1,0:T(8,128)S(1)}, u32[]{:S(2)}, u32[]{:S(2)}) collective-permute-start(f32[4,128,512]{2,1,0:T(8,128)S(1)} %get-tuple-element.83), channel_id=1, source_target_pairs={{0,8},{1,3},{2,10},{3,5},{4,12},{5,7},{6,14},{7,1},{8,16},{9,11},{... | collective-permute-start | bytes 3145736 | tf_op jit(solution)/shard_map/ppermute | solution.py:196
  49.8 29.0 %collective-permute-start.9 = (f32[4,128,512]{2,1,0:T(8,128)S(1)}, f32[4,128,512]{2,1,0:T(8,128)S(1)}, u32[]{:S(2)}, u32[]{:S(2)}) collective-permute-start(f32[4,128,512]{2,1,0:T(8,128)S(1)} %get-tuple-element.82), channel_id=1, source_target_pairs={{0,24},{1,7},{2,26},{3,1},{4,28},{5,3},{6,30},{7,5},{8,0},{9,15},{... | collective-permute-start | bytes 3145736 | tf_op jit(solution)/shard_map/ppermute | solution.py:196
  70.4 20.5 %collective-permute-start.15 = (f32[4,128,512]{2,1,0:T(8,128)S(1)}, f32[4,128,512]{2,1,0:T(8,128)S(1)}, u32[]{:S(2)}, u32[]{:S(2)}) collective-permute-start(f32[4,128,512]{2,1,0:T(8,128)S(1)} %get-tuple-element.96), channel_id=1, source_target_pairs={{0,24},{1,7},{2,26},{3,1},{4,28},{5,3},{6,30},{7,5},{8,0},{9,15},{... | collective-permute-start | bytes 3145736 | tf_op jit(solution)/shard_map/ppermute | solution.py:196
  70.5 24.4 %collective-permute-start.16 = (f32[4,128,512]{2,1,0:T(8,128)S(1)}, f32[4,128,512]{2,1,0:T(8,128)S(1)}, u32[]{:S(2)}, u32[]{:S(2)}) collective-permute-start(f32[4,128,512]{2,1,0:T(8,128)S(1)} %get-tuple-element.97), channel_id=1, source_target_pairs={{0,8},{1,3},{2,10},{3,5},{4,12},{5,7},{6,14},{7,1},{8,16},{9,11},{... | collective-permute-start | bytes 3145736 | tf_op jit(solution)/shard_map/ppermute | solution.py:196
  78.9 20.1 %collective-permute-start.13 = (f32[2,128,512]{2,1,0:T(8,128)S(1)}, f32[2,128,512]{2,1,0:T(8,128)S(1)}, u32[]{:S(2)}, u32[]{:S(2)}) collective-permute-start(f32[2,128,512]{2,1,0:T(8,128)S(1)} %get-tuple-element.92), channel_id=1, source_target_pairs={{0,6},{1,25},{2,0},{3,27},{4,2},{5,29},{6,4},{7,31},{8,14},{9,1},{... | collective-permute-start | bytes 1572872 | tf_op jit(solution)/shard_map/ppermute | solution.py:196
  82.2 16.8 %collective-permute-start.14 = (f32[2,128,512]{2,1,0:T(8,128)S(1)}, f32[2,128,512]{2,1,0:T(8,128)S(1)}, u32[]{:S(2)}, u32[]{:S(2)}) collective-permute-start(f32[2,128,512]{2,1,0:T(8,128)S(1)} %get-tuple-element.93), channel_id=1, source_target_pairs={{0,2},{1,9},{2,4},{3,11},{4,6},{5,13},{6,0},{7,15},{8,10},{9,17},{... | collective-permute-start | bytes 1572872 | tf_op jit(solution)/shard_map/ppermute | solution.py:196
  95.2 17.1 %copy-start = (f32[1,256,1024]{2,1,0:T(8,128)S(1)}, f32[1,256,1024]{2,1,0:T(8,128)}, u32[]{:S(2)}) copy-start(f32[1,256,1024]{2,1,0:T(8,128)} %param.11) | copy-start | bytes 3145732
  95.2 17.1 %copy-start.3 = (bf16[256,256]{1,0:T(8,128)(2,1)S(1)}, bf16[256,256]{1,0:T(8,128)(2,1)}, u32[]{:S(2)}) copy-start(bf16[256,256]{1,0:T(8,128)(2,1)} %constant.12.clone.refs_2_) | copy-start | bytes 393220
  95.2 17.1 %copy-start.4 = (bf16[256,256]{1,0:T(8,128)(2,1)S(1)}, bf16[256,256]{1,0:T(8,128)(2,1)}, u32[]{:S(2)}) copy-start(bf16[256,256]{1,0:T(8,128)(2,1)} %constant.13.clone.refs_3_) | copy-start | bytes 393220
  95.2 10.5 %collective-permute-start.19 = (f32[2,128,512]{2,1,0:T(8,128)S(1)}, f32[2,128,512]{2,1,0:T(8,128)S(1)}, u32[]{:S(2)}, u32[]{:S(2)}) collective-permute-start(f32[2,128,512]{2,1,0:T(8,128)S(1)} %get-tuple-element.104), channel_id=1, source_target_pairs={{0,6},{1,25},{2,0},{3,27},{4,2},{5,29},{6,4},{7,31},{8,14},{9,1},{... | collective-permute-start | bytes 1572872 | tf_op jit(solution)/shard_map/ppermute | solution.py:196
  99.0 10.4 %collective-permute-start.20 = (f32[2,128,512]{2,1,0:T(8,128)S(1)}, f32[2,128,512]{2,1,0:T(8,128)S(1)}, u32[]{:S(2)}, u32[]{:S(2)}) collective-permute-start(f32[2,128,512]{2,1,0:T(8,128)S(1)} %get-tuple-element.105), channel_id=1, source_target_pairs={{0,2},{1,9},{2,4},{3,11},{4,6},{5,13},{6,0},{7,15},{8,10},{9,17},{... | collective-permute-start | bytes 1572872 | tf_op jit(solution)/shard_map/ppermute | solution.py:196
  99.1 13.1 %collective-permute-start.17 = (f32[128,512]{1,0:T(8,128)S(1)}, f32[128,512]{1,0:T(8,128)S(1)}, u32[]{:S(2)}, u32[]{:S(2)}) collective-permute-start(f32[128,512]{1,0:T(8,128)S(1)} %get-tuple-element.100), channel_id=1, source_target_pairs={{0,6},{1,25},{2,0},{3,27},{4,2},{5,29},{6,4},{7,31},{8,14},{9,1},{... | collective-permute-start | bytes 786440 | tf_op jit(solution)/shard_map/ppermute | solution.py:196
  102.4 9.9 %collective-permute-start.18 = (f32[128,512]{1,0:T(8,128)S(1)}, f32[128,512]{1,0:T(8,128)S(1)}, u32[]{:S(2)}, u32[]{:S(2)}) collective-permute-start(f32[128,512]{1,0:T(8,128)S(1)} %get-tuple-element.101), channel_id=1, source_target_pairs={{0,2},{1,9},{2,4},{3,11},{4,6},{5,13},{6,0},{7,15},{8,10},{9,17},{... | collective-permute-start | bytes 786440 | tf_op jit(solution)/shard_map/ppermute | solution.py:196
  109.5 6.4 %collective-permute-start.21 = (f32[128,512]{1,0:T(8,128)S(1)}, f32[128,512]{1,0:T(8,128)S(1)}, u32[]{:S(2)}, u32[]{:S(2)}) collective-permute-start(f32[128,512]{1,0:T(8,128)S(1)} %get-tuple-element.111), channel_id=1, source_target_pairs={{0,6},{1,25},{2,0},{3,27},{4,2},{5,29},{6,4},{7,31},{8,14},{9,1},{... | collective-permute-start | bytes 786440 | tf_op jit(solution)/shard_map/ppermute | solution.py:196
  109.5 7.7 %collective-permute-start.22 = (f32[128,512]{1,0:T(8,128)S(1)}, f32[128,512]{1,0:T(8,128)S(1)}, u32[]{:S(2)}, u32[]{:S(2)}) collective-permute-start(f32[128,512]{1,0:T(8,128)S(1)} %get-tuple-element.112), channel_id=1, source_target_pairs={{0,2},{1,9},{2,4},{3,11},{4,6},{5,13},{6,0},{7,15},{8,10},{9,17},{... | collective-permute-start | bytes 786440 | tf_op jit(solution)/shard_map/ppermute | solution.py:196
  117.2 6.2 %copy-start.1 = (bf16[256,256]{1,0:T(8,128)(2,1)S(1)}, bf16[256,256]{1,0:T(8,128)(2,1)}, u32[]{:S(2)}) copy-start(bf16[256,256]{1,0:T(8,128)(2,1)} %constant.14.clone.refs_3_.refs_4_) | copy-start | bytes 393220
  117.2 6.2 %copy-start.2 = (bf16[256,256]{1,0:T(8,128)(2,1)S(1)}, bf16[256,256]{1,0:T(8,128)(2,1)}, u32[]{:S(2)}) copy-start(bf16[256,256]{1,0:T(8,128)(2,1)} %constant.15.clone.refs_4_.refs_5_) | copy-start | bytes 393220
  118.7 7.1 %collective-permute-start.23 = (f32[16,128]{1,0:T(8,128)S(1)}, f32[16,128]{1,0:T(8,128)S(1)}, u32[]{:S(2)}, u32[]{:S(2)}) collective-permute-start(f32[16,128]{1,0:T(8,128)S(1)} %get-tuple-element.116.refs_2_.refs_0_), channel_id=1, source_target_pairs={{0,32},{32,0},{64,96},{96,64},{1,33},{33,1},{65,97},{97,65},{2,34}... | collective-permute-start | bytes 24584 | tf_op jit(solution)/shard_map/ppermute | solution.py:200
  120.2 5.6 %collective-permute-start.24 = (f32[16,128]{1,0:T(8,128)S(1)}, f32[16,128]{1,0:T(8,128)S(1)}, u32[]{:S(2)}, u32[]{:S(2)}) collective-permute-start(f32[16,128]{1,0:T(8,128)S(1)} %get-tuple-element.116.refs_2_.refs_0_), channel_id=1, source_target_pairs={{0,64},{32,96},{64,0},{96,32},{1,65},{33,97},{65,1},{97,33},{2,66}... | collective-permute-start | bytes 24584 | tf_op jit(solution)/shard_map/ppermute | solution.py:200
  122.9 4.9 %collective-permute-start.25 = (f32[16,128]{1,0:T(8,128)S(1)}, f32[16,128]{1,0:T(8,128)S(1)}, u32[]{:S(2)}, u32[]{:S(2)}) collective-permute-start(f32[16,128]{1,0:T(8,128)S(1)} %get-tuple-element.116.refs_2_.refs_0_), channel_id=1, source_target_pairs={{0,96},{32,64},{64,32},{96,0},{1,97},{33,65},{65,33},{97,1},{2,98}... | collective-permute-start | bytes 24584 | tf_op jit(solution)/shard_map/ppermute | solution.py:200

commit v4 on v3

--- a/solution.py
+++ b/solution.py
@@ -68,6 +68,10 @@
             out[-1].start()
     for cp in out[-SLOTS:]:
         cp.wait()
+
+
+def gate_kernel(out_ref):
+    out_ref[...] = jnp.zeros((8, 128), F32)
 
 
 def near_conv_kernel(stages, r0, rows, g_ref, w_ref, buf, sems):
@@ -414,7 +418,8 @@
     got_a, n = other_core(g, (0,), a0, a_rows)
     got, n = other_core(g, (1,), a0, a_rows, [n])
     got_a.update(got)
-    got_b, n = other_core(g, (0, 1), b0, b_rows, [n, got_a[0][0]])
+    got_b, n = other_core(g, (0, 1), b0, b_rows, [n])
+    _, n = call(gate_kernel, vm((8, 128)), [], "gate", after=[n, got_a[0][0]])
     first, last = parts = [Part(g, a0, a_rows, got_a), Part(g, b0, b_rows, got_b)]
     n = first.send([n], cost=AHEAD)
     n = last.send([n])

time: 131 us -> 131 us (level)
    pallas_call x21 -> x22, Pallas kernels: 41.1 us -> 41.7 us  [call(): pl.pallas_call(kernel, out_shape=outs + [vm((8, 128))], in_specs=in_specs...]
  transfers between devices with their start and end apart: 26 -> 26, of which waited for: 14 -> 14; matrix products, arithmetic and copies ran while one was open for 0% -> 0% of each run, Pallas kernels for 20% -> 21%
where the time goes in v4:
time: 131 us; the launch traced here: 130 us
  waiting for transfers between devices  51.6 us (39%)
  Pallas kernels  41.7 us (32%)
  starting transfers between devices  35.3 us (27%)
  between operations  1.74 us (1%)
    ppermute x16, waiting for transfers between devices, along(): return lax.ppermute(x, 'shard', pairs)  46.5 us
    pallas_call x22, Pallas kernels, call(): pl.pallas_call(kernel, out_shape=outs + [vm((8, 128))], in_specs=in_specs...  41.7 us
    ppermute x16, starting transfers between devices, along(): return lax.ppermute(x, 'shard', pairs)  25 us
    ppermute x6, starting transfers between devices, swap_grp(): return lax.ppermute(x, 'grp', [(i, i ^ k) for i in range(NX)])  9.48 us
    ppermute x6, waiting for transfers between devices, swap_grp(): return lax.ppermute(x, 'grp', [(i, i ^ k) for i in range(NX)])  3.91 us
  transfers between devices with their start and end apart: 26, of which 14 were waited for; matrix products, arithmetic and copies ran while one was open for 0% of the time, Pallas kernels for 21%

profile of v4, /device:TPU:0, one launch (start us, length us, event | category | flops | bytes accessed | tf_op | source)
XLA Modules:
  0.0 130.4 jit_solution(8492819328228980510)
XLA Ops:
  0.6 1.4 %conv0.2 = (f32[1,2,4,128,512]{4,3,2,1,0:T(8,128)S(1)}, f32[8,128]{1,0:T(8,128)S(1)}) custom-call(bf16[4,4,2,256,1024]{4,3,2,1,0:T(8,128)(2,1)} %bitcast.7), custom_call_target="tpu_custom_call" | custom-call | flops 1000000 | bytes 4000000 | tf_op jit(solution)/shard_map/conv0/pallas_call | solution.py:170
  2.0 0.1 collective-permute-start.1
  2.1 1.4 %conv1.1 = (f32[1,2,4,128,512]{4,3,2,1,0:T(8,128)S(1)}, f32[8,128]{1,0:T(8,128)S(1)}) custom-call(bf16[4,4,2,256,1024]{4,3,2,1,0:T(8,128)(2,1)} %bitcast.8, f32[8,128]{1,0:T(8,128)S(1)} %get-tuple-element.63.refs_1_), custom_call_target="tpu_custom_call" | custom-call | flops 1000000 | bytes 4000000 | tf_op jit(solution)/shard_map/conv1/pallas_call | solution.py:170
  3.5 0.5 collective-permute-start.2
  4.1 3.3 %conv0.3 = (f32[2,2,4,128,512]{4,3,2,1,0:T(8,128)}, f32[8,128]{1,0:T(8,128)S(1)}) custom-call(bf16[4,4,2,256,1024]{4,3,2,1,0:T(8,128)(2,1)} %bitcast.9, f32[8,128]{1,0:T(8,128)S(1)} %get-tuple-element.64.refs_1_), custom_call_target="tpu_custom_call" | custom-call | flops 1000000 | bytes 4000000 | tf_op jit(solution)/shard_map/conv0/pallas_call | solution.py:170
  7.4 0.1 collective-permute-start
  7.5 0.6 gate.1
  8.1 1.1 collective-permute-done.2.refs_2_
  9.3 3.5 %send.2 = (f32[2,4,128,512]{3,2,1,0:T(8,128)}, f32[2,4,128,512]{3,2,1,0:T(8,128)}, f32[8,128]{1,0:T(8,128)S(1)}) custom-call(bf16[4,4,2,256,1024]{4,3,2,1,0:T(8,128)(2,1)} %bitcast.10, f32[1,2,4,128,512]{4,3,2,1,0:T(8,128)S(1)} %collective-permute-done.1.refs_1_, f32[1,2,4,128,512]{4,3,2,1,0:T(8,128)S(1)} %collective-permute-done.2.refs_2_, ...), custom_call_target="tpu_custom_call" | custom-call | flops 199999995904 | bytes 1000000000 | tf_op jit(solution)/shard_map/send/pallas_call | solution.py:170
  12.8 4.2 %collective-permute-start.6 = (f32[2,4,128,512]{3,2,1,0:T(8,128)}, f32[2,4,128,512]{3,2,1,0:T(8,128)S(1)}, u32[]{:S(2)}, u32[]{:S(2)}) collective-permute-start(f32[2,4,128,512]{3,2,1,0:T(8,128)} %get-tuple-element.76), channel_id=1, source_target_pairs={{0,24},{1,7},{2,26},{3,1},{4,28},{5,3},{6,30},{7,5},{8,0},{9,15},{... | collective-permute-start | bytes 6291464 | tf_op jit(solution)/shard_map/ppermute | solution.py:200
  17.0 0.1 reshape.10.refs_0_
  17.1 5.2 %send.3 = (f32[2,4,128,512]{3,2,1,0:T(8,128)}, f32[2,4,128,512]{3,2,1,0:T(8,128)}, f32[8,128]{1,0:T(8,128)S(1)}) custom-call(bf16[4,4,2,256,1024]{4,3,2,1,0:T(8,128)(2,1)} %bitcast.11, f32[2,2,4,128,512]{4,3,2,1,0:T(8,128)} %collective-permute-done.refs_1_, f32[8,128]{1,0:T(8,128)S(1)} %get-tuple-element.70.refs_2_), custom_call_target="tpu_custom_call" | custom-call | flops 1000000 | bytes 4000000 | tf_op jit(solution)/shard_map/send/pallas_call | solution.py:170
  22.3 0.0 copy-start.5
  22.3 0.0 copy-start.6
  22.4 4.5 %conv2.1 = (f32[2,2,4,256,512]{4,3,2,1,0:T(8,128)}, f32[8,128]{1,0:T(8,128)S(1)}) custom-call(bf16[4,4,2,256,1024]{4,3,2,1,0:T(8,128)(2,1)} %bitcast.12, f32[8,128]{1,0:T(8,128)S(1)} %get-tuple-element.71.refs_1_), custom_call_target="tpu_custom_call" | custom-call | flops 1000000 | bytes 4000000 | tf_op jit(solution)/shard_map/conv2/pallas_call | solution.py:170
  26.9 1.6 %collective-permute-start.3 = (s32[16,128]{1,0:T(8,128)S(1)}, s32[16,128]{1,0:T(8,128)S(1)}, u32[]{:S(2)}, u32[]{:S(2)}) collective-permute-start(s32[16,128]{1,0:T(8,128)S(1)} %get-tuple-element.73.refs_0_), channel_id=1, source_target_pairs={{0,32},{32,0},{64,96},{96,64},{1,33},{33,1},{65,97},{97,65},{2,34}... | collective-permute-start | bytes 24584 | tf_op jit(solution)/shard_map/ppermute | solution.py:204
  28.4 2.7 %collective-permute-start.4 = (s32[16,128]{1,0:T(8,128)S(1)}, s32[16,128]{1,0:T(8,128)S(1)}, u32[]{:S(2)}, u32[]{:S(2)}) collective-permute-start(s32[16,128]{1,0:T(8,128)S(1)} %get-tuple-element.73.refs_0_), channel_id=1, source_target_pairs={{0,64},{32,96},{64,0},{96,32},{1,65},{33,97},{65,1},{97,33},{2,66}... | collective-permute-start | bytes 24584 | tf_op jit(solution)/shard_map/ppermute | solution.py:204
  31.2 0.5 collective-permute-start.5
  31.6 0.0 collective-permute-done.3.refs_1_
  31.7 0.0 collective-permute-start.8
  31.7 1.9 %collective-permute-done.4.refs_2_ = s32[16,128]{1,0:T(8,128)S(1)} collective-permute-done((s32[16,128]{1,0:T(8,128)S(1)}, s32[16,128]{1,0:T(8,128)S(1)}, u32[]{:S(2)}, u32[]{:S(2)}) %collective-permute-start.4) | collective-permute-done | bytes 8224 | tf_op jit(solution)/shard_map/ppermute | solution.py:204
  33.6 3.2 %collective-permute-start.11 = (f32[2,4,128,512]{3,2,1,0:T(8,128)}, f32[2,4,128,512]{3,2,1,0:T(8,128)}, u32[]{:S(2)}, u32[]{:S(2)}) collective-permute-start(f32[2,4,128,512]{3,2,1,0:T(8,128)} %get-tuple-element.86), channel_id=1, source_target_pairs={{0,24},{1,7},{2,26},{3,1},{4,28},{5,3},{6,30},{7,5},{8,0},{9,15},{... | collective-permute-start | bytes 6291464 | tf_op jit(solution)/shard_map/ppermute | solution.py:200
  36.8 0.0 collective-permute-done.5.refs_3_
  36.9 1.8 %tables.1 = (bf16[4,4,512,256]{3,2,1,0:T(8,128)(2,1)S(1)}, f32[4,4,64,512]{3,2,1,0:T(8,128)S(1)}, f32[8,128]{1,0:T(8,128)S(1)}) custom-call(s32[16,128]{1,0:T(8,128)S(1)} %get-tuple-element.73.refs_0_, s32[16,128]{1,0:T(8,128)S(1)} %collective-permute-done.3.refs_1_, s32[16,128]{1,0:T(8,128)S(1)} %collective-permute-done.4.refs_2_, ...), custom_call_target="tpu_custom_call" | custom-call | flops 1000000 | bytes 4000000 | tf_op jit(solution)/shard_map/tables/pallas_call | solution.py:170
  38.7 2.2 %collective-permute-done.6.refs_4_.refs_2_ = f32[2,4,128,512]{3,2,1,0:T(8,128)S(1)} collective-permute-done((f32[2,4,128,512]{3,2,1,0:T(8,128)}, f32[2,4,128,512]{3,2,1,0:T(8,128)S(1)}, u32[]{:S(2)}, u32[]{:S(2)}) %collective-permute-start.6) | collective-permute-done | bytes 2097184 | tf_op jit(solution)/shard_map/ppermute | solution.py:200
  40.9 3.7 %collective-permute-done.7.refs_5_.refs_3_ = f32[2,4,128,512]{3,2,1,0:T(8,128)} collective-permute-done((f32[2,4,128,512]{3,2,1,0:T(8,128)}, f32[2,4,128,512]{3,2,1,0:T(8,128)}, u32[]{:S(2)}, u32[]{:S(2)}) %collective-permute-start.7) | collective-permute-done | bytes 2097184 | tf_op jit(solution)/shard_map/ppermute | solution.py:200
  44.6 0.7 own.1
  45.3 2.5 %pass.2 = (f32[4,128,512]{2,1,0:T(8,128)S(1)}, f32[4,128,512]{2,1,0:T(8,128)S(1)}, f32[8,128]{1,0:T(8,128)S(1)}) custom-call(bf16[4,4,2,256,1024]{4,3,2,1,0:T(8,128)(2,1)} %bitcast.13, f32[2,2,4,256,512]{4,3,2,1,0:T(8,128)} %collective-permute-done.8.refs_1_, f32[2,4,128,512]{3,2,1,0:T(8,128)S(1)} %collective-permute-done.6.refs_4_.refs_2_, ...), custom_call_target="tpu_custom_call" | custom-call | flops 1000000 | bytes 4000000 | tf_op jit(solution)/shard_map/pass/pallas_call | solution.py:170
  47.9 0.3 collective-permute-start.10
  48.2 3.0 %collective-permute-start.9 = (f32[4,128,512]{2,1,0:T(8,128)S(1)}, f32[4,128,512]{2,1,0:T(8,128)S(1)}, u32[]{:S(2)}, u32[]{:S(2)}) collective-permute-start(f32[4,128,512]{2,1,0:T(8,128)S(1)} %get-tuple-element.84), channel_id=1, source_target_pairs={{0,24},{1,7},{2,26},{3,1},{4,28},{5,3},{6,30},{7,5},{8,0},{9,15},{... | collective-permute-start | bytes 3145736 | tf_op jit(solution)/shard_map/ppermute | solution.py:200
  51.2 2.5 %before.2 = (f32[2,4,128,512]{3,2,1,0:T(8,128)S(1)}, f32[8,128]{1,0:T(8,128)S(1)}) custom-call(bf16[4,4,2,256,1024]{4,3,2,1,0:T(8,128)(2,1)} %bitcast.14, f32[2,2,4,256,512]{4,3,2,1,0:T(8,128)} %collective-permute-done.8.refs_1_, f32[2,4,128,512]{3,2,1,0:T(8,128)S(1)} %collective-permute-done.6.refs_4_.refs_2_, ...), custom_call_target="tpu_custom_call" | custom-call | flops 1000000 | bytes 4000000 | tf_op jit(solution)/shard_map/before/pallas_call | solution.py:170
  53.7 9.7 %collective-permute-done.11.refs_2_ = f32[2,4,128,512]{3,2,1,0:T(8,128)} collective-permute-done((f32[2,4,128,512]{3,2,1,0:T(8,128)}, f32[2,4,128,512]{3,2,1,0:T(8,128)}, u32[]{:S(2)}, u32[]{:S(2)}) %collective-permute-start.11) | collective-permute-done | bytes 2097184 | tf_op jit(solution)/shard_map/ppermute | solution.py:200
  63.4 3.7 %collective-permute-done.12.refs_3_ = f32[2,4,128,512]{3,2,1,0:T(8,128)} collective-permute-done((f32[2,4,128,512]{3,2,1,0:T(8,128)}, f32[2,4,128,512]{3,2,1,0:T(8,128)}, u32[]{:S(2)}, u32[]{:S(2)}) %collective-permute-start.12) | collective-permute-done | bytes 2097184 | tf_op jit(solution)/shard_map/ppermute | solution.py:200
  67.1 2.8 %pass.3 = (f32[4,128,512]{2,1,0:T(8,128)S(1)}, f32[4,128,512]{2,1,0:T(8,128)S(1)}, f32[8,128]{1,0:T(8,128)S(1)}) custom-call(bf16[4,4,2,256,1024]{4,3,2,1,0:T(8,128)(2,1)} %bitcast.15, f32[2,2,4,256,512]{4,3,2,1,0:T(8,128)} %collective-permute-done.8.refs_1_, f32[2,4,128,512]{3,2,1,0:T(8,128)} %collective-permute-done.11.refs_2_, ...), custom_call_target="tpu_custom_call" | custom-call | flops 1000000 | bytes 4000000 | tf_op jit(solution)/shard_map/pass/pallas_call | solution.py:170
  69.9 0.1 collective-permute-start.15
  69.9 2.0 %collective-permute-start.16 = (f32[4,128,512]{2,1,0:T(8,128)S(1)}, f32[4,128,512]{2,1,0:T(8,128)S(1)}, u32[]{:S(2)}, u32[]{:S(2)}) collective-permute-start(f32[4,128,512]{2,1,0:T(8,128)S(1)} %get-tuple-element.99), channel_id=1, source_target_pairs={{0,8},{1,3},{2,10},{3,5},{4,12},{5,7},{6,14},{7,1},{8,16},{9,11},{... | collective-permute-start | bytes 3145736 | tf_op jit(solution)/shard_map/ppermute | solution.py:200
  71.9 6.2 %collective-permute-done.10.refs_2_ = f32[4,128,512]{2,1,0:T(8,128)S(1)} collective-permute-done((f32[4,128,512]{2,1,0:T(8,128)S(1)}, f32[4,128,512]{2,1,0:T(8,128)S(1)}, u32[]{:S(2)}, u32[]{:S(2)}) %collective-permute-start.10) | collective-permute-done | bytes 1048608 | tf_op jit(solution)/shard_map/ppermute | solution.py:200
  78.2 0.2 turn.2
  78.4 3.3 %collective-permute-start.13 = (f32[2,128,512]{2,1,0:T(8,128)S(1)}, f32[2,128,512]{2,1,0:T(8,128)S(1)}, u32[]{:S(2)}, u32[]{:S(2)}) collective-permute-start(f32[2,128,512]{2,1,0:T(8,128)S(1)} %get-tuple-element.94), channel_id=1, source_target_pairs={{0,6},{1,25},{2,0},{3,27},{4,2},{5,29},{6,4},{7,31},{8,14},{9,1},{... | collective-permute-start | bytes 1572872 | tf_op jit(solution)/shard_map/ppermute | solution.py:200
  81.7 2.8 %before.3 = (f32[2,4,128,512]{3,2,1,0:T(8,128)S(1)}, f32[8,128]{1,0:T(8,128)S(1)}) custom-call(bf16[4,4,2,256,1024]{4,3,2,1,0:T(8,128)(2,1)} %bitcast.16, f32[2,2,4,256,512]{4,3,2,1,0:T(8,128)} %collective-permute-done.8.refs_1_, f32[2,4,128,512]{3,2,1,0:T(8,128)} %collective-permute-done.11.refs_2_, f32[2,4,128,512]{3,2,1,0:T(8,128)} %collective-permute-done.12.refs_3_, ...), custom_call_target="tpu_custom_call" | custom-call | flops 1000000 | bytes 4000000 | tf_op jit(solution)/shard_map/before/pallas_call | solution.py:170
  84.5 6.1 %collective-permute-done.15.refs_1_ = f32[4,128,512]{2,1,0:T(8,128)S(1)} collective-permute-done((f32[4,128,512]{2,1,0:T(8,128)S(1)}, f32[4,128,512]{2,1,0:T(8,128)S(1)}, u32[]{:S(2)}, u32[]{:S(2)}) %collective-permute-start.15) | collective-permute-done | bytes 1048608 | tf_op jit(solution)/shard_map/ppermute | solution.py:200
  90.6 4.0 %collective-permute-done.16.refs_2_ = f32[4,128,512]{2,1,0:T(8,128)S(1)} collective-permute-done((f32[4,128,512]{2,1,0:T(8,128)S(1)}, f32[4,128,512]{2,1,0:T(8,128)S(1)}, u32[]{:S(2)}, u32[]{:S(2)}) %collective-permute-start.16) | collective-permute-done | bytes 1048608 | tf_op jit(solution)/shard_map/ppermute | solution.py:200
  94.6 0.3 turn.3
  94.9 0.0 copy-start
  94.9 0.0 copy-start.3
  94.9 0.0 copy-start.4
  94.9 3.5 %collective-permute-start.19 = (f32[2,128,512]{2,1,0:T(8,128)S(1)}, f32[2,128,512]{2,1,0:T(8,128)S(1)}, u32[]{:S(2)}, u32[]{:S(2)}) collective-permute-start(f32[2,128,512]{2,1,0:T(8,128)S(1)} %get-tuple-element.106), channel_id=1, source_target_pairs={{0,6},{1,25},{2,0},{3,27},{4,2},{5,29},{6,4},{7,31},{8,14},{9,1},{... | collective-permute-start | bytes 1572872 | tf_op jit(solution)/shard_map/ppermute | solution.py:200
  98.5 0.1 relay.2
  98.5 3.3 %collective-permute-start.17 = (f32[128,512]{1,0:T(8,128)S(1)}, f32[128,512]{1,0:T(8,128)S(1)}, u32[]{:S(2)}, u32[]{:S(2)}) collective-permute-start(f32[128,512]{1,0:T(8,128)S(1)} %get-tuple-element.102), channel_id=1, source_target_pairs={{0,6},{1,25},{2,0},{3,27},{4,2},{5,29},{6,4},{7,31},{8,14},{9,1},{... | collective-permute-start | bytes 786440 | tf_op jit(solution)/shard_map/ppermute | solution.py:200
  101.8 3.3 %collective-permute-done.19.refs_2_.refs_11_ = f32[2,128,512]{2,1,0:T(8,128)S(1)} collective-permute-done((f32[2,128,512]{2,1,0:T(8,128)S(1)}, f32[2,128,512]{2,1,0:T(8,128)S(1)}, u32[]{:S(2)}, u32[]{:S(2)}) %collective-permute-start.19) | collective-permute-done | bytes 524320 | tf_op jit(solution)/shard_map/ppermute | solution.py:200
  105.2 3.7 %collective-permute-done.20.refs_3_.refs_10_ = f32[2,128,512]{2,1,0:T(8,128)S(1)} collective-permute-done((f32[2,128,512]{2,1,0:T(8,128)S(1)}, f32[2,128,512]{2,1,0:T(8,128)S(1)}, u32[]{:S(2)}, u32[]{:S(2)}) %collective-permute-start.20) | collective-permute-done | bytes 524320 | tf_op jit(solution)/shard_map/ppermute | solution.py:200
  108.9 0.1 relay.3
  108.9 0.1 collective-permute-start.21
  109.0 2.0 %collective-permute-start.22 = (f32[128,512]{1,0:T(8,128)S(1)}, f32[128,512]{1,0:T(8,128)S(1)}, u32[]{:S(2)}, u32[]{:S(2)}) collective-permute-start(f32[128,512]{1,0:T(8,128)S(1)} %get-tuple-element.114), channel_id=1, source_target_pairs={{0,2},{1,9},{2,4},{3,11},{4,6},{5,13},{6,0},{7,15},{8,10},{9,17},{... | collective-permute-start | bytes 786440 | tf_op jit(solution)/shard_map/ppermute | solution.py:200
  111.7 1.1 values.2
  112.8 2.6 %collective-permute-done.21.refs_8_ = f32[128,512]{1,0:T(8,128)S(1)} collective-permute-done((f32[128,512]{1,0:T(8,128)S(1)}, f32[128,512]{1,0:T(8,128)S(1)}, u32[]{:S(2)}, u32[]{:S(2)}) %collective-permute-start.21) | collective-permute-done | bytes 262176 | tf_op jit(solution)/shard_map/ppermute | solution.py:200
  115.4 1.3 collective-permute-done.22.refs_9_
  116.7 1.5 %values.3 = (f32[128,1024]{1,0:T(8,128)S(1)}, f32[16,128]{1,0:T(8,128)S(1)}, f32[8,128]{1,0:T(8,128)}) custom-call(f32[256,1024]{1,0:T(8,128)S(1)} %bitcast.6, s32[1]{0:T(128)S(6)} %copy.12.refs_1_, bf16[256,256]{1,0:T(8,128)(2,1)S(1)} %copy-done.3, bf16[256,256]{1,0:T(8,128)(2,1)S(1)} %copy-done.4, bf16[4,4,256,128]{3,2,1,0:T(8,128)(2,1)S(1)} %get-tuple-element.78.refs_4_, ...), custom_call_target="tpu_custom_call" | custom-call | flops 1000000 | bytes 4000000 | tf_op jit(solution)/shard_map/values/pallas_call | solution.py:170
  118.2 1.5 %collective-permute-start.23 = (f32[16,128]{1,0:T(8,128)S(1)}, f32[16,128]{1,0:T(8,128)S(1)}, u32[]{:S(2)}, u32[]{:S(2)}) collective-permute-start(f32[16,128]{1,0:T(8,128)S(1)} %get-tuple-element.118.refs_2_.refs_0_), channel_id=1, source_target_pairs={{0,32},{32,0},{64,96},{96,64},{1,33},{33,1},{65,97},{97,65},{2,34}... | collective-permute-start | bytes 24584 | tf_op jit(solution)/shard_map/ppermute | solution.py:204
  119.7 2.7 %collective-permute-start.24 = (f32[16,128]{1,0:T(8,128)S(1)}, f32[16,128]{1,0:T(8,128)S(1)}, u32[]{:S(2)}, u32[]{:S(2)}) collective-permute-start(f32[16,128]{1,0:T(8,128)S(1)} %get-tuple-element.118.refs_2_.refs_0_), channel_id=1, source_target_pairs={{0,64},{32,96},{64,0},{96,32},{1,65},{33,97},{65,1},{97,33},{2,66}... | collective-permute-start | bytes 24584 | tf_op jit(solution)/shard_map/ppermute | solution.py:204
  122.4 0.5 collective-permute-start.25
  122.9 2.4 %keep.1 = (f32[256,1024]{1,0:T(8,128)}, f32[8,128]{1,0:T(8,128)}) custom-call(f32[128,1024]{1,0:T(8,128)S(1)} %get-tuple-element.110.refs_0_, f32[128,1024]{1,0:T(8,128)S(1)} %get-tuple-element.117.refs_1_, f32[16,128]{1,0:T(8,128)S(1)} %get-tuple-element.118.refs_2_.refs_0_, bf16[256,256]{1,0:T(8,128)(2,1)S(1)} %copy-done.1, ...), custom_call_target="tpu_custom_call" | custom-call | flops 1000000 | bytes 4000000 | tf_op jit(solution)/shard_map/keep/pallas_call | solution.py:170
  125.3 2.0 %collective-permute-done.25.refs_3_ = f32[16,128]{1,0:T(8,128)S(1)} collective-permute-done((f32[16,128]{1,0:T(8,128)S(1)}, f32[16,128]{1,0:T(8,128)S(1)}, u32[]{:S(2)}, u32[]{:S(2)}) %collective-permute-start.25) | collective-permute-done | bytes 8224 | tf_op jit(solution)/shard_map/ppermute | solution.py:204
  127.2 3.0 %update.1 = (f32[256,1024]{1,0:T(8,128)}, f32[8,128]{1,0:T(8,128)}) custom-call(f32[16,128]{1,0:T(8,128)S(1)} %get-tuple-element.118.refs_2_.refs_0_, f32[16,128]{1,0:T(8,128)S(1)} %collective-permute-done.23.refs_1_, f32[16,128]{1,0:T(8,128)S(1)} %collective-permute-done.24.refs_2_, f32[16,128]{1,0:T(8,128)S(1)} %collective-permute-done.25.refs_3_, ...), custom_call_target="tpu_custom_call" | custom-call | flops 1000000 | bytes 4000000 | tf_op jit(solution)/shard_map/update/pallas_call | solution.py:170
  (27 shorter events, 0.1 us)
Async XLA Ops:
  2.0 5.5 %collective-permute-start.1 = (f32[1,2,4,128,512]{4,3,2,1,0:T(8,128)S(1)}, f32[1,2,4,128,512]{4,3,2,1,0:T(8,128)S(1)}, u32[]{:S(2)}, u32[]{:S(2)}) collective-permute-start(f32[1,2,4,128,512]{4,3,2,1,0:T(8,128)S(1)} %get-tuple-element.66), channel_id=1, source_target_pairs={{0,1},{1,0},{2,3},{3,2},{4,5},{5,4},{6,7},{7,6},{8,9},{9,8},{10,11... | collective-permute-start | bytes 6291464 | tf_op jit(solution)/shard_map/ppermute | solution.py:192
  3.5 5.7 %collective-permute-start.2 = (f32[1,2,4,128,512]{4,3,2,1,0:T(8,128)S(1)}, f32[1,2,4,128,512]{4,3,2,1,0:T(8,128)S(1)}, u32[]{:S(2)}, u32[]{:S(2)}) collective-permute-start(f32[1,2,4,128,512]{4,3,2,1,0:T(8,128)S(1)} %get-tuple-element.67), channel_id=1, source_target_pairs={{0,1},{1,0},{2,3},{3,2},{4,5},{5,4},{6,7},{7,6},{8,9},{9,8},{10,11... | collective-permute-start | bytes 6291464 | tf_op jit(solution)/shard_map/ppermute | solution.py:192
  7.4 9.7 %collective-permute-start = (f32[2,2,4,128,512]{4,3,2,1,0:T(8,128)}, f32[2,2,4,128,512]{4,3,2,1,0:T(8,128)}, u32[]{:S(2)}, u32[]{:S(2)}) collective-permute-start(f32[2,2,4,128,512]{4,3,2,1,0:T(8,128)} %get-tuple-element.65), channel_id=1, source_target_pairs={{0,1},{1,0},{2,3},{3,2},{4,5},{5,4},{6,7},{7,6},{8,9},{9,8},{10,11... | collective-permute-start | bytes 12582920 | tf_op jit(solution)/shard_map/ppermute | solution.py:192
  9.3 7.8 %copy-start.7 = (s32[1,4,16,32]{3,2,1,0:T(8,128)S(1)}, s32[1,4,16,32]{3,2,1,0:T(8,128)}, u32[]{:S(2)}) copy-start(s32[1,4,16,32]{3,2,1,0:T(8,128)} %param.12) | copy-start | bytes 24580
  12.8 28.1 %collective-permute-start.6 = (f32[2,4,128,512]{3,2,1,0:T(8,128)}, f32[2,4,128,512]{3,2,1,0:T(8,128)S(1)}, u32[]{:S(2)}, u32[]{:S(2)}) collective-permute-start(f32[2,4,128,512]{3,2,1,0:T(8,128)} %get-tuple-element.76), channel_id=1, source_target_pairs={{0,24},{1,7},{2,26},{3,1},{4,28},{5,3},{6,30},{7,5},{8,0},{9,15},{... | collective-permute-start | bytes 6291464 | tf_op jit(solution)/shard_map/ppermute | solution.py:200
  17.0 27.6 %collective-permute-start.7 = (f32[2,4,128,512]{3,2,1,0:T(8,128)}, f32[2,4,128,512]{3,2,1,0:T(8,128)}, u32[]{:S(2)}, u32[]{:S(2)}) collective-permute-start(f32[2,4,128,512]{3,2,1,0:T(8,128)} %get-tuple-element.77), channel_id=1, source_target_pairs={{0,8},{1,3},{2,10},{3,5},{4,12},{5,7},{6,14},{7,1},{8,16},{9,11},{... | collective-permute-start | bytes 6291464 | tf_op jit(solution)/shard_map/ppermute | solution.py:200
  22.3 14.5 %copy-start.5 = (bf16[64,64]{1,0:T(8,128)(2,1)S(1)}, bf16[64,64]{1,0:T(8,128)(2,1)}, u32[]{:S(2)}) copy-start(bf16[64,64]{1,0:T(8,128)(2,1)} %constant.16.clone.refs_4_.refs_1_) | copy-start | bytes 24580
  22.3 14.5 %copy-start.6 = (bf16[64,64]{1,0:T(8,128)(2,1)S(1)}, bf16[64,64]{1,0:T(8,128)(2,1)}, u32[]{:S(2)}) copy-start(bf16[64,64]{1,0:T(8,128)(2,1)} %constant.17.clone.refs_5_.refs_2_) | copy-start | bytes 24580
  26.9 4.8 %collective-permute-start.3 = (s32[16,128]{1,0:T(8,128)S(1)}, s32[16,128]{1,0:T(8,128)S(1)}, u32[]{:S(2)}, u32[]{:S(2)}) collective-permute-start(s32[16,128]{1,0:T(8,128)S(1)} %get-tuple-element.73.refs_0_), channel_id=1, source_target_pairs={{0,32},{32,0},{64,96},{96,64},{1,33},{33,1},{65,97},{97,65},{2,34}... | collective-permute-start | bytes 24584 | tf_op jit(solution)/shard_map/ppermute | solution.py:204
  28.4 5.2 %collective-permute-start.4 = (s32[16,128]{1,0:T(8,128)S(1)}, s32[16,128]{1,0:T(8,128)S(1)}, u32[]{:S(2)}, u32[]{:S(2)}) collective-permute-start(s32[16,128]{1,0:T(8,128)S(1)} %get-tuple-element.73.refs_0_), channel_id=1, source_target_pairs={{0,64},{32,96},{64,0},{96,32},{1,65},{33,97},{65,1},{97,33},{2,66}... | collective-permute-start | bytes 24584 | tf_op jit(solution)/shard_map/ppermute | solution.py:204
  31.2 5.7 %collective-permute-start.5 = (s32[16,128]{1,0:T(8,128)S(1)}, s32[16,128]{1,0:T(8,128)S(1)}, u32[]{:S(2)}, u32[]{:S(2)}) collective-permute-start(s32[16,128]{1,0:T(8,128)S(1)} %get-tuple-element.73.refs_0_), channel_id=1, source_target_pairs={{0,96},{32,64},{64,32},{96,0},{1,97},{33,65},{65,33},{97,1},{2,98}... | collective-permute-start | bytes 24584 | tf_op jit(solution)/shard_map/ppermute | solution.py:204
  31.7 13.7 %collective-permute-start.8 = (f32[2,2,4,256,512]{4,3,2,1,0:T(8,128)}, f32[2,2,4,256,512]{4,3,2,1,0:T(8,128)}, u32[]{:S(2)}, u32[]{:S(2)}) collective-permute-start(f32[2,2,4,256,512]{4,3,2,1,0:T(8,128)} %get-tuple-element.80), channel_id=1, source_target_pairs={{0,1},{1,0},{2,3},{3,2},{4,5},{5,4},{6,7},{7,6},{8,9},{9,8},{10,11... | collective-permute-start | bytes 25165832 | tf_op jit(solution)/shard_map/ppermute | solution.py:192
  33.6 29.8 %collective-permute-start.11 = (f32[2,4,128,512]{3,2,1,0:T(8,128)}, f32[2,4,128,512]{3,2,1,0:T(8,128)}, u32[]{:S(2)}, u32[]{:S(2)}) collective-permute-start(f32[2,4,128,512]{3,2,1,0:T(8,128)} %get-tuple-element.86), channel_id=1, source_target_pairs={{0,24},{1,7},{2,26},{3,1},{4,28},{5,3},{6,30},{7,5},{8,0},{9,15},{... | collective-permute-start | bytes 6291464 | tf_op jit(solution)/shard_map/ppermute | solution.py:200
  36.8 30.2 %collective-permute-start.12 = (f32[2,4,128,512]{3,2,1,0:T(8,128)}, f32[2,4,128,512]{3,2,1,0:T(8,128)}, u32[]{:S(2)}, u32[]{:S(2)}) collective-permute-start(f32[2,4,128,512]{3,2,1,0:T(8,128)} %get-tuple-element.87), channel_id=1, source_target_pairs={{0,8},{1,3},{2,10},{3,5},{4,12},{5,7},{6,14},{7,1},{8,16},{9,11},{... | collective-permute-start | bytes 6291464 | tf_op jit(solution)/shard_map/ppermute | solution.py:200
  47.9 30.3 %collective-permute-start.10 = (f32[4,128,512]{2,1,0:T(8,128)S(1)}, f32[4,128,512]{2,1,0:T(8,128)S(1)}, u32[]{:S(2)}, u32[]{:S(2)}) collective-permute-start(f32[4,128,512]{2,1,0:T(8,128)S(1)} %get-tuple-element.85), channel_id=1, source_target_pairs={{0,8},{1,3},{2,10},{3,5},{4,12},{5,7},{6,14},{7,1},{8,16},{9,11},{... | collective-permute-start | bytes 3145736 | tf_op jit(solution)/shard_map/ppermute | solution.py:200
  48.2 30.0 %collective-permute-start.9 = (f32[4,128,512]{2,1,0:T(8,128)S(1)}, f32[4,128,512]{2,1,0:T(8,128)S(1)}, u32[]{:S(2)}, u32[]{:S(2)}) collective-permute-start(f32[4,128,512]{2,1,0:T(8,128)S(1)} %get-tuple-element.84), channel_id=1, source_target_pairs={{0,24},{1,7},{2,26},{3,1},{4,28},{5,3},{6,30},{7,5},{8,0},{9,15},{... | collective-permute-start | bytes 3145736 | tf_op jit(solution)/shard_map/ppermute | solution.py:200
  69.9 20.8 %collective-permute-start.15 = (f32[4,128,512]{2,1,0:T(8,128)S(1)}, f32[4,128,512]{2,1,0:T(8,128)S(1)}, u32[]{:S(2)}, u32[]{:S(2)}) collective-permute-start(f32[4,128,512]{2,1,0:T(8,128)S(1)} %get-tuple-element.98), channel_id=1, source_target_pairs={{0,24},{1,7},{2,26},{3,1},{4,28},{5,3},{6,30},{7,5},{8,0},{9,15},{... | collective-permute-start | bytes 3145736 | tf_op jit(solution)/shard_map/ppermute | solution.py:200
  69.9 24.6 %collective-permute-start.16 = (f32[4,128,512]{2,1,0:T(8,128)S(1)}, f32[4,128,512]{2,1,0:T(8,128)S(1)}, u32[]{:S(2)}, u32[]{:S(2)}) collective-permute-start(f32[4,128,512]{2,1,0:T(8,128)S(1)} %get-tuple-element.99), channel_id=1, source_target_pairs={{0,8},{1,3},{2,10},{3,5},{4,12},{5,7},{6,14},{7,1},{8,16},{9,11},{... | collective-permute-start | bytes 3145736 | tf_op jit(solution)/shard_map/ppermute | solution.py:200
  78.4 20.1 %collective-permute-start.13 = (f32[2,128,512]{2,1,0:T(8,128)S(1)}, f32[2,128,512]{2,1,0:T(8,128)S(1)}, u32[]{:S(2)}, u32[]{:S(2)}) collective-permute-start(f32[2,128,512]{2,1,0:T(8,128)S(1)} %get-tuple-element.94), channel_id=1, source_target_pairs={{0,6},{1,25},{2,0},{3,27},{4,2},{5,29},{6,4},{7,31},{8,14},{9,1},{... | collective-permute-start | bytes 1572872 | tf_op jit(solution)/shard_map/ppermute | solution.py:200
  81.7 16.8 %collective-permute-start.14 = (f32[2,128,512]{2,1,0:T(8,128)S(1)}, f32[2,128,512]{2,1,0:T(8,128)S(1)}, u32[]{:S(2)}, u32[]{:S(2)}) collective-permute-start(f32[2,128,512]{2,1,0:T(8,128)S(1)} %get-tuple-element.95), channel_id=1, source_target_pairs={{0,2},{1,9},{2,4},{3,11},{4,6},{5,13},{6,0},{7,15},{8,10},{9,17},{... | collective-permute-start | bytes 1572872 | tf_op jit(solution)/shard_map/ppermute | solution.py:200
  94.9 16.8 %copy-start = (f32[1,256,1024]{2,1,0:T(8,128)S(1)}, f32[1,256,1024]{2,1,0:T(8,128)}, u32[]{:S(2)}) copy-start(f32[1,256,1024]{2,1,0:T(8,128)} %param.11) | copy-start | bytes 3145732
  94.9 16.8 %copy-start.3 = (bf16[256,256]{1,0:T(8,128)(2,1)S(1)}, bf16[256,256]{1,0:T(8,128)(2,1)}, u32[]{:S(2)}) copy-start(bf16[256,256]{1,0:T(8,128)(2,1)} %constant.12.clone.refs_2_) | copy-start | bytes 393220
  94.9 16.8 %copy-start.4 = (bf16[256,256]{1,0:T(8,128)(2,1)S(1)}, bf16[256,256]{1,0:T(8,128)(2,1)}, u32[]{:S(2)}) copy-start(bf16[256,256]{1,0:T(8,128)(2,1)} %constant.13.clone.refs_3_) | copy-start | bytes 393220
  94.9 10.2 %collective-permute-start.19 = (f32[2,128,512]{2,1,0:T(8,128)S(1)}, f32[2,128,512]{2,1,0:T(8,128)S(1)}, u32[]{:S(2)}, u32[]{:S(2)}) collective-permute-start(f32[2,128,512]{2,1,0:T(8,128)S(1)} %get-tuple-element.106), channel_id=1, source_target_pairs={{0,6},{1,25},{2,0},{3,27},{4,2},{5,29},{6,4},{7,31},{8,14},{9,1},{... | collective-permute-start | bytes 1572872 | tf_op jit(solution)/shard_map/ppermute | solution.py:200
  98.5 10.4 %collective-permute-start.20 = (f32[2,128,512]{2,1,0:T(8,128)S(1)}, f32[2,128,512]{2,1,0:T(8,128)S(1)}, u32[]{:S(2)}, u32[]{:S(2)}) collective-permute-start(f32[2,128,512]{2,1,0:T(8,128)S(1)} %get-tuple-element.107), channel_id=1, source_target_pairs={{0,2},{1,9},{2,4},{3,11},{4,6},{5,13},{6,0},{7,15},{8,10},{9,17},{... | collective-permute-start | bytes 1572872 | tf_op jit(solution)/shard_map/ppermute | solution.py:200
  98.5 13.1 %collective-permute-start.17 = (f32[128,512]{1,0:T(8,128)S(1)}, f32[128,512]{1,0:T(8,128)S(1)}, u32[]{:S(2)}, u32[]{:S(2)}) collective-permute-start(f32[128,512]{1,0:T(8,128)S(1)} %get-tuple-element.102), channel_id=1, source_target_pairs={{0,6},{1,25},{2,0},{3,27},{4,2},{5,29},{6,4},{7,31},{8,14},{9,1},{... | collective-permute-start | bytes 786440 | tf_op jit(solution)/shard_map/ppermute | solution.py:200
  101.8 9.9 %collective-permute-start.18 = (f32[128,512]{1,0:T(8,128)S(1)}, f32[128,512]{1,0:T(8,128)S(1)}, u32[]{:S(2)}, u32[]{:S(2)}) collective-permute-start(f32[128,512]{1,0:T(8,128)S(1)} %get-tuple-element.103), channel_id=1, source_target_pairs={{0,2},{1,9},{2,4},{3,11},{4,6},{5,13},{6,0},{7,15},{8,10},{9,17},{... | collective-permute-start | bytes 786440 | tf_op jit(solution)/shard_map/ppermute | solution.py:200
  108.9 6.4 %collective-permute-start.21 = (f32[128,512]{1,0:T(8,128)S(1)}, f32[128,512]{1,0:T(8,128)S(1)}, u32[]{:S(2)}, u32[]{:S(2)}) collective-permute-start(f32[128,512]{1,0:T(8,128)S(1)} %get-tuple-element.113), channel_id=1, source_target_pairs={{0,6},{1,25},{2,0},{3,27},{4,2},{5,29},{6,4},{7,31},{8,14},{9,1},{... | collective-permute-start | bytes 786440 | tf_op jit(solution)/shard_map/ppermute | solution.py:200
  109.0 7.7 %collective-permute-start.22 = (f32[128,512]{1,0:T(8,128)S(1)}, f32[128,512]{1,0:T(8,128)S(1)}, u32[]{:S(2)}, u32[]{:S(2)}) collective-permute-start(f32[128,512]{1,0:T(8,128)S(1)} %get-tuple-element.114), channel_id=1, source_target_pairs={{0,2},{1,9},{2,4},{3,11},{4,6},{5,13},{6,0},{7,15},{8,10},{9,17},{... | collective-permute-start | bytes 786440 | tf_op jit(solution)/shard_map/ppermute | solution.py:200
  116.7 6.2 %copy-start.1 = (bf16[256,256]{1,0:T(8,128)(2,1)S(1)}, bf16[256,256]{1,0:T(8,128)(2,1)}, u32[]{:S(2)}) copy-start(bf16[256,256]{1,0:T(8,128)(2,1)} %constant.14.clone.refs_3_.refs_4_) | copy-start | bytes 393220
  116.7 6.2 %copy-start.2 = (bf16[256,256]{1,0:T(8,128)(2,1)S(1)}, bf16[256,256]{1,0:T(8,128)(2,1)}, u32[]{:S(2)}) copy-start(bf16[256,256]{1,0:T(8,128)(2,1)} %constant.15.clone.refs_4_.refs_5_) | copy-start | bytes 393220
  118.2 7.1 %collective-permute-start.23 = (f32[16,128]{1,0:T(8,128)S(1)}, f32[16,128]{1,0:T(8,128)S(1)}, u32[]{:S(2)}, u32[]{:S(2)}) collective-permute-start(f32[16,128]{1,0:T(8,128)S(1)} %get-tuple-element.118.refs_2_.refs_0_), channel_id=1, source_target_pairs={{0,32},{32,0},{64,96},{96,64},{1,33},{33,1},{65,97},{97,65},{2,34}... | collective-permute-start | bytes 24584 | tf_op jit(solution)/shard_map/ppermute | solution.py:204
  119.7 5.6 %collective-permute-start.24 = (f32[16,128]{1,0:T(8,128)S(1)}, f32[16,128]{1,0:T(8,128)S(1)}, u32[]{:S(2)}, u32[]{:S(2)}) collective-permute-start(f32[16,128]{1,0:T(8,128)S(1)} %get-tuple-element.118.refs_2_.refs_0_), channel_id=1, source_target_pairs={{0,64},{32,96},{64,0},{96,32},{1,65},{33,97},{65,1},{97,33},{2,66}... | collective-permute-start | bytes 24584 | tf_op jit(solution)/shard_map/ppermute | solution.py:204
  122.4 4.9 %collective-permute-start.25 = (f32[16,128]{1,0:T(8,128)S(1)}, f32[16,128]{1,0:T(8,128)S(1)}, u32[]{:S(2)}, u32[]{:S(2)}) collective-permute-start(f32[16,128]{1,0:T(8,128)S(1)} %get-tuple-element.118.refs_2_.refs_0_), channel_id=1, source_target_pairs={{0,96},{32,64},{64,32},{96,0},{1,97},{33,65},{65,33},{97,1},{2,98}... | collective-permute-start | bytes 24584 | tf_op jit(solution)/shard_map/ppermute | solution.py:204
